TPU v7x, 32 devices: a whole 2x2x4 slice. The times are simulated.
32 devices in a mesh: grp: 2 (over y), bx: 16 (over z, x, core).
Axes of the slice: x: 2, y: 2, z: 4, core: 2. Of those that a mesh axis runs over, the one named last changes fastest.
Arguments:
- density_map: float32 [128, 64, 256], P(('grp', 'bx')), parts along dimension 0, may hold values from -6 to 6
- amplitude: float32 [65536], P(('grp', 'bx')), parts along dimension 0, may hold values from 0.5 to 4
- fraction: float32 [3, 65536], P(None, ('grp', 'bx')), parts along dimension 1, may hold values from 0.25 to 0.75
- torsion_axis: float32 [3, 65536], P(None, ('grp', 'bx')), parts along dimension 1, may hold values from -4 to 4
- brick_owner: int32 [65536, 1], P(('grp', 'bx')), parts along dimension 0, may hold values from 0 to 15; in each aligned block of 2048 rows (0 to 2047, 2048 to 4095, ...) at most 384 rows name the same one
- plane_offset: int32 [65536], P(('grp', 'bx')), parts along dimension 0, may hold values from 0 to 3
- row_offset: int32 [65536], P(('grp', 'bx')), parts along dimension 0, may hold values from 0 to 63
- column_offset: int32 [65536], P(('grp', 'bx')), parts along dimension 0, may hold values from 0 to 255
- chain_index: int32 [65536], P(('grp', 'bx')), parts along dimension 0, may hold values from 0 to 7, never falling along the last dimension, each value on 1 to 16384 neighbouring positions
Outputs:
- torques: float32 [2, 65536], P(None, ('grp', 'bx')), parts along dimension 1
- atom_gradient: float32 [6, 65536], P(None, ('grp', 'bx')), parts along dimension 1
There are 2 independent parts, one for each index of `grp`. A program takes and returns all parts, laid end to end along the dimension named above; each array names one. Nothing has to cross between parts.
Inputs may be any that keep to these rules, and one draw needn't show every extreme that they name: `brick_owner`: among the atoms of one device, at most 384 lie in one slab, and exactly 384 in some slab for some device. `chain_index`: never falls along the atoms, so each chain is one run of atoms; a chain may cover many devices.
All inputs are finite; a program needn't handle non-finite values.
Results may differ from a plain program's by a relative error of at most 0.0003.
Values sent between devices are 32-bit elements; how exact they have to be, the bound alone decides.
No kernel may reach another device: no remote copies, remote signals or barrier semaphores. Data moves between devices by JAX's collectives and lax.ppermute only.
A program may use at most 64 MiB of HBM per device.

v0:
```python
import jax
import jax.numpy as jnp
from jax import lax
from jax.sharding import PartitionSpec as P

side_tap = 0.25
middle_tap = 0.5
probe_step = 0.2


def from_behind(shard, axis, by):
    length = lax.axis_size(axis)
    pairs = [(i, i + by) for i in range(length) if 0 <= i + by < length]
    return lax.ppermute(shard, axis, pairs)


def with_halo(shard, sides, width):
    for axis, dim in sides:
        size, length = (lax.axis_size(axis), shard.shape[dim])
        up = [(i, (i + 1) % size) for i in range(size - 1)]
        down = [(j, i) for i, j in up]
        last = lax.slice_in_dim(shard, length - width, length, axis=dim)
        first = lax.slice_in_dim(shard, 0, width, axis=dim)
        before = lax.ppermute(last, axis, up)
        after = lax.ppermute(first, axis, down)
        shard = jnp.concatenate([before, shard, after], axis=dim)
    return shard


def prefix(part, axis, combine, identity):
    count = lax.axis_size(axis)
    place = lax.axis_index(axis)
    ahead = count - 1 - place
    gathered = jax.tree.map(lambda a: lax.all_gather(a, axis), part)
    state = jax.tree.map(lambda a, e: jnp.zeros_like(a) + jnp.asarray(e, a.dtype), part, identity)

    def one(hop, state):
        source = count - 1 - hop
        return combine(
            state, jax.tree.map(lambda a: lax.dynamic_index_in_dim(a, source, 0, False), gathered)
        )

    return lax.fori_loop(0, ahead, one, state)


def blur_planes(extended):
    return side_tap * extended[:-2] + middle_tap * extended[1:-1] + side_tap * extended[2:]


def blur_sheet(volume):
    volume = (
        side_tap * jnp.roll(volume, 1, 1) + middle_tap * volume + side_tap * jnp.roll(volume, -1, 1)
    )
    return (
        side_tap * jnp.roll(volume, 1, 2) + middle_tap * volume + side_tap * jnp.roll(volume, -1, 2)
    )


def corner_list(fraction, cells, rows, columns):
    sheet = rows * columns
    plane_at = cells // sheet
    row_at = cells // columns % rows
    column_at = cells % columns
    listing = []
    for lift_x in (0, 1):
        for lift_y in (0, 1):
            for lift_z in (0, 1):
                weight_x = fraction[0] if lift_x else 1.0 - fraction[0]
                weight_y = fraction[1] if lift_y else 1.0 - fraction[1]
                weight_z = fraction[2] if lift_z else 1.0 - fraction[2]
                target = (
                    (plane_at + lift_x) * sheet
                    + (row_at + lift_y) % rows * columns
                    + (column_at + lift_z) % columns
                )
                listing.append(((lift_x, lift_y, lift_z), (weight_x, weight_y, weight_z), target))
    return listing


def evaluate(fraction, amplitude, cells, density_map):
    planes, rows, columns = density_map.shape
    listing = corner_list(fraction, cells, rows, columns)
    targets = jnp.concatenate([item[2] for item in listing])
    values = jnp.concatenate([amplitude * item[1][0] * item[1][1] * item[1][2] for item in listing])
    extended = jnp.zeros(((planes + 1) * rows * columns,), jnp.float32).at[targets].add(values)
    extended = extended.reshape(planes + 1, rows, columns)
    spilled = from_behind(extended[planes], "bx", 1)
    density = extended[:planes].at[0].add(spilled)
    padded = with_halo(density, (("bx", 0),), 1)
    misfit = blur_sheet(blur_planes(padded)) - density_map
    misfit_wide = with_halo(misfit, (("bx", 0),), 1)
    pulled = blur_sheet(blur_planes(misfit_wide))
    above = from_behind(pulled[0], "bx", -1)
    field = jnp.concatenate([pulled, above[None]], 0)
    flat = field.reshape(-1)
    totals = [jnp.zeros_like(amplitude) for _ in range(3)]
    for lifts, weights, target in listing:
        sampled = flat[target]
        others = (weights[1] * weights[2], weights[0] * weights[2], weights[0] * weights[1])
        for which in range(3):
            sign = 1.0 if lifts[which] else -1.0
            totals[which] = totals[which] + sampled * sign * others[which]
    return jnp.stack([amplitude * item for item in totals])


def send_back(values):
    return lax.all_to_all(values, "bx", split_axis=1, concat_axis=1, tiled=True)


def cross_rows(left, right):
    return jnp.stack(
        [
            left[1] * right[2] - left[2] * right[1],
            left[2] * right[0] - left[0] * right[2],
            left[0] * right[1] - left[1] * right[0],
        ]
    )


def join_chain(earlier, later):
    return (later[0], later[1] + jnp.where(earlier[0] == later[0], earlier[1], 0.0))


def chain_suffix(values, chains):
    flipped = (chains[::-1][None, :], values[:, ::-1])
    result = lax.associative_scan(join_chain, flipped, axis=1)
    return result[1][:, ::-1]


def combine_blocks(earlier, later):
    higher_ids, higher_sums = earlier
    lower_ids, lower_sums = later
    lower_empty = lower_ids[..., 0] < 0.0
    higher_empty = higher_ids[..., 0] < 0.0
    first_chain = jnp.where(lower_empty, higher_ids[..., 0], lower_ids[..., 0])
    last_chain = jnp.where(higher_empty, lower_ids[..., 1], higher_ids[..., 1])
    joined = (
        ~lower_empty
        & ~higher_empty
        & (lower_ids[..., 0] == lower_ids[..., 1])
        & (lower_ids[..., 1] == higher_ids[..., 0])
    )
    sums = jnp.where(
        lower_empty[..., None],
        higher_sums,
        lower_sums + jnp.where(joined[..., None], higher_sums, 0.0),
    )
    return (jnp.stack([first_chain, last_chain], -1), sums)


def shards(
    density_map,
    amplitude,
    fraction,
    torsion_axis,
    brick_owner,
    plane_offset,
    row_offset,
    column_offset,
    chain_index,
):
    planes, rows, columns = density_map.shape
    atom_count = amplitude.shape[0]
    devices = lax.axis_size("bx")
    capacity = 3 * atom_count // devices
    slots = devices * capacity
    target_brick = brick_owner[:, 0]
    onehot = (target_brick[:, None] == jnp.arange(devices, dtype=jnp.int32)[None, :]).astype(
        jnp.int32
    )
    ranking = jnp.sum(jnp.cumsum(onehot, 0) * onehot, 1) - 1
    slot_of = target_brick * capacity + ranking
    cells = plane_offset * (rows * columns) + row_offset * columns + column_offset
    outgoing = (
        jnp.zeros((4, slots), jnp.float32)
        .at[:, slot_of]
        .set(jnp.concatenate([fraction, amplitude[None]], 0))
    )
    cells_out = jnp.zeros((1, slots), jnp.int32).at[0, slot_of].set(cells)
    incoming, cells_in = (
        lax.all_to_all(outgoing, "bx", split_axis=1, concat_axis=1, tiled=True),
        lax.all_to_all(cells_out, "bx", split_axis=1, concat_axis=1, tiled=True),
    )
    cells_in = cells_in[0]
    weight_in = incoming[3]
    first_gradient = evaluate(incoming[:3], weight_in, cells_in, density_map)
    returned = send_back(first_gradient)[:, slot_of]
    moved = fraction - probe_step * jnp.tanh(returned)
    resend = jnp.zeros((3, slots), jnp.float32).at[:, slot_of].set(moved)
    moved_in = lax.all_to_all(resend, "bx", split_axis=1, concat_axis=1, tiled=True)
    second_gradient = evaluate(moved_in, weight_in, cells_in, density_map)
    gradients = jnp.concatenate([returned, send_back(second_gradient)[:, slot_of]], 0)
    base_cells = jnp.stack(
        [
            (target_brick * planes + plane_offset).astype(jnp.float32),
            row_offset.astype(jnp.float32),
            column_offset.astype(jnp.float32),
        ]
    )
    positions = (base_cells + fraction, base_cells + moved)
    pieces = []
    for which in range(2):
        pieces.append(gradients[3 * which : 3 * which + 3])
        pieces.append(cross_rows(positions[which], gradients[3 * which : 3 * which + 3]))
    pieces.append(jnp.ones((1, atom_count), jnp.float32))
    local_sums = chain_suffix(jnp.concatenate(pieces, 0), chain_index)
    block_ids = jnp.stack([chain_index[0], chain_index[-1]]).astype(jnp.float32)
    head_sums = local_sums[:, 0]
    empty_ids = jnp.full((2,), -1.0, jnp.float32)
    empty_sums = jnp.zeros_like(head_sums)
    carry_ids, carry_sums = prefix(
        (block_ids, head_sums), "bx", combine_blocks, (empty_ids, empty_sums)
    )
    continues = (chain_index.astype(jnp.float32) == carry_ids[0]).astype(jnp.float32)
    totals = local_sums + continues[None, :] * carry_sums[:, None]
    torques = []
    for which in range(2):
        force = totals[6 * which : 6 * which + 3]
        moment = totals[6 * which + 3 : 6 * which + 6]
        lever = cross_rows(positions[which], force)
        torques.append(
            jnp.sum(torsion_axis * (moment - lever), 0) / (columns * jnp.sqrt(totals[12]))
        )
    return (jnp.stack(torques), gradients)


def solution(mesh):
    return jax.shard_map(
        shards,
        mesh=mesh,
        in_specs=(
            P(("grp", "bx"), None, None),
            P(("grp", "bx")),
            P(None, ("grp", "bx")),
            P(None, ("grp", "bx")),
            P(("grp", "bx"), None),
            P(("grp", "bx")),
            P(("grp", "bx")),
            P(("grp", "bx")),
            P(("grp", "bx")),
        ),
        out_specs=(P(None, ("grp", "bx")), P(None, ("grp", "bx"))),
        check_vma=False,
    )
```

profile of v0, /device:TPU:0, one launch (start us, length us, event | category | flops | bytes accessed | tf_op | source)
XLA Modules:
  0.0 1593.4 jit_solution(7066892333019502718)
XLA Ops:
  1.3 4.5 reduce-window.6
  9.6 1.4 add_convert_fusion
  11.0 8.6 scatter_custom_fusion.4
  19.6 7.4 all-to-all-start.1
  33.1 1.4 fusion.138
  51.0 1.4 copy.342
  52.3 6.7 scatter_custom_fusion
  59.1 1.8 copy.343
  60.9 6.0 all-to-all-start
  68.4 5.9 all-to-all-done
  74.5 290.3 %scatter_custom_fusion.1 = f32[81920]{0:T(1024)S(1)} fusion(s32[49152]{0:T(1024)S(1)} %bitcast.227, f32[49152]{0:T(1024)S(1)} %multiply_dynamic-update-slice_fusion.8, f32[]{:T(128)} %constant.285.clone.1), kind=kCustom, calls=%fused_computation.95 | custom fusion | flops 49152 | bytes 327684 | tf_op jit(solution)/shard_map/scatter-add | solution.py:85
  364.9 1.4 collective-permute-start
  367.2 33.1 %collective-permute-start.1 = (f32[1,64,256]{2,1,0:T(8,128)S(1)}, f32[1,64,256]{2,1,0:T(8,128)S(1)}, u32[]{:S(2)}, u32[]{:S(2)}) collective-permute-start(f32[1,64,256]{2,1,0:T(8,128)S(1)} %slice.1071), channel_id=1, source_target_pairs={{0,1},{1,2},{2,3},{3,4},{4,5},{5,6},{6,7},{7,8},{8,9},{9,10},{10,1... | collective-permute-start | bytes 196616 | tf_op jit(solution)/shard_map/ppermute | solution.py:24
  401.7 6.5 collective-permute-done.2
  408.9 4.8 collective-permute-start.3
  413.7 1.3 collective-permute-start.4
  415.1 2.1 collective-permute-done.4
  417.8 1.5 collective-permute-start.5
  419.4 6.1 collective-permute-done.5
  425.7 34.3 %gather_fusion.1 = f32[6144]{0:T(1024)S(1)} fusion(f32[81920]{0:T(1024)S(1)} %bitcast.150, s32[6144]{0:T(1024)S(1)} %broadcast_clamp_fusion.6), kind=kCustom, calls=%fused_computation.1 | custom fusion | bytes 73728 | tf_op jit(solution)/shard_map/gather | solution.py:98
  460.0 34.3 %gather_fusion = f32[6144]{0:T(1024)S(1)} fusion(f32[81920]{0:T(1024)S(1)} %bitcast.151, s32[6144]{0:T(1024)S(1)} %broadcast_clamp_fusion.7), kind=kCustom, calls=%fused_computation | custom fusion | bytes 73728 | tf_op jit(solution)/shard_map/gather | solution.py:98
  494.4 34.3 %gather_fusion.2 = f32[6144]{0:T(1024)S(1)} fusion(f32[81920]{0:T(1024)S(1)} %bitcast.152, s32[6144]{0:T(1024)S(1)} %broadcast_clamp_fusion.5), kind=kCustom, calls=%fused_computation.2 | custom fusion | bytes 73728 | tf_op jit(solution)/shard_map/gather | solution.py:98
  528.7 34.3 %gather_fusion.3 = f32[6144]{0:T(1024)S(1)} fusion(f32[81920]{0:T(1024)S(1)} %bitcast.153, s32[6144]{0:T(1024)S(1)} %broadcast_clamp_fusion.4), kind=kCustom, calls=%fused_computation.3 | custom fusion | bytes 73728 | tf_op jit(solution)/shard_map/gather | solution.py:98
  563.0 34.3 %gather_fusion.4 = f32[6144]{0:T(1024)S(1)} fusion(f32[81920]{0:T(1024)S(1)} %bitcast.154, s32[6144]{0:T(1024)S(1)} %broadcast_clamp_fusion.3), kind=kCustom, calls=%fused_computation.4 | custom fusion | bytes 73728 | tf_op jit(solution)/shard_map/gather | solution.py:98
  597.3 34.3 %gather_fusion.5 = f32[6144]{0:T(1024)S(1)} fusion(f32[81920]{0:T(1024)S(1)} %bitcast.155, s32[6144]{0:T(1024)S(1)} %broadcast_clamp_fusion.2), kind=kCustom, calls=%fused_computation.5 | custom fusion | bytes 73728 | tf_op jit(solution)/shard_map/gather | solution.py:98
  631.6 34.3 %gather_fusion.6 = f32[6144]{0:T(1024)S(1)} fusion(f32[81920]{0:T(1024)S(1)} %bitcast.156, s32[6144]{0:T(1024)S(1)} %broadcast_clamp_fusion.1), kind=kCustom, calls=%fused_computation.6 | custom fusion | bytes 73728 | tf_op jit(solution)/shard_map/gather | solution.py:98
  666.0 34.3 %gather_fusion.7 = f32[6144]{0:T(1024)S(1)} fusion(f32[81920]{0:T(1024)S(1)} %bitcast.157, s32[6144]{0:T(1024)S(1)} %broadcast_clamp_fusion), kind=kCustom, calls=%fused_computation.7 | custom fusion | bytes 73728 | tf_op jit(solution)/shard_map/gather | solution.py:98
  701.0 7.3 all-to-all-start.2
  710.4 5.4 all-to-all-done.2
  716.8 8.3 gather_fusion.8
  725.2 1.6 copy.350
  726.7 1.5 fusion.82
  728.2 1.4 copy.351
  729.6 6.7 scatter_custom_fusion.2
  736.4 1.8 copy.352
  738.1 3.6 all-to-all-start.3
  741.8 1.4 fusion.109
  747.1 21.6 %all-gather.1 = f32[16,1,2]{2,1,0:T(1,128)S(1)} all-gather(f32[1,1,2]{2,1,0:T(1,128)S(1)} %fusion.109), channel_id=1, replica_groups=mesh['grp'=2,'bx'=16] {'bx'}, dimensions={0}, use_global_device_ids=true | all-gather | bytes 136 | tf_op jit(solution)/shard_map/all_gather | solution.py:34
  771.4 290.7 %scatter_custom_fusion.3 = f32[81920]{0:T(1024)S(1)} fusion(s32[49152]{0:T(1024)} %bitcast.228, f32[49152]{0:T(1024)S(1)} %multiply_dynamic-update-slice_fusion, f32[]{:T(128)} %constant.285.clone.1), kind=kCustom, calls=%fused_computation.93 | custom fusion | flops 49152 | bytes 328192 | tf_op jit(solution)/shard_map/scatter-add | solution.py:85
  1062.1 1.3 collective-permute-start.6
  1064.8 30.8 %collective-permute-start.7 = (f32[1,64,256]{2,1,0:T(8,128)S(1)}, f32[1,64,256]{2,1,0:T(8,128)S(1)}, u32[]{:S(2)}, u32[]{:S(2)}) collective-permute-start(f32[1,64,256]{2,1,0:T(8,128)S(1)} %slice.1103), channel_id=1, source_target_pairs={{0,1},{1,2},{2,3},{3,4},{4,5},{5,6},{6,7},{7,8},{8,9},{9,10},{10,1... | collective-permute-start | bytes 196616 | tf_op jit(solution)/shard_map/ppermute | solution.py:24
  1097.4 6.4 collective-permute-done.8
  1105.8 5.5 collective-permute-start.9
  1112.9 1.7 collective-permute-start.11
  1114.6 3.5 collective-permute-done.11
  1118.3 34.3 %gather_fusion.10 = f32[6144]{0:T(1024)S(1)} fusion(f32[81920]{0:T(1024)S(1)} %bitcast.158, s32[6144]{0:T(1024)S(1)} %copy-done.2), kind=kCustom, calls=%fused_computation.10 | custom fusion | bytes 73728 | tf_op jit(solution)/shard_map/gather | solution.py:98
  1152.6 34.3 %gather_fusion.11 = f32[6144]{0:T(1024)S(1)} fusion(f32[81920]{0:T(1024)S(1)} %bitcast.159, s32[6144]{0:T(1024)S(1)} %copy-done.6), kind=kCustom, calls=%fused_computation.11 | custom fusion | bytes 73728 | tf_op jit(solution)/shard_map/gather | solution.py:98
  1186.9 34.3 %gather_fusion.9 = f32[6144]{0:T(1024)S(1)} fusion(f32[81920]{0:T(1024)S(1)} %bitcast.160, s32[6144]{0:T(1024)S(1)} %broadcast_clamp_fusion.7), kind=kCustom, calls=%fused_computation.9 | custom fusion | bytes 73728 | tf_op jit(solution)/shard_map/gather | solution.py:98
  1221.2 34.3 %gather_fusion.12 = f32[6144]{0:T(1024)S(1)} fusion(f32[81920]{0:T(1024)S(1)} %bitcast.161, s32[6144]{0:T(1024)S(1)} %copy-done.4), kind=kCustom, calls=%fused_computation.12 | custom fusion | bytes 73728 | tf_op jit(solution)/shard_map/gather | solution.py:98
  1255.5 34.3 %gather_fusion.13 = f32[6144]{0:T(1024)S(1)} fusion(f32[81920]{0:T(1024)S(1)} %bitcast.162, s32[6144]{0:T(1024)S(1)} %copy-done.8), kind=kCustom, calls=%fused_computation.13 | custom fusion | bytes 73728 | tf_op jit(solution)/shard_map/gather | solution.py:98
  1289.8 34.3 %gather_fusion.14 = f32[6144]{0:T(1024)S(1)} fusion(f32[81920]{0:T(1024)S(1)} %bitcast.163, s32[6144]{0:T(1024)S(1)} %copy-done.10), kind=kCustom, calls=%fused_computation.14 | custom fusion | bytes 73728 | tf_op jit(solution)/shard_map/gather | solution.py:98
  1324.2 34.3 %gather_fusion.15 = f32[6144]{0:T(1024)S(1)} fusion(f32[81920]{0:T(1024)S(1)} %bitcast.164, s32[6144]{0:T(1024)S(1)} %copy-done.12), kind=kCustom, calls=%fused_computation.15 | custom fusion | bytes 73728 | tf_op jit(solution)/shard_map/gather | solution.py:98
  1358.5 34.3 %gather_fusion.16 = f32[6144]{0:T(1024)S(1)} fusion(f32[81920]{0:T(1024)S(1)} %bitcast.165, s32[6144]{0:T(1024)S(1)} %copy-done.14), kind=kCustom, calls=%fused_computation.16 | custom fusion | bytes 73728 | tf_op jit(solution)/shard_map/gather | solution.py:98
  1393.7 10.5 all-to-all-start.4
  1404.4 7.2 all-to-all-done.4
  1412.7 7.6 gather_fusion.17
  1420.3 1.6 copy.358
  1422.8 1.8 slice.942
  1424.6 1.8 slice.945
  1436.0 1.8 slice.908
  1444.4 2.0 pad.173
  1447.2 1.8 pad.172
  1449.5 30.0 %all-reduce.43 = f32[208]{0:T(256)S(1)} all-reduce(f32[208]{0:T(256)S(1)} %dynamic-update-slice.6), channel_id=2, replica_groups=mesh['grp'=2,'bx'=16] {'bx'}, use_global_device_ids=true, to_apply=%add.43 | all-reduce | flops 208 | bytes 1664
  1479.5 111.5 %while.16 = (s32[]{:T(128)}, f32[2]{0:T(128)S(1)}, f32[13]{0:T(128)S(1)}, s32[]{:T(128)}, f32[16,2]{0,1:T(2,128)S(1)}, /*index=5*/f32[16,13]{1,0:T(8,128)S(1)}, ...) while((s32[]{:T(128)}, f32[2]{0:T(128)S(1)}, f32[13]{0:T(128)S(1)}, s32[]{:T(128)}, ...), condition=%wide.region_9.10_spmd, body=%wide.region_8.9_spmd.sunk | while | flops 58 | bytes 460 | solution.py:43
  (547 shorter events, 88.3 us)
Async XLA Ops:
  8.1 52.8 %copy-start.18 = (s32[2048,1]{0,1:T(1,128)}, s32[2048,1]{0,1:T(1,128)S(1)}, u32[]{:S(2)}) copy-start(s32[2048,1]{0,1:T(1,128)S(1)} %compare_select_fusion.19) | copy-start | bytes 24580
  19.6 41.2 %all-to-all-start.1 = ((s32[1,16,384]{2,0,1:T(1,128)}), s32[1,16,384]{2,0,1:T(1,128)S(1)}, u32[]{:S(2)}, u32[]{:S(2)}) async-start(s32[1,16,384]{2,0,1:T(1,128)} %bitcast.15), calls=%async_computation.1 | async-start | bytes 49152 | tf_op jit(solution)/shard_map/all_to_all | solution.py:182
  28.5 22.5 %copy-start.39 = (s32[1,256]{1,0:T(1,128)}, s32[1,256]{1,0:T(1,128)S(1)}, u32[]{:S(2)}) copy-start(s32[1,256]{1,0:T(1,128)S(1)} %slice.916) | copy-start | bytes 3076
  31.7 19.3 %copy-start.63 = (s32[1,127]{1,0:T(1,128)}, s32[1,127]{1,0:T(1,128)S(1)}, u32[]{:S(2)}) copy-start(s32[1,127]{1,0:T(1,128)S(1)} %slice.918) | copy-start | bytes 1528
  60.9 13.4 all-to-all-start
  67.3 297.5 %copy-start.17 = (s32[49152,1]{0,1:T(1,128)}, s32[49152,1]{0,1:T(1,128)S(1)}, u32[]{:S(2)}) copy-start(s32[49152,1]{0,1:T(1,128)S(1)} %compare_select_fusion) | copy-start | bytes 589828
  68.3 357.4 %copy-start.1 = (s32[6144]{0:T(1024)}, s32[6144]{0:T(1024)S(1)}, u32[]{:S(2)}) copy-start(s32[6144]{0:T(1024)S(1)} %broadcast_clamp_fusion.6) | copy-start | bytes 73732
  68.3 426.0 %copy-start.5 = (s32[6144]{0:T(1024)}, s32[6144]{0:T(1024)S(1)}, u32[]{:S(2)}) copy-start(s32[6144]{0:T(1024)S(1)} %broadcast_clamp_fusion.5) | copy-start | bytes 73732
  68.3 460.3 %copy-start.3 = (s32[6144]{0:T(1024)}, s32[6144]{0:T(1024)S(1)}, u32[]{:S(2)}) copy-start(s32[6144]{0:T(1024)S(1)} %broadcast_clamp_fusion.4) | copy-start | bytes 73732
  364.9 43.8 %copy-start = (f32[4,64,256]{2,1,0:T(8,128)S(1)}, f32[4,64,256]{2,1,0:T(8,128)}, u32[]{:S(2)}) copy-start(f32[4,64,256]{2,1,0:T(8,128)} %param.15) | copy-start | bytes 786436
  364.9 2.3 collective-permute-start
  366.3 196.6 %copy-start.7 = (s32[6144]{0:T(1024)}, s32[6144]{0:T(1024)S(1)}, u32[]{:S(2)}) copy-start(s32[6144]{0:T(1024)S(1)} %broadcast_clamp_fusion.3) | copy-start | bytes 73732
  367.2 34.4 %collective-permute-start.1 = (f32[1,64,256]{2,1,0:T(8,128)S(1)}, f32[1,64,256]{2,1,0:T(8,128)S(1)}, u32[]{:S(2)}, u32[]{:S(2)}) collective-permute-start(f32[1,64,256]{2,1,0:T(8,128)S(1)} %slice.1071), channel_id=1, source_target_pairs={{0,1},{1,2},{2,3},{3,4},{4,5},{5,6},{6,7},{7,8},{8,9},{9,10},{10,1... | collective-permute-start | bytes 196616 | tf_op jit(solution)/shard_map/ppermute | solution.py:24
  400.3 7.9 collective-permute-start.2
  401.6 195.7 %copy-start.9 = (s32[6144]{0:T(1024)}, s32[6144]{0:T(1024)S(1)}, u32[]{:S(2)}) copy-start(s32[6144]{0:T(1024)S(1)} %broadcast_clamp_fusion.2) | copy-start | bytes 73732
  408.9 6.2 collective-permute-start.3
  413.7 3.4 collective-permute-start.4
  415.0 216.6 %copy-start.11 = (s32[6144]{0:T(1024)}, s32[6144]{0:T(1024)S(1)}, u32[]{:S(2)}) copy-start(s32[6144]{0:T(1024)S(1)} %broadcast_clamp_fusion.1) | copy-start | bytes 73732
  417.8 7.7 collective-permute-start.5
  419.3 246.6 %copy-start.13 = (s32[6144]{0:T(1024)}, s32[6144]{0:T(1024)S(1)}, u32[]{:S(2)}) copy-start(s32[6144]{0:T(1024)S(1)} %broadcast_clamp_fusion) | copy-start | bytes 73732
  665.9 42.5 %copy-start.64 = (s32[1,127]{1,0:T(1,128)S(1)}, s32[1,127]{1,0:T(1,128)}, u32[]{:S(2)}) copy-start(s32[1,127]{1,0:T(1,128)} %copy-done.63) | copy-start | bytes 1528
  665.9 43.7 %copy-start.21 = (s32[2048]{0:T(1024)S(1)}, s32[2048]{0:T(1024)}, u32[]{:S(2)}) copy-start(s32[2048]{0:T(1024)} %copy-done.20) | copy-start | bytes 24580
  666.0 43.9 %copy-start.24 = (s32[1,1024]{1,0:T(1,128)S(1)}, s32[1,1024]{1,0:T(1,128)}, u32[]{:S(2)}) copy-start(s32[1,1024]{1,0:T(1,128)} %copy-done.23) | copy-start | bytes 12292
  701.0 14.8 all-to-all-start.2
  729.6 39.7 %copy-start.60 = (u32[32]{0:T(128)S(1)}, u32[32]{0:T(128)}, u32[]{:S(2)}) copy-start(u32[32]{0:T(128)} %constant.406) | copy-start | bytes 388
  738.1 358.8 %copy-start.31 = (s32[1,512]{1,0:T(1,128)S(1)}, s32[1,512]{1,0:T(1,128)}, u32[]{:S(2)}) copy-start(s32[1,512]{1,0:T(1,128)} %copy-done.29) | copy-start | bytes 6148
  738.1 33.0 %all-to-all-start.3 = ((f32[3,16,384]{2,0,1:T(4,128)}), f32[3,16,384]{2,0,1:T(4,128)S(1)}, u32[]{:S(2)}, u32[]{:S(2)}) async-start(f32[3,16,384]{2,0,1:T(4,128)} %copy.352), calls=%async_computation.3 | async-start | bytes 196608 | tf_op jit(solution)/shard_map/all_to_all | solution.py:190
  1062.1 2.6 collective-permute-start.6
  1064.8 32.6 %collective-permute-start.7 = (f32[1,64,256]{2,1,0:T(8,128)S(1)}, f32[1,64,256]{2,1,0:T(8,128)S(1)}, u32[]{:S(2)}, u32[]{:S(2)}) collective-permute-start(f32[1,64,256]{2,1,0:T(8,128)S(1)} %slice.1103), channel_id=1, source_target_pairs={{0,1},{1,2},{2,3},{3,4},{4,5},{5,6},{6,7},{7,8},{8,9},{9,10},{10,1... | collective-permute-start | bytes 196616 | tf_op jit(solution)/shard_map/ppermute | solution.py:24
  1095.6 8.2 collective-permute-start.8
  1104.5 7.3 collective-permute-start.10
  1105.8 6.4 collective-permute-start.9
  1112.9 5.2 collective-permute-start.11
  1118.3 34.3 %copy-start.6 = (s32[6144]{0:T(1024)S(1)}, s32[6144]{0:T(1024)}, u32[]{:S(2)}) copy-start(s32[6144]{0:T(1024)} %copy-done.5) | copy-start | bytes 73732
  1186.9 34.3 %copy-start.4 = (s32[6144]{0:T(1024)S(1)}, s32[6144]{0:T(1024)}, u32[]{:S(2)}) copy-start(s32[6144]{0:T(1024)} %copy-done.3) | copy-start | bytes 73732
  1221.2 34.3 %copy-start.8 = (s32[6144]{0:T(1024)S(1)}, s32[6144]{0:T(1024)}, u32[]{:S(2)}) copy-start(s32[6144]{0:T(1024)} %copy-done.7) | copy-start | bytes 73732
  1255.5 34.3 %copy-start.10 = (s32[6144]{0:T(1024)S(1)}, s32[6144]{0:T(1024)}, u32[]{:S(2)}) copy-start(s32[6144]{0:T(1024)} %copy-done.9) | copy-start | bytes 73732
  1289.8 34.3 %copy-start.12 = (s32[6144]{0:T(1024)S(1)}, s32[6144]{0:T(1024)}, u32[]{:S(2)}) copy-start(s32[6144]{0:T(1024)} %copy-done.11) | copy-start | bytes 73732
  1324.1 34.3 %copy-start.14 = (s32[6144]{0:T(1024)S(1)}, s32[6144]{0:T(1024)}, u32[]{:S(2)}) copy-start(s32[6144]{0:T(1024)} %copy-done.13) | copy-start | bytes 73732
  1358.5 45.7 %copy-start.15 = (f32[3,2048]{1,0:T(4,128)S(1)}, f32[3,2048]{1,0:T(4,128)}, u32[]{:S(2)}) copy-start(f32[3,2048]{1,0:T(4,128)} %get-tuple-element.224) | copy-start | bytes 73732
  1392.8 19.9 %copy-start.19 = (s32[2048]{0:T(1024)S(1)}, s32[2048]{0:T(1024)}, u32[]{:S(2)}) copy-start(s32[2048]{0:T(1024)} %broadcast_clamp_fusion.8) | copy-start | bytes 24580
  1392.8 29.7 %copy-start.16 = (f32[3,2048]{1,0:T(4,128)S(1)}, f32[3,2048]{1,0:T(4,128)}, u32[]{:S(2)}) copy-start(f32[3,2048]{1,0:T(4,128)} %get-tuple-element.219) | copy-start | bytes 73732
  1393.0 34.8 %copy-start.36 = (pred[1024]{0:T(1024)(128)(4,1)S(1)}, pred[1024]{0:T(1024)(128)(4,1)}, u32[]{:S(2)}) copy-start(pred[1024]{0:T(1024)(128)(4,1)} %compare_reduce_fusion) | copy-start | bytes 3076
  1393.7 36.2 %copy-start.42 = (pred[512]{0:T(512)(128)(4,1)S(1)}, pred[512]{0:T(512)(128)(4,1)}, u32[]{:S(2)}) copy-start(pred[512]{0:T(512)(128)(4,1)} %compare_reduce_fusion.2) | copy-start | bytes 1540
  1393.7 17.9 %all-to-all-start.4 = ((f32[3,16,384]{2,0,1:T(4,128)}), f32[3,16,384]{2,0,1:T(4,128)S(1)}, u32[]{:S(2)}, u32[]{:S(2)}) async-start(f32[3,16,384]{2,0,1:T(4,128)} %copy.356), calls=%async_computation.4 | async-start | bytes 196608 | tf_op jit(solution)/shard_map/all_to_all | solution.py:107
  1404.2 27.7 %copy-start.56 = (pred[128]{0:T(512)(128)(4,1)S(1)}, pred[128]{0:T(512)(128)(4,1)}, u32[]{:S(2)}) copy-start(pred[128]{0:T(512)(128)(4,1)} %compare_bitcast_fusion.11) | copy-start | bytes 388
  1404.3 28.0 %copy-start.55 = (pred[64]{0:T(512)(128)(4,1)S(1)}, pred[64]{0:T(512)(128)(4,1)}, u32[]{:S(2)}) copy-start(pred[64]{0:T(512)(128)(4,1)} %compare_bitcast_fusion.9) | copy-start | bytes 196
  1404.3 28.3 %copy-start.54 = (pred[32]{0:T(512)(128)(4,1)S(1)}, pred[32]{0:T(512)(128)(4,1)}, u32[]{:S(2)}) copy-start(pred[32]{0:T(512)(128)(4,1)} %compare_bitcast_fusion.7) | copy-start | bytes 100
  1404.3 28.5 %copy-start.53 = (pred[16]{0:T(512)(128)(4,1)S(1)}, pred[16]{0:T(512)(128)(4,1)}, u32[]{:S(2)}) copy-start(pred[16]{0:T(512)(128)(4,1)} %compare_bitcast_fusion.5) | copy-start | bytes 52
  1404.3 28.7 %copy-start.52 = (pred[8]{0:T(512)(128)(4,1)S(1)}, pred[8]{0:T(512)(128)(4,1)}, u32[]{:S(2)}) copy-start(pred[8]{0:T(512)(128)(4,1)} %compare_bitcast_fusion.3) | copy-start | bytes 28
  1404.3 28.9 %copy-start.51 = (pred[4]{0:T(512)(128)(4,1)S(1)}, pred[4]{0:T(512)(128)(4,1)}, u32[]{:S(2)}) copy-start(pred[4]{0:T(512)(128)(4,1)} %compare_bitcast_fusion.1) | copy-start | bytes 16
  1404.3 33.6 %copy-start.50 = (pred[2]{0:T(512)(128)(4,1)S(1)}, pred[2]{0:T(512)(128)(4,1)}, u32[]{:S(2)}) copy-start(pred[2]{0:T(512)(128)(4,1)} %compare_bitcast_fusion) | copy-start | bytes 10
  1404.3 34.1 %copy-start.48 = (pred[3]{0:T(512)(128)(4,1)S(1)}, pred[3]{0:T(512)(128)(4,1)}, u32[]{:S(2)}) copy-start(pred[3]{0:T(512)(128)(4,1)} %compare_bitcast_fusion.2) | copy-start | bytes 13
  1404.3 34.3 %copy-start.49 = (pred[7]{0:T(512)(128)(4,1)S(1)}, pred[7]{0:T(512)(128)(4,1)}, u32[]{:S(2)}) copy-start(pred[7]{0:T(512)(128)(4,1)} %compare_bitcast_fusion.4) | copy-start | bytes 25
  1404.3 34.7 %copy-start.46 = (pred[15]{0:T(512)(128)(4,1)S(1)}, pred[15]{0:T(512)(128)(4,1)}, u32[]{:S(2)}) copy-start(pred[15]{0:T(512)(128)(4,1)} %compare_bitcast_fusion.6) | copy-start | bytes 49
  1404.3 34.9 %copy-start.47 = (pred[31]{0:T(512)(128)(4,1)S(1)}, pred[31]{0:T(512)(128)(4,1)}, u32[]{:S(2)}) copy-start(pred[31]{0:T(512)(128)(4,1)} %compare_bitcast_fusion.8) | copy-start | bytes 97
  1404.4 35.4 %copy-start.44 = (pred[63]{0:T(512)(128)(4,1)S(1)}, pred[63]{0:T(512)(128)(4,1)}, u32[]{:S(2)}) copy-start(pred[63]{0:T(512)(128)(4,1)} %compare_bitcast_fusion.10) | copy-start | bytes 193
  1404.4 35.8 %copy-start.45 = (pred[127]{0:T(512)(128)(4,1)S(1)}, pred[127]{0:T(512)(128)(4,1)}, u32[]{:S(2)}) copy-start(pred[127]{0:T(512)(128)(4,1)} %compare_bitcast_fusion.12) | copy-start | bytes 385
  1412.6 28.9 %copy-start.41 = (pred[255]{0:T(512)(128)(4,1)S(1)}, pred[255]{0:T(512)(128)(4,1)}, u32[]{:S(2)}) copy-start(pred[255]{0:T(512)(128)(4,1)} %compare_reduce_fusion.5) | copy-start | bytes 769
  1412.6 29.6 %copy-start.43 = (pred[511]{0:T(512)(128)(4,1)S(1)}, pred[511]{0:T(512)(128)(4,1)}, u32[]{:S(2)}) copy-start(pred[511]{0:T(512)(128)(4,1)} %compare_reduce_fusion.3) | copy-start | bytes 1537
  1412.7 34.3 %copy-start.37 = (pred[1023]{0:T(1024)(128)(4,1)S(1)}, pred[1023]{0:T(1024)(128)(4,1)}, u32[]{:S(2)}) copy-start(pred[1023]{0:T(1024)(128)(4,1)} %compare_reduce_fusion.1) | copy-start | bytes 3073
  1420.3 59.3 %copy-start.27 = (f32[16,1,2]{0,2,1:T(2,128)S(1)}, f32[16,1,2]{0,2,1:T(2,128)}, u32[]{:S(2)}) copy-start(f32[16,1,2]{0,2,1:T(2,128)} %copy.359) | copy-start | bytes 388
  1421.8 169.2 %copy-start.26 = (s32[2048]{0:T(1024)S(1)}, s32[2048]{0:T(1024)}, u32[]{:S(2)}) copy-start(s32[2048]{0:T(1024)} %param.23) | copy-start | bytes 24580
  1422.8 169.6 %copy-start.28 = (f32[3,2048]{1,0:T(4,128)S(1)}, f32[3,2048]{1,0:T(4,128)}, u32[]{:S(2)}) copy-start(f32[3,2048]{1,0:T(4,128)} %param.18) | copy-start | bytes 73732
  (18 other events, 257.2 us)
where the time goes:
time: 1610 us; the launch traced here: 1590 us
  local copies, waits for them, and re-layouts  660 us (41%)
  other arithmetic  620 us (39%)
  starting transfers between devices  120 us (7%)
  loops' own time  91.9 us (6%)
  blocking collectives  51.6 us (3%)
  waiting for transfers between devices  44.2 us (3%)
    scatter-add x2, other arithmetic, evaluate(): jnp.zeros(((planes + 1) * rows * columns,), jnp.float32).at[targets]  581 us
    gather x30, local copies, waits for them, and re-layouts, evaluate(): sampled = flat[target]  549 us
    another operation x1, loops' own time, prefix(): return lax.fori_loop(0, ahead, one, state)  91.9 us
    ppermute x4, starting transfers between devices, with_halo(): before = lax.ppermute(last, axis, up)  74.2 us
  transfers between devices with their start and end apart: 17, of which 10 were waited for; matrix products, arithmetic and copies ran while one was open for 3% of the time, Pallas kernels for 0%

commit v1 on v0

v1 whole, which is shorter than its diff:
```python
import functools

import jax
import jax.numpy as jnp
from jax import lax
from jax.experimental import pallas as pl
from jax.experimental.pallas import tpu as pltpu
from jax.sharding import PartitionSpec as P

side_tap = 0.25
middle_tap = 0.5
probe_step = 0.2
lanes = 128
fields = 8
f32, bf16 = jnp.float32, jnp.bfloat16
room = 48 * 1024 * 1024


def dot_nt(left, right):
    return lax.dot_general(left, right, (((1,), (1,)), ((), ())), preferred_element_type=f32)


def dot_nn(left, right):
    return lax.dot_general(left, right, (((1,), (0,)), ((), ())), preferred_element_type=f32)


def halves(x):
    high = x.astype(bf16)
    return high, (x - high.astype(f32)).astype(bf16)


def thirds(x):
    high, rest = x.astype(bf16), None
    rest = x - high.astype(f32)
    middle = rest.astype(bf16)
    return high, middle, (rest - middle.astype(f32)).astype(bf16)


def down_rows(count, width):
    return lax.broadcasted_iota(jnp.int32, (count, width), 0)


def spread(row, count):
    tile = jnp.broadcast_to(row, (16, row.shape[1])).astype(bf16)
    return jnp.concatenate([tile] * (count // 16), 0)


def counting(count, width):
    part = down_rows(count, lanes).astype(f32).astype(bf16)
    return jnp.concatenate([part] * (width // lanes), 1)


def pack_kernel(
    devices, sub, rows, owner_ref, plane_ref, row_ref, column_ref, chain_ref, amp_ref, frac_ref,
    message_ref, slot_ref,
):
    atoms = owner_ref.shape[1]
    blocks = atoms // lanes
    tiles = devices * sub
    owner = owner_ref[...]
    mine = down_rows(devices, atoms) == owner
    onehot = jnp.where(mine, 1.0, 0.0)
    stacked = jnp.concatenate(
        [onehot[:, j * lanes : (j + 1) * lanes] for j in range(blocks)], 0
    ).astype(bf16)
    k = lax.broadcasted_iota(jnp.int32, (lanes, 2 * lanes), 0)
    a = lax.broadcasted_iota(jnp.int32, (lanes, 2 * lanes), 1)
    before = jnp.where((k < a) | (a >= lanes), 1.0, 0.0).astype(bf16)
    counts = dot_nn(stacked, before)
    running = jnp.zeros((devices, lanes), f32)
    ranks = []
    for j in range(blocks):
        part = counts[j * devices : (j + 1) * devices]
        here = onehot[:, j * lanes : (j + 1) * lanes]
        ranks.append(jnp.sum((part[:, :lanes] + running) * here, 0, keepdims=True))
        running = running + part[:, lanes:]
    rank = jnp.concatenate(ranks, 1).astype(jnp.int32)
    tile = owner * sub + lax.shift_right_logical(rank, 7)
    lane = rank & (lanes - 1)
    slot_ref[...] = jnp.concatenate([tile, lane], 0)
    values = jnp.concatenate(
        [
            (plane_ref[...] * rows + row_ref[...]).astype(f32),
            column_ref[...].astype(f32),
            frac_ref[...],
            amp_ref[...],
            chain_ref[...].astype(f32),
            jnp.zeros((1, atoms), f32),
        ],
        0,
    )
    pieces = [piece.astype(f32) for piece in thirds(values)]
    width = 512
    for c in range(atoms // width):
        at = slice(c * width, (c + 1) * width)
        spot = jnp.where(down_rows(lanes, width) == lane[:, at], 1.0, 0.0).astype(bf16)
        which = jnp.broadcast_to(tile[:, at], (fields, width))
        picks = [which == t for t in range(tiles)]
        total = None
        for piece in pieces:
            part = piece[:, at]
            left = jnp.concatenate([jnp.where(pick, part, 0.0) for pick in picks], 0).astype(bf16)
            one = dot_nt(left, spot)
            total = one if total is None else total + one
        if c == 0:
            message_ref[...] = total
        else:
            message_ref[...] += total
    last = jnp.broadcast_to(chain_ref[:, atoms - 1 :].astype(f32), (1, lanes))
    for b in range(devices):
        message_ref[b * sub * fields + fields - 1 : b * sub * fields + fields, :] = last


def neighbours_of(state, rows, columns):
    cell, column = state[0:1], state[1:2]
    plane = jnp.floor(cell * (1.0 / rows))
    row = cell - plane * rows
    next_row = jnp.where(row == rows - 1.0, 0.0, row + 1.0)
    next_column = jnp.where(column == columns - 1.0, 0.0, column + 1.0)
    return plane, row, next_row, column, next_column


def density_part(state, planes, rows, columns):
    width = state.shape[1]
    plane, row, next_row, column, next_column = neighbours_of(state, rows, columns)
    fx, fy, fz, amplitude = (state[2 + i : 3 + i] for i in range(4))
    zero = jnp.zeros((), bf16)
    steps = counting(columns, width)
    here, there = steps == spread(column, columns), steps == spread(next_column, columns)

    def columns_of(near, far):
        return jnp.where(here, spread(near, columns), jnp.where(there, spread(far, columns), zero))

    near, far = halves(1.0 - fz), halves(fz)
    right_high = columns_of(near[0].astype(f32), far[0].astype(f32))
    right_low = columns_of(near[1].astype(f32), far[1].astype(f32))
    level = down_rows(fields, width).astype(f32)
    along = amplitude * jnp.where(level == plane, 1.0 - fx, jnp.where(level == plane + 1.0, fx, 0.0))
    near, far = halves(along * (1.0 - fy)), halves(along * fy)
    steps = counting(rows, width)
    here, there = steps == spread(row, rows), steps == spread(next_row, rows)
    lefts = []
    for grade in range(2):
        first, second = near[grade].astype(f32), far[grade].astype(f32)
        lefts.append(
            jnp.concatenate(
                [
                    jnp.where(
                        here,
                        spread(first[p : p + 1], rows),
                        jnp.where(there, spread(second[p : p + 1], rows), zero),
                    )
                    for p in range(planes + 1)
                ],
                0,
            )
        )
    return (
        dot_nt(lefts[0], right_high) + dot_nt(lefts[0], right_low) + dot_nt(lefts[1], right_high)
    )


def gradient_part(state, table_ref, planes, rows, columns):
    width = state.shape[1]
    plane, row, next_row, column, _ = neighbours_of(state, rows, columns)
    fx, fy, fz, amplitude = (state[2 + i : 3 + i] for i in range(4))
    spot = jnp.where(
        counting(columns, width) == spread(column, columns),
        jnp.ones((), bf16),
        jnp.zeros((), bf16),
    )
    sampled = dot_nn(table_ref[...], jnp.concatenate([spot, spot], 0))
    sheets = [sampled[i * rows : (i + 1) * rows] for i in range(2 * (planes + 1))]
    steps = down_rows(rows, width).astype(f32)
    at_plane = [jnp.broadcast_to(plane, (rows, width)) == float(p) for p in range(planes)]
    at_row = (steps == row, steps == next_row)
    corner = {}
    for e2 in range(2):
        for e0 in range(2):
            chosen = sheets[e2 * (planes + 1) + e0]
            for p in range(1, planes):
                chosen = jnp.where(at_plane[p], sheets[e2 * (planes + 1) + e0 + p], chosen)
            for e1 in range(2):
                corner[e0, e1, e2] = jnp.sum(jnp.where(at_row[e1], chosen, 0.0), 0, keepdims=True)
    wx, wy, wz = (1.0 - fx, fx), (1.0 - fy, fy), (1.0 - fz, fz)
    gx = gy = gz = 0.0
    for u in range(2):
        for v in range(2):
            gx = gx + wy[u] * wz[v] * (corner[1, u, v] - corner[0, u, v])
            gy = gy + wx[u] * wz[v] * (corner[u, 1, v] - corner[u, 0, v])
            gz = gz + wx[u] * wy[v] * (corner[u, v, 1] - corner[u, v, 0])
    return jnp.concatenate([amplitude * gx, amplitude * gy, amplitude * gz], 0)


def blur_sheet(sheet):
    rows, columns = sheet.shape
    sheet = middle_tap * sheet + side_tap * (pltpu.roll(sheet, 1, 0) + pltpu.roll(sheet, rows - 1, 0))
    return middle_tap * sheet + side_tap * (
        pltpu.roll(sheet, 1, 1) + pltpu.roll(sheet, columns - 1, 1)
    )


def blur_along(sheets):
    return [
        middle_tap * sheets[i] + side_tap * (sheets[i - 1] + sheets[i + 1])
        for i in range(1, len(sheets) - 1)
    ]


def make_table(
    place_ref, devices, planes, rows, columns, own_ref, below_ref, above_ref, map_ref, map_below_ref,
    map_above_ref, table_ref,
):
    not_first = jnp.where(place_ref[0] == 0, 0.0, 1.0)
    not_last = jnp.where(place_ref[0] == devices - 1, 0.0, 1.0)
    own = [own_ref[p * rows : (p + 1) * rows, :] for p in range(planes + 1)]
    below = [below_ref[p * rows : (p + 1) * rows, :] for p in range(3)]
    above = [above_ref[p * rows : (p + 1) * rows, :] for p in range(3)]
    own[0] = own[0] + below[2]
    own[planes] = own[planes] * not_last + above[0]
    density = blur_along(below[:2] + own + above[1:])
    observed = (
        [map_below_ref[0]] + [map_ref[p] for p in range(planes)] + [map_above_ref[0], map_above_ref[1]]
    )
    misfit = [blur_sheet(sheet) - seen for sheet, seen in zip(density, observed)]
    misfit[0] = misfit[0] * not_first
    misfit[planes + 1] = misfit[planes + 1] * not_last
    misfit[planes + 2] = misfit[planes + 2] * not_last
    pulled = [blur_sheet(sheet) for sheet in blur_along(misfit)]
    pulled[planes] = pulled[planes] * not_last
    for p in range(planes + 1):
        shifted = pltpu.roll(pulled[p], columns - 1, 1)
        for turn, sheet in enumerate((pulled[p], shifted)):
            high, low = halves(sheet)
            at = slice((turn * (planes + 1) + p) * rows, (turn * (planes + 1) + p + 1) * rows)
            table_ref[at, :columns] = high
            table_ref[at, columns:] = low


def load_tiles(ref, first, count):
    return jnp.concatenate(
        [
            ref[pl.ds(pl.multiple_of((first + i) * fields, fields), fields), :]
            for i in range(count)
        ],
        1,
    )


def store_tiles(ref, first, count, value):
    for i in range(count):
        ref[pl.ds(pl.multiple_of((first + i) * fields, fields), fields), :] = value[
            :, i * lanes : (i + 1) * lanes
        ]


def share_out(total_ref, planes, rows, own_ref, up_ref, down_ref):
    own_ref[...] = total_ref[...]
    up_ref[...] = total_ref[(planes - 2) * rows :, :]
    down_ref[...] = total_ref[: 3 * rows, :]


def density_kernel(planes, rows, columns, batch, message_ref, own_ref, up_ref, down_ref):
    tiles = message_ref.shape[0] // fields
    own_ref[...] = jnp.zeros_like(own_ref)

    def step(i, carry):
        state = load_tiles(message_ref, i * batch, batch)
        own_ref[...] += density_part(state, planes, rows, columns)
        return carry

    lax.fori_loop(0, tiles // batch, step, 0)
    up_ref[...] = own_ref[(planes - 2) * rows :, :]
    down_ref[...] = own_ref[: 3 * rows, :]


def middle_kernel(
    devices, planes, rows, columns, batch, place_ref, message_ref, was_ref, below_ref, above_ref,
    map_ref, map_below_ref, map_above_ref, moved_ref, first_ref, own_ref, up_ref, down_ref, table_ref,
):
    tiles = message_ref.shape[0] // fields
    make_table(
        place_ref, devices, planes, rows, columns, was_ref, below_ref, above_ref, map_ref,
        map_below_ref, map_above_ref, table_ref,
    )
    own_ref[...] = jnp.zeros_like(own_ref)

    def step(i, carry):
        state = load_tiles(message_ref, i * batch, batch)
        gradient = gradient_part(state, table_ref, planes, rows, columns)
        moved = jnp.concatenate(
            [state[0:2], state[2:5] - probe_step * jnp.tanh(gradient), state[5:8]], 0
        )
        store_tiles(moved_ref, i * batch, batch, moved)
        store_tiles(
            first_ref, i * batch, batch,
            jnp.concatenate([gradient, jnp.zeros((5, gradient.shape[1]), f32)], 0),
        )
        own_ref[...] += density_part(moved, planes, rows, columns)
        return carry

    lax.fori_loop(0, tiles // batch, step, 0)
    up_ref[...] = own_ref[(planes - 2) * rows :, :]
    down_ref[...] = own_ref[: 3 * rows, :]


def cross_list(left, right):
    return [
        left[1] * right[2] - left[2] * right[1],
        left[2] * right[0] - left[0] * right[2],
        left[0] * right[1] - left[1] * right[0],
    ]


def last_kernel(
    devices, sub, planes, rows, columns, batch, place_ref, message_ref, moved_ref, first_ref, was_ref,
    below_ref, above_ref, map_ref, map_below_ref, map_above_ref, reply_ref, table_ref, sums_ref,
):
    tiles = message_ref.shape[0] // fields
    make_table(
        place_ref, devices, planes, rows, columns, was_ref, below_ref, above_ref, map_ref,
        map_below_ref, map_above_ref, table_ref,
    )
    sums_ref[...] = jnp.zeros_like(sums_ref)
    last_of = jnp.concatenate(
        [
            message_ref[d * sub * fields + fields - 1 : d * sub * fields + fields, :]
            for d in range(devices)
        ],
        0,
    )
    width = batch * lanes
    last_of = jnp.concatenate([last_of] * batch, 1)
    receiver = down_rows(devices, width)
    slab_plane = (place_ref[0] * planes).astype(f32)

    def step(i, carry):
        state = load_tiles(message_ref, i * batch, batch)
        moved = load_tiles(moved_ref, i * batch, batch)
        first = load_tiles(first_ref, i * batch, batch)[0:3]
        second = gradient_part(moved, table_ref, planes, rows, columns)
        plane, row, _, column, _ = neighbours_of(state, rows, columns)
        base = (plane + slab_plane, row, column)
        pieces = []
        for gradient, offset in ((first, state), (second, moved)):
            g = [gradient[d : d + 1] for d in range(3)]
            pieces += g + cross_list([base[d] + offset[2 + d : 3 + d] for d in range(3)], g)
        pieces.append(jnp.where(state[5:6] > 0.0, 1.0, 0.0))
        pieces.append(jnp.zeros((3, width), f32))
        block = jnp.concatenate(pieces, 0)
        source = jnp.concatenate(
            [
                jnp.full((devices, lanes), (i * batch + t) // sub, jnp.int32)
                for t in range(batch)
            ],
            1,
        )
        chosen = jnp.where((source > receiver) & (last_of == state[6:7]), 1.0, 0.0).astype(bf16)
        part = sum(dot_nt(chosen, piece) for piece in thirds(block))
        sums_ref[:, : part.shape[1]] += part
        store_tiles(
            reply_ref, i * batch, batch,
            jnp.concatenate([first, second, jnp.zeros((2, width), f32)], 0),
        )
        return carry

    lax.fori_loop(0, tiles // batch, step, 0)
    for d in range(devices):
        reply_ref[d * sub * fields + fields - 1 : d * sub * fields + fields, :] = sums_ref[
            d : d + 1, :
        ]


def chain_kernel(
    devices, sub, planes, columns, reply_ref, slot_ref, owner_ref, plane_ref, row_ref, column_ref,
    chain_ref, chain_rows_ref, frac_ref, axis_ref, torque_ref, gradient_ref,
):
    atoms = owner_ref.shape[1]
    blocks = atoms // lanes
    tiles = devices * sub
    high, low = halves(reply_ref[...])
    left = jnp.concatenate([high, low], 1)
    width = 512
    found = []
    for c in range(atoms // width):
        at = slice(c * width, (c + 1) * width)
        spot = jnp.where(down_rows(lanes, width) == slot_ref[1:2, at], 1.0, 0.0).astype(bf16)
        picked = dot_nn(left, jnp.concatenate([spot, spot], 0))
        which = jnp.broadcast_to(slot_ref[0:1, at], (fields, width))
        total = jnp.zeros((fields, width), f32)
        for t in range(tiles):
            total = jnp.where(which == t, picked[t * fields : (t + 1) * fields], total)
        found.append(total)
    gradients = jnp.concatenate(found, 1)[0:6]
    gradient_ref[...] = gradients
    fraction = frac_ref[...]
    moved = fraction - probe_step * jnp.tanh(gradients[0:3])
    base = (
        (owner_ref[...] * planes + plane_ref[...]).astype(f32),
        row_ref[...].astype(f32),
        column_ref[...].astype(f32),
    )
    positions = [[base[d] + offset[d : d + 1] for d in range(3)] for offset in (fraction, moved)]
    pieces = []
    for e in range(2):
        g = [gradients[3 * e + d : 3 * e + d + 1] for d in range(3)]
        pieces += g + cross_list(positions[e], g)
    pieces.append(jnp.ones((1, atoms), f32))
    pieces.append(jnp.zeros((3, atoms), f32))
    stacked = jnp.concatenate(thirds(jnp.concatenate(pieces, 0)), 0)

    def joined(x):
        return x[0:16] + x[16:32] + x[32:48]

    chain = chain_ref[...].astype(f32)
    chain_rows = chain_rows_ref[...].astype(f32)
    ends = jnp.broadcast_to(chain_rows[:, lanes - 1 :], (blocks, atoms))
    later = lax.broadcasted_iota(jnp.int32, (blocks, atoms), 1) >= lanes * (
        down_rows(blocks, atoms) + 1
    )
    bridge = jnp.where(later & (ends == chain), 1.0, 0.0).astype(bf16)
    carries = joined(dot_nt(stacked, bridge))
    arrived = jnp.zeros((1, lanes), f32)
    for d in range(devices):
        arrived = arrived + reply_ref[d * sub * fields + fields - 1 : d * sub * fields + fields, :]
    diagonal = down_rows(16, lanes) == lax.broadcasted_iota(jnp.int32, (16, lanes), 1)
    arrived = jnp.sum(jnp.where(diagonal, arrived, 0.0), 1, keepdims=True)
    padded = jnp.concatenate([chain_rows, jnp.zeros((lanes - blocks, lanes), f32)], 0)
    down_chain = jnp.transpose(padded)
    not_before = down_rows(lanes, lanes) >= lax.broadcasted_iota(jnp.int32, (lanes, lanes), 1)
    closing = chain[:, atoms - 1 :]
    sums = []
    for j in range(blocks):
        at = slice(j * lanes, (j + 1) * lanes)
        mask = not_before & (down_chain[:, j : j + 1] == chain[:, at])
        local = joined(dot_nn(stacked[:, at], jnp.where(mask, 1.0, 0.0).astype(bf16)))
        end = chain[:, (j + 1) * lanes - 1 : (j + 1) * lanes]
        carry = carries[:, j : j + 1] + jnp.where(end == closing, arrived, 0.0)
        sums.append(local + jnp.where(chain[:, at] == end, carry, 0.0))
    totals = jnp.concatenate(sums, 1)
    scale = 1.0 / (columns * jnp.sqrt(totals[12:13]))
    torques = []
    for e in range(2):
        force = [totals[6 * e + d : 6 * e + d + 1] for d in range(3)]
        lever = cross_list(positions[e], force)
        turn = 0.0
        for d in range(3):
            turn = turn + axis_ref[d : d + 1] * (totals[6 * e + 3 + d : 6 * e + 4 + d] - lever[d])
        torques.append(turn * scale)
    torque_ref[...] = jnp.concatenate(torques, 0)


def whole(count):
    return [pl.BlockSpec(memory_space=pltpu.VMEM)] * count


def settings():
    return pltpu.CompilerParams(vmem_limit_bytes=room)


def shape_of(*dims, dtype=f32):
    return jax.ShapeDtypeStruct(dims, dtype)


def shift(value, by):
    count = lax.axis_size("bx")
    return lax.ppermute(value, "bx", [(i, i + by) for i in range(count) if 0 <= i + by < count])


def exchange(value):
    return lax.all_to_all(value, "bx", split_axis=0, concat_axis=0, tiled=True)


def shards(
    density_map,
    amplitude,
    fraction,
    torsion_axis,
    brick_owner,
    plane_offset,
    row_offset,
    column_offset,
    chain_index,
):
    planes, rows, columns = density_map.shape
    atoms = amplitude.shape[0]
    devices = lax.axis_size("bx")
    capacity = 3 * atoms // devices
    sub = -(-capacity // lanes)
    tiles = devices * sub
    batch = 4
    grid = (planes, rows, columns)
    place = lax.axis_index("bx").astype(jnp.int32).reshape(1)
    scalar = [pl.BlockSpec(memory_space=pltpu.SMEM)]

    map_below = shift(density_map[planes - 1 :], 1)
    map_above = shift(density_map[:2], -1)

    owner, plane, row, column, chain = (
        item.reshape(1, atoms)
        for item in (brick_owner, plane_offset, row_offset, column_offset, chain_index)
    )
    message, slot = pl.pallas_call(
        functools.partial(pack_kernel, devices, sub, rows),
        out_shape=(shape_of(tiles * fields, lanes), shape_of(2, atoms, dtype=jnp.int32)),
        in_specs=whole(7),
        out_specs=whole(2),
        compiler_params=settings(),
        name="pack",
    )(owner, plane, row, column, chain, amplitude.reshape(1, atoms), fraction)
    message = exchange(message)

    own_shape = shape_of((planes + 1) * rows, columns)
    edge_shape = shape_of(3 * rows, columns)
    own, up, down = pl.pallas_call(
        functools.partial(density_kernel, *grid, batch),
        out_shape=(own_shape, edge_shape, edge_shape),
        in_specs=whole(1),
        out_specs=whole(3),
        compiler_params=settings(),
        name="density",
    )(message)
    below, above = shift(up, 1), shift(down, -1)
    table = pltpu.VMEM((2 * (planes + 1) * rows, 2 * columns), bf16)
    moved, first, own, up, down = pl.pallas_call(
        functools.partial(middle_kernel, devices, *grid, batch),
        out_shape=(
            shape_of(tiles * fields, lanes),
            shape_of(tiles * fields, lanes),
            own_shape,
            edge_shape,
            edge_shape,
        ),
        in_specs=scalar + whole(7),
        out_specs=whole(5),
        scratch_shapes=[table],
        compiler_params=settings(),
        name="middle",
    )(place, message, own, below, above, density_map, map_below, map_above)
    below, above = shift(up, 1), shift(down, -1)
    reply = pl.pallas_call(
        functools.partial(last_kernel, devices, sub, *grid, batch),
        out_shape=shape_of(tiles * fields, lanes),
        in_specs=scalar + whole(9),
        out_specs=whole(1)[0],
        scratch_shapes=[table, pltpu.VMEM((devices, lanes), f32)],
        compiler_params=settings(),
        name="last",
    )(place, message, moved, first, own, below, above, density_map, map_below, map_above)
    reply = exchange(reply)
    torques, gradients = pl.pallas_call(
        functools.partial(chain_kernel, devices, sub, planes, columns),
        out_shape=(shape_of(2, atoms), shape_of(6, atoms)),
        in_specs=whole(10),
        out_specs=whole(2),
        compiler_params=settings(),
        name="chains",
    )(
        reply, slot, owner, plane, row, column, chain, chain_index.reshape(atoms // lanes, lanes),
        fraction, torsion_axis,
    )
    return torques, gradients


def solution(mesh):
    return jax.shard_map(
        shards,
        mesh=mesh,
        in_specs=(
            P(("grp", "bx"), None, None),
            P(("grp", "bx")),
            P(None, ("grp", "bx")),
            P(None, ("grp", "bx")),
            P(("grp", "bx"), None),
            P(("grp", "bx")),
            P(("grp", "bx")),
            P(("grp", "bx")),
            P(("grp", "bx")),
        ),
        out_specs=(P(None, ("grp", "bx")), P(None, ("grp", "bx"))),
        check_vma=False,
    )
```

time: 1610 us -> 97 us (0.06)
  local copies, waits for them, and re-layouts: 660 us -> 4.99 us
  other arithmetic: 620 us -> 0 us
  starting transfers between devices: 120 us -> 13.3 us
  loops' own time: 91.9 us -> 0 us
  waiting for transfers between devices: 44.2 us -> 4.77 us
  Pallas kernels: 0 us -> 37.2 us
  blocking collectives: 51.6 us -> 35.2 us
    scatter-add x4 -> x0, other arithmetic: 581 us -> none  [the longest x2 581 us: evaluate(): jnp.zeros(((planes + 1) * rows * columns,), jnp.float32).at[targets]]
    gather x34 -> x0, local copies, waits for them, and re-layouts: 568 us -> none  [the longest x30 549 us: evaluate(): sampled = flat[target]]
    another operation x1 -> x0, loops' own time: 91.9 us -> none  [prefix(): return lax.fori_loop(0, ahead, one, state)]
    ppermute x12 -> x6, starting transfers between devices: 85.3 us -> 13.3 us  [shift(): lax.ppermute(value, 'bx', [(i, i + by) for i in range(count) if 0 <= i +...]
    slice x131 -> x2, local copies, waits for them, and re-layouts: 42.3 us -> 0.02 us  [the longest x1 0.01 us: shards(): map_above = shift(density_map[:2], -1)]
    pallas_call x0 -> x5, Pallas kernels: none -> 37.2 us  [the longest x1 18 us: shards(): pl.pallas_call(functools.partial(middle_kernel, devices, *grid, batch), o...]
    all_to_all x0 -> x2, blocking collectives: none -> 35.2 us  [exchange(): return lax.all_to_all(value, 'bx', split_axis=0, concat_axis=0, tiled=True)]
    all_to_all x5 -> x0, starting transfers between devices: 34.8 us -> none  [the longest x2 17.8 us: send_back(): return lax.all_to_all(values, 'bx', split_axis=1, concat_axis=1, tiled=True)]
  transfers between devices with their start and end apart: 17 -> 6, of which waited for: 10 -> 2; matrix products, arithmetic and copies ran while one was open for 3% -> 0% of each run, Pallas kernels for 0% -> 0%
where the time goes in v1:
time: 97 us; the launch traced here: 96.3 us
  Pallas kernels  37.2 us (38%)
  blocking collectives  35.2 us (36%)
  starting transfers between devices  13.3 us (14%)
  local copies, waits for them, and re-layouts  4.99 us (5%)
  waiting for transfers between devices  4.77 us (5%)
    all_to_all x2, blocking collectives, exchange(): return lax.all_to_all(value, 'bx', split_axis=0, concat_axis=0, tiled=True)  35.2 us
    pallas_call x1, Pallas kernels, shards(): pl.pallas_call(functools.partial(middle_kernel, devices, *grid, batch), o...  18 us
    ppermute x6, starting transfers between devices, shift(): lax.ppermute(value, 'bx', [(i, i + by) for i in range(count) if 0 <= i +...  13.3 us
    pallas_call x1, Pallas kernels, shards(): pl.pallas_call(functools.partial(last_kernel, devices, sub, *grid, batch)...  10 us
    pallas_call x1, Pallas kernels, shards(): pl.pallas_call(functools.partial(density_kernel, *grid, batch), out_shape...  5.83 us
    unnamed x28, local copies, waits for them, and re-layouts  4.97 us
    ppermute x6, waiting for transfers between devices, shift(): lax.ppermute(value, 'bx', [(i, i + by) for i in range(count) if 0 <= i +...  4.77 us
  transfers between devices with their start and end apart: 6, of which 2 were waited for; matrix products, arithmetic and copies ran while one was open for 0% of the time, Pallas kernels for 0%

profile of v1, /device:TPU:0, one launch (start us, length us, event | category | flops | bytes accessed | tf_op | source)
XLA Modules:
  0.0 96.3 jit_solution(7819455316627020675)
XLA Ops:
  0.6 0.0 copy-start.3
  0.6 0.7 copy-done.3
  1.3 0.0 copy-start.1
  1.3 0.8 copy-done.1
  2.1 0.0 copy-start.5
  2.1 0.7 copy-done.5
  2.8 0.0 copy-start.7
  2.8 0.7 copy-done.7
  3.5 0.0 copy-start.9
  3.5 0.7 copy-done.9
  4.2 0.0 copy-start.11
  4.2 0.7 copy-done.11
  4.9 0.0 copy-start.13
  4.9 0.7 copy-done.13
  5.6 1.6 %pack.1 = (f32[384,128]{1,0:T(8,128)S(1)}, s32[2,2048]{1,0:T(2,128)S(1)}) custom-call(s32[1,2048]{1,0:T(1,128)S(1)} %bitcast.21, s32[1,2048]{1,0:T(1,128)S(1)} %bitcast.23, s32[1,2048]{1,0:T(1,128)S(1)} %bitcast.25, s32[1,2048]{1,0:T(1,128)S(1)} %bitcast.27, s32[1,2048]{1,0:T(1,128)S(1)} %bitcast.18, f32[1,2048]{1,0:T(1,128)S(1)} %bitcast.29, ...), custom_call_target="tpu_custom_call" | custom-call | tf_op jit(solution)/shard_map/pack/pallas_call | solution.py:503
  7.2 0.0 copy-start
  7.2 16.3 %all_to_all.22 = f32[16,24,128]{2,1,0:T(8,128)S(1)} all-to-all(f32[16,24,128]{2,1,0:T(8,128)S(1)} %bitcast.17), channel_id=1, replica_groups=mesh['grp'=2,'bx'=16] {'bx'}, dimensions={0} | all-to-all | bytes 393216 | tf_op jit(solution)/shard_map/all_to_all | solution.py:471
  23.5 5.8 %density.1 = (f32[320,256]{1,0:T(8,128)S(1)}, f32[192,256]{1,0:T(8,128)S(1)}, f32[192,256]{1,0:T(8,128)S(1)}) custom-call(f32[384,128]{1,0:T(8,128)S(1)} %bitcast.12), custom_call_target="tpu_custom_call" | custom-call | tf_op jit(solution)/shard_map/density/pallas_call | solution.py:515
  29.3 1.7 %collective-permute-start = (f32[192,256]{1,0:T(8,128)S(1)}, f32[192,256]{1,0:T(8,128)S(1)}, u32[]{:S(2)}, u32[]{:S(2)}) collective-permute-start(f32[192,256]{1,0:T(8,128)S(1)} %get-tuple-element.14), channel_id=1, source_target_pairs={{0,1},{1,2},{2,3},{3,4},{4,5},{5,6},{6,7},{7,8},{8,9},{9,10},{10,1... | collective-permute-start | bytes 589832 | tf_op jit(solution)/shard_map/ppermute | solution.py:467
  31.0 1.3 %collective-permute-start.1 = (f32[192,256]{1,0:T(8,128)S(1)}, f32[192,256]{1,0:T(8,128)S(1)}, u32[]{:S(2)}, u32[]{:S(2)}) collective-permute-start(f32[192,256]{1,0:T(8,128)S(1)} %get-tuple-element.15), channel_id=1, source_target_pairs={{1,0},{2,1},{3,2},{4,3},{5,4},{6,5},{7,6},{8,7},{9,8},{10,9},{11,1... | collective-permute-start | bytes 589832 | tf_op jit(solution)/shard_map/ppermute | solution.py:467
  32.3 0.0 copy-done
  32.3 1.3 %collective-permute-start.3 = (f32[2,64,256]{2,1,0:T(8,128)S(1)}, f32[2,64,256]{2,1,0:T(8,128)S(1)}, u32[]{:S(2)}, u32[]{:S(2)}) collective-permute-start(f32[2,64,256]{2,1,0:T(8,128)S(1)} %slice.7), channel_id=1, source_target_pairs={{1,0},{2,1},{3,2},{4,3},{5,4},{6,5},{7,6},{8,7},{9,8},{10,9},{11,1... | collective-permute-start | bytes 393224 | tf_op jit(solution)/shard_map/ppermute | solution.py:467
  33.6 3.7 %collective-permute-start.2 = (f32[1,64,256]{2,1,0:T(8,128)S(1)}, f32[1,64,256]{2,1,0:T(8,128)S(1)}, u32[]{:S(2)}, u32[]{:S(2)}) collective-permute-start(f32[1,64,256]{2,1,0:T(8,128)S(1)} %slice.6), channel_id=1, source_target_pairs={{0,1},{1,2},{2,3},{3,4},{4,5},{5,6},{6,7},{7,8},{8,9},{9,10},{10,1... | collective-permute-start | bytes 196616 | tf_op jit(solution)/shard_map/ppermute | solution.py:467
  37.3 0.9 collective-permute-done.2.map_below_ref
  38.2 0.0 collective-permute-done.3.map_above_ref
  38.2 0.0 collective-permute-done.below_ref
  38.2 0.0 collective-permute-done.1.above_ref
  38.2 18.0 %middle.1 = (f32[384,128]{1,0:T(8,128)S(1)}, f32[384,128]{1,0:T(8,128)S(1)}, f32[320,256]{1,0:T(8,128)S(1)}, f32[192,256]{1,0:T(8,128)S(1)}, f32[192,256]{1,0:T(8,128)S(1)}) custom-call(s32[1]{0:T(128)} %bitcast.place_ref, f32[384,128]{1,0:T(8,128)S(1)} %bitcast.13, f32[320,256]{1,0:T(8,128)S(1)} %get-tuple-element.13.was_ref, ...), custom_call_target="tpu_custom_call" | custom-call | tf_op jit(solution)/shard_map/middle/pallas_call | solution.py:525
  56.2 4.1 %collective-permute-start.4 = (f32[192,256]{1,0:T(8,128)S(1)}, f32[192,256]{1,0:T(8,128)S(1)}, u32[]{:S(2)}, u32[]{:S(2)}) collective-permute-start(f32[192,256]{1,0:T(8,128)S(1)} %get-tuple-element.19), channel_id=1, source_target_pairs={{0,1},{1,2},{2,3},{3,4},{4,5},{5,6},{6,7},{7,8},{8,9},{9,10},{10,1... | collective-permute-start | bytes 589832 | tf_op jit(solution)/shard_map/ppermute | solution.py:467
  60.2 1.3 %collective-permute-start.5 = (f32[192,256]{1,0:T(8,128)S(1)}, f32[192,256]{1,0:T(8,128)S(1)}, u32[]{:S(2)}, u32[]{:S(2)}) collective-permute-start(f32[192,256]{1,0:T(8,128)S(1)} %get-tuple-element.20), channel_id=1, source_target_pairs={{1,0},{2,1},{3,2},{4,3},{5,4},{6,5},{7,6},{8,7},{9,8},{10,9},{11,1... | collective-permute-start | bytes 589832 | tf_op jit(solution)/shard_map/ppermute | solution.py:467
  61.5 0.0 collective-permute-done.4.below_ref
  61.6 3.9 %collective-permute-done.5.above_ref = f32[192,256]{1,0:T(8,128)S(1)} collective-permute-done((f32[192,256]{1,0:T(8,128)S(1)}, f32[192,256]{1,0:T(8,128)S(1)}, u32[]{:S(2)}, u32[]{:S(2)}) %collective-permute-start.5) | collective-permute-done | bytes 196640 | tf_op jit(solution)/shard_map/ppermute | solution.py:467
  65.4 10.0 %last.1 = f32[384,128]{1,0:T(8,128)S(1)} custom-call(s32[1]{0:T(128)} %bitcast.place_ref, f32[384,128]{1,0:T(8,128)S(1)} %bitcast.14, f32[384,128]{1,0:T(8,128)S(1)} %get-tuple-element.16.moved_ref, f32[384,128]{1,0:T(8,128)S(1)} %get-tuple-element.17.first_ref, f32[320,256]{1,0:T(8,128)S(1)} %get-tuple-element.18.was_ref, ...), custom_call_target="tpu_custom_call" | custom-call | tf_op jit(solution)/shard_map/last/pallas_call | solution.py:541
  75.5 0.0 copy-start.2
  75.5 0.0 copy-start.4
  75.5 0.0 copy-start.6
  75.5 0.0 copy-start.8
  75.5 0.0 copy-start.10
  75.5 0.0 copy-start.12
  75.6 18.9 %all_to_all.23 = f32[16,24,128]{2,1,0:T(8,128)S(1)} all-to-all(f32[16,24,128]{2,1,0:T(8,128)S(1)} %bitcast.15), channel_id=1, replica_groups=mesh['grp'=2,'bx'=16] {'bx'}, dimensions={0} | all-to-all | bytes 393216 | tf_op jit(solution)/shard_map/all_to_all | solution.py:471
  94.5 0.0 copy-done.2
  94.5 0.0 copy-done.4
  94.5 0.0 copy-done.6
  94.5 0.0 copy-done.8
  94.5 0.0 copy-done.10
  94.5 0.0 copy-done.12
  94.5 1.7 %chains.1 = (f32[2,2048]{1,0:T(2,128)}, f32[6,2048]{1,0:T(8,128)}) custom-call(f32[384,128]{1,0:T(8,128)S(1)} %bitcast.16, s32[2,2048]{1,0:T(2,128)S(1)} %get-tuple-element.21.slot_ref, s32[1,2048]{1,0:T(1,128)S(1)} %bitcast.22, s32[1,2048]{1,0:T(1,128)S(1)} %bitcast.24, s32[1,2048]{1,0:T(1,128)S(1)} %bitcast.26, s32[1,2048]{1,0:T(1,128)S(1)} %bitcast.28, ...), custom_call_target="tpu_custom_call" | custom-call | tf_op jit(solution)/shard_map/chains/pallas_call | solution.py:551
  (2 shorter events, 0.0 us)
Async XLA Ops:
  0.6 0.7 copy-start.3
  1.3 0.8 copy-start.1
  2.1 0.7 copy-start.5
  2.8 0.7 copy-start.7
  3.5 0.7 copy-start.9
  4.2 0.7 copy-start.11
  4.9 0.7 copy-start.13
  7.2 25.1 %copy-start = (f32[4,64,256]{2,1,0:T(8,128)S(1)}, f32[4,64,256]{2,1,0:T(8,128)}, u32[]{:S(2)}) copy-start(f32[4,64,256]{2,1,0:T(8,128)} %map_ref.3) | copy-start | bytes 786436
  29.3 8.9 %collective-permute-start = (f32[192,256]{1,0:T(8,128)S(1)}, f32[192,256]{1,0:T(8,128)S(1)}, u32[]{:S(2)}, u32[]{:S(2)}) collective-permute-start(f32[192,256]{1,0:T(8,128)S(1)} %get-tuple-element.14), channel_id=1, source_target_pairs={{0,1},{1,2},{2,3},{3,4},{4,5},{5,6},{6,7},{7,8},{8,9},{9,10},{10,1... | collective-permute-start | bytes 589832 | tf_op jit(solution)/shard_map/ppermute | solution.py:467
  31.0 7.2 %collective-permute-start.1 = (f32[192,256]{1,0:T(8,128)S(1)}, f32[192,256]{1,0:T(8,128)S(1)}, u32[]{:S(2)}, u32[]{:S(2)}) collective-permute-start(f32[192,256]{1,0:T(8,128)S(1)} %get-tuple-element.15), channel_id=1, source_target_pairs={{1,0},{2,1},{3,2},{4,3},{5,4},{6,5},{7,6},{8,7},{9,8},{10,9},{11,1... | collective-permute-start | bytes 589832 | tf_op jit(solution)/shard_map/ppermute | solution.py:467
  32.3 5.9 %collective-permute-start.3 = (f32[2,64,256]{2,1,0:T(8,128)S(1)}, f32[2,64,256]{2,1,0:T(8,128)S(1)}, u32[]{:S(2)}, u32[]{:S(2)}) collective-permute-start(f32[2,64,256]{2,1,0:T(8,128)S(1)} %slice.7), channel_id=1, source_target_pairs={{1,0},{2,1},{3,2},{4,3},{5,4},{6,5},{7,6},{8,7},{9,8},{10,9},{11,1... | collective-permute-start | bytes 393224 | tf_op jit(solution)/shard_map/ppermute | solution.py:467
  33.6 4.6 %collective-permute-start.2 = (f32[1,64,256]{2,1,0:T(8,128)S(1)}, f32[1,64,256]{2,1,0:T(8,128)S(1)}, u32[]{:S(2)}, u32[]{:S(2)}) collective-permute-start(f32[1,64,256]{2,1,0:T(8,128)S(1)} %slice.6), channel_id=1, source_target_pairs={{0,1},{1,2},{2,3},{3,4},{4,5},{5,6},{6,7},{7,8},{8,9},{9,10},{10,1... | collective-permute-start | bytes 196616 | tf_op jit(solution)/shard_map/ppermute | solution.py:467
  56.2 5.4 %collective-permute-start.4 = (f32[192,256]{1,0:T(8,128)S(1)}, f32[192,256]{1,0:T(8,128)S(1)}, u32[]{:S(2)}, u32[]{:S(2)}) collective-permute-start(f32[192,256]{1,0:T(8,128)S(1)} %get-tuple-element.19), channel_id=1, source_target_pairs={{0,1},{1,2},{2,3},{3,4},{4,5},{5,6},{6,7},{7,8},{8,9},{9,10},{10,1... | collective-permute-start | bytes 589832 | tf_op jit(solution)/shard_map/ppermute | solution.py:467
  60.2 5.2 %collective-permute-start.5 = (f32[192,256]{1,0:T(8,128)S(1)}, f32[192,256]{1,0:T(8,128)S(1)}, u32[]{:S(2)}, u32[]{:S(2)}) collective-permute-start(f32[192,256]{1,0:T(8,128)S(1)} %get-tuple-element.20), channel_id=1, source_target_pairs={{1,0},{2,1},{3,2},{4,3},{5,4},{6,5},{7,6},{8,7},{9,8},{10,9},{11,1... | collective-permute-start | bytes 589832 | tf_op jit(solution)/shard_map/ppermute | solution.py:467
  75.5 19.0 %copy-start.2 = (f32[3,2048]{1,0:T(4,128)S(1)}, f32[3,2048]{1,0:T(4,128)}, u32[]{:S(2)}) copy-start(f32[3,2048]{1,0:T(4,128)} %frac_ref.3) | copy-start | bytes 73732
  75.5 19.0 %copy-start.4 = (f32[3,2048]{1,0:T(4,128)S(1)}, f32[3,2048]{1,0:T(4,128)}, u32[]{:S(2)}) copy-start(f32[3,2048]{1,0:T(4,128)} %axis_ref.1) | copy-start | bytes 73732
  75.5 19.0 %copy-start.6 = (s32[2048,1]{0,1:T(1,128)S(1)}, s32[2048,1]{0,1:T(1,128)}, u32[]{:S(2)}) copy-start(s32[2048,1]{0,1:T(1,128)} %param.13) | copy-start | bytes 24580
  75.5 19.0 %copy-start.8 = (s32[2048]{0:T(1024)S(1)}, s32[2048]{0:T(1024)}, u32[]{:S(2)}) copy-start(s32[2048]{0:T(1024)} %param.14) | copy-start | bytes 24580
  75.5 19.0 %copy-start.10 = (s32[2048]{0:T(1024)S(1)}, s32[2048]{0:T(1024)}, u32[]{:S(2)}) copy-start(s32[2048]{0:T(1024)} %param.15) | copy-start | bytes 24580
  75.5 19.0 %copy-start.12 = (s32[2048]{0:T(1024)S(1)}, s32[2048]{0:T(1024)}, u32[]{:S(2)}) copy-start(s32[2048]{0:T(1024)} %param.16) | copy-start | bytes 24580

commit v2 on v1

--- a/solution.py
+++ b/solution.py
@@ -207,22 +207,33 @@
     ]
 
 
-def make_table(
-    place_ref, devices, planes, rows, columns, own_ref, below_ref, above_ref, map_ref, map_below_ref,
-    map_above_ref, table_ref,
-):
+def edges(place_ref, devices):
     not_first = jnp.where(place_ref[0] == 0, 0.0, 1.0)
     not_last = jnp.where(place_ref[0] == devices - 1, 0.0, 1.0)
-    own = [own_ref[p * rows : (p + 1) * rows, :] for p in range(planes + 1)]
-    below = [below_ref[p * rows : (p + 1) * rows, :] for p in range(3)]
-    above = [above_ref[p * rows : (p + 1) * rows, :] for p in range(3)]
-    own[0] = own[0] + below[2]
-    own[planes] = own[planes] * not_last + above[0]
-    density = blur_along(below[:2] + own + above[1:])
-    observed = (
-        [map_below_ref[0]] + [map_ref[p] for p in range(planes)] + [map_above_ref[0], map_above_ref[1]]
-    )
-    misfit = [blur_sheet(sheet) - seen for sheet, seen in zip(density, observed)]
+    return not_first, not_last
+
+
+def share_misfit(place_ref, devices, planes, rows, total, map_ref, own_ref, up_ref, down_ref):
+    _, not_last = edges(place_ref, devices)
+    density = [total[p * rows : (p + 1) * rows] for p in range(planes + 1)]
+    density[planes] = density[planes] * not_last
+    zero = jnp.zeros_like(density[0])
+    parts = [blur_sheet(sheet) for sheet in blur_along([zero, zero] + density + [zero, zero])]
+    for p in range(planes):
+        parts[p + 1] = parts[p + 1] - map_ref[p]
+    for p in range(planes + 3):
+        own_ref[p * rows : (p + 1) * rows, :] = parts[p]
+    for p in range(3):
+        up_ref[p * rows : (p + 1) * rows, :] = parts[planes + p]
+        down_ref[p * rows : (p + 1) * rows, :] = parts[p]
+
+
+def make_table(place_ref, devices, planes, rows, columns, own_ref, below_ref, above_ref, table_ref):
+    not_first, not_last = edges(place_ref, devices)
+    misfit = [own_ref[p * rows : (p + 1) * rows, :] for p in range(planes + 3)]
+    for p in range(3):
+        misfit[p] = misfit[p] + below_ref[p * rows : (p + 1) * rows, :]
+        misfit[planes + p] = misfit[planes + p] + above_ref[p * rows : (p + 1) * rows, :]
     misfit[0] = misfit[0] * not_first
     misfit[planes + 1] = misfit[planes + 1] * not_last
     misfit[planes + 2] = misfit[planes + 2] * not_last
@@ -240,8 +251,7 @@
 def load_tiles(ref, first, count):
     return jnp.concatenate(
         [
-            ref[pl.ds(pl.multiple_of((first + i) * fields, fields), fields), :]
-            for i in range(count)
+            ref[(first + i) * fields : (first + i + 1) * fields, :] for i in range(count)
         ],
         1,
     )
@@ -249,43 +259,36 @@
 
 def store_tiles(ref, first, count, value):
     for i in range(count):
-        ref[pl.ds(pl.multiple_of((first + i) * fields, fields), fields), :] = value[
+        ref[(first + i) * fields : (first + i + 1) * fields, :] = value[
             :, i * lanes : (i + 1) * lanes
         ]
 
 
-def share_out(total_ref, planes, rows, own_ref, up_ref, down_ref):
-    own_ref[...] = total_ref[...]
-    up_ref[...] = total_ref[(planes - 2) * rows :, :]
-    down_ref[...] = total_ref[: 3 * rows, :]
-
-
-def density_kernel(planes, rows, columns, batch, message_ref, own_ref, up_ref, down_ref):
-    tiles = message_ref.shape[0] // fields
-    own_ref[...] = jnp.zeros_like(own_ref)
-
-    def step(i, carry):
-        state = load_tiles(message_ref, i * batch, batch)
-        own_ref[...] += density_part(state, planes, rows, columns)
-        return carry
-
-    lax.fori_loop(0, tiles // batch, step, 0)
-    up_ref[...] = own_ref[(planes - 2) * rows :, :]
-    down_ref[...] = own_ref[: 3 * rows, :]
+def all_density(state_ref, planes, rows, columns, batch):
+    tiles = state_ref.shape[0] // fields
+    total = None
+    for i in range(tiles // batch):
+        part = density_part(load_tiles(state_ref, i * batch, batch), planes, rows, columns)
+        total = part if total is None else total + part
+    return total
+
+
+def density_kernel(
+    devices, planes, rows, columns, batch, place_ref, message_ref, map_ref, own_ref, up_ref, down_ref
+):
+    total = all_density(message_ref, planes, rows, columns, batch)
+    share_misfit(place_ref, devices, planes, rows, total, map_ref, own_ref, up_ref, down_ref)
 
 
 def middle_kernel(
     devices, planes, rows, columns, batch, place_ref, message_ref, was_ref, below_ref, above_ref,
-    map_ref, map_below_ref, map_above_ref, moved_ref, first_ref, own_ref, up_ref, down_ref, table_ref,
+    map_ref, moved_ref, first_ref, own_ref, up_ref, down_ref, table_ref,
 ):
     tiles = message_ref.shape[0] // fields
     make_table(
-        place_ref, devices, planes, rows, columns, was_ref, below_ref, above_ref, map_ref,
-        map_below_ref, map_above_ref, table_ref,
-    )
-    own_ref[...] = jnp.zeros_like(own_ref)
-
-    def step(i, carry):
+        place_ref, devices, planes, rows, columns, was_ref, below_ref, above_ref, table_ref
+    )
+    for i in range(tiles // batch):
         state = load_tiles(message_ref, i * batch, batch)
         gradient = gradient_part(state, table_ref, planes, rows, columns)
         moved = jnp.concatenate(
@@ -296,12 +299,8 @@
             first_ref, i * batch, batch,
             jnp.concatenate([gradient, jnp.zeros((5, gradient.shape[1]), f32)], 0),
         )
-        own_ref[...] += density_part(moved, planes, rows, columns)
-        return carry
-
-    lax.fori_loop(0, tiles // batch, step, 0)
-    up_ref[...] = own_ref[(planes - 2) * rows :, :]
-    down_ref[...] = own_ref[: 3 * rows, :]
+    total = all_density(moved_ref, planes, rows, columns, batch)
+    share_misfit(place_ref, devices, planes, rows, total, map_ref, own_ref, up_ref, down_ref)
 
 
 def cross_list(left, right):
@@ -314,12 +313,11 @@
 
 def last_kernel(
     devices, sub, planes, rows, columns, batch, place_ref, message_ref, moved_ref, first_ref, was_ref,
-    below_ref, above_ref, map_ref, map_below_ref, map_above_ref, reply_ref, table_ref, sums_ref,
+    below_ref, above_ref, reply_ref, table_ref, sums_ref,
 ):
     tiles = message_ref.shape[0] // fields
     make_table(
-        place_ref, devices, planes, rows, columns, was_ref, below_ref, above_ref, map_ref,
-        map_below_ref, map_above_ref, table_ref,
+        place_ref, devices, planes, rows, columns, was_ref, below_ref, above_ref, table_ref
     )
     sums_ref[...] = jnp.zeros_like(sums_ref)
     last_of = jnp.concatenate(
@@ -334,7 +332,7 @@
     receiver = down_rows(devices, width)
     slab_plane = (place_ref[0] * planes).astype(f32)
 
-    def step(i, carry):
+    for i in range(tiles // batch):
         state = load_tiles(message_ref, i * batch, batch)
         moved = load_tiles(moved_ref, i * batch, batch)
         first = load_tiles(first_ref, i * batch, batch)[0:3]
@@ -362,9 +360,6 @@
             reply_ref, i * batch, batch,
             jnp.concatenate([first, second, jnp.zeros((2, width), f32)], 0),
         )
-        return carry
-
-    lax.fori_loop(0, tiles // batch, step, 0)
     for d in range(devices):
         reply_ref[d * sub * fields + fields - 1 : d * sub * fields + fields, :] = sums_ref[
             d : d + 1, :
@@ -488,13 +483,10 @@
     capacity = 3 * atoms // devices
     sub = -(-capacity // lanes)
     tiles = devices * sub
-    batch = 4
+    batch = max(b for b in range(1, 25) if tiles % b == 0)
     grid = (planes, rows, columns)
     place = lax.axis_index("bx").astype(jnp.int32).reshape(1)
     scalar = [pl.BlockSpec(memory_space=pltpu.SMEM)]
-
-    map_below = shift(density_map[planes - 1 :], 1)
-    map_above = shift(density_map[:2], -1)
 
     owner, plane, row, column, chain = (
         item.reshape(1, atoms)
@@ -510,16 +502,16 @@
     )(owner, plane, row, column, chain, amplitude.reshape(1, atoms), fraction)
     message = exchange(message)
 
-    own_shape = shape_of((planes + 1) * rows, columns)
+    own_shape = shape_of((planes + 3) * rows, columns)
     edge_shape = shape_of(3 * rows, columns)
     own, up, down = pl.pallas_call(
-        functools.partial(density_kernel, *grid, batch),
+        functools.partial(density_kernel, devices, *grid, batch),
         out_shape=(own_shape, edge_shape, edge_shape),
-        in_specs=whole(1),
+        in_specs=scalar + whole(2),
         out_specs=whole(3),
         compiler_params=settings(),
         name="density",
-    )(message)
+    )(place, message, density_map)
     below, above = shift(up, 1), shift(down, -1)
     table = pltpu.VMEM((2 * (planes + 1) * rows, 2 * columns), bf16)
     moved, first, own, up, down = pl.pallas_call(
@@ -531,22 +523,22 @@
             edge_shape,
             edge_shape,
         ),
-        in_specs=scalar + whole(7),
+        in_specs=scalar + whole(5),
         out_specs=whole(5),
         scratch_shapes=[table],
         compiler_params=settings(),
         name="middle",
-    )(place, message, own, below, above, density_map, map_below, map_above)
+    )(place, message, own, below, above, density_map)
     below, above = shift(up, 1), shift(down, -1)
     reply = pl.pallas_call(
         functools.partial(last_kernel, devices, sub, *grid, batch),
         out_shape=shape_of(tiles * fields, lanes),
-        in_specs=scalar + whole(9),
+        in_specs=scalar + whole(6),
         out_specs=whole(1)[0],
         scratch_shapes=[table, pltpu.VMEM((devices, lanes), f32)],
         compiler_params=settings(),
         name="last",
-    )(place, message, moved, first, own, below, above, density_map, map_below, map_above)
+    )(place, message, moved, first, own, below, above)
     reply = exchange(reply)
     torques, gradients = pl.pallas_call(
         functools.partial(chain_kernel, devices, sub, planes, columns),

time: 97 us -> 79.6 us (0.82)
  blocking collectives: 35.2 us -> 18 us
  Pallas kernels: 37.2 us -> 24.8 us
  waiting for transfers between devices: 4.77 us -> 12.6 us
  starting transfers between devices: 13.3 us -> 17.6 us
    all_to_all x2 -> x1, blocking collectives: 35.2 us -> 18 us  [exchange(): return lax.all_to_all(value, 'bx', split_axis=0, concat_axis=0, tiled=True)]
    all_to_all x0 -> x1, waiting for transfers between devices: none -> 8.99 us  [exchange(): return lax.all_to_all(value, 'bx', split_axis=0, concat_axis=0, tiled=True)]
    all_to_all x0 -> x1, starting transfers between devices: none -> 7.36 us  [exchange(): return lax.all_to_all(value, 'bx', split_axis=0, concat_axis=0, tiled=True)]
    pallas_call x1, Pallas kernels: 18 us -> 10.9 us  [shards(): pl.pallas_call(functools.partial(middle_kernel, devices, *grid, batch), o...]
    pallas_call x1, Pallas kernels: 10 us -> 6.01 us  [shards(): pl.pallas_call(functools.partial(last_kernel, devices, sub, *grid, batch)...]
    ppermute x6 -> x4, starting transfers between devices: 13.3 us -> 10.2 us  [shift(): lax.ppermute(value, 'bx', [(i, i + by) for i in range(count) if 0 <= i +...]
    pallas_call x1, Pallas kernels: 5.83 us -> 3.93 us  [shards(): pl.pallas_call(functools.partial(density_kernel, devices, *grid, batch),...]
    ppermute x6 -> x4, waiting for transfers between devices: 4.77 us -> 3.65 us  [shift(): lax.ppermute(value, 'bx', [(i, i + by) for i in range(count) if 0 <= i +...]
  transfers between devices with their start and end apart: 6 -> 5, of which waited for: 2 -> 3; matrix products, arithmetic and copies ran while one was open for 0% -> 0% of each run, Pallas kernels for 0% -> 0%
where the time goes in v2:
time: 79.6 us; the launch traced here: 78.9 us
  Pallas kernels  24.8 us (31%)
  blocking collectives  18 us (23%)
  starting transfers between devices  17.6 us (22%)
  waiting for transfers between devices  12.6 us (16%)
  local copies, waits for them, and re-layouts  5.02 us (6%)
  between operations  0.83 us (1%)
    all_to_all x1, blocking collectives, exchange(): return lax.all_to_all(value, 'bx', split_axis=0, concat_axis=0, tiled=True)  18 us
    pallas_call x1, Pallas kernels, shards(): pl.pallas_call(functools.partial(middle_kernel, devices, *grid, batch), o...  10.9 us
    ppermute x4, starting transfers between devices, shift(): lax.ppermute(value, 'bx', [(i, i + by) for i in range(count) if 0 <= i +...  10.2 us
    all_to_all x1, waiting for transfers between devices, exchange(): return lax.all_to_all(value, 'bx', split_axis=0, concat_axis=0, tiled=True)  8.99 us
    all_to_all x1, starting transfers between devices, exchange(): return lax.all_to_all(value, 'bx', split_axis=0, concat_axis=0, tiled=True)  7.36 us
    pallas_call x1, Pallas kernels, shards(): pl.pallas_call(functools.partial(last_kernel, devices, sub, *grid, batch)...  6.01 us
    unnamed x30, local copies, waits for them, and re-layouts  5.02 us
    pallas_call x1, Pallas kernels, shards(): pl.pallas_call(functools.partial(density_kernel, devices, *grid, batch),...  3.93 us
  transfers between devices with their start and end apart: 5, of which 3 were waited for; matrix products, arithmetic and copies ran while one was open for 0% of the time, Pallas kernels for 0%

profile of v2, /device:TPU:0, one launch (start us, length us, event | category | flops | bytes accessed | tf_op | source)
XLA Modules:
  0.0 78.9 jit_solution(12694908098858043110)
XLA Ops:
  0.6 0.0 copy-start
  0.6 0.0 copy-start.1
  0.7 0.8 %copy-done.1 = f32[3,2048]{1,0:T(4,128)S(1)} copy-done((f32[3,2048]{1,0:T(4,128)S(1)}, f32[3,2048]{1,0:T(4,128)}, u32[]{:S(2)}) %copy-start.1) | copy-done | bytes 24600
  1.4 0.0 copy-start.3
  1.4 0.7 copy-done.3
  2.1 0.0 copy-start.6
  2.1 0.7 copy-done.6
  2.8 0.0 copy-start.8
  2.8 0.7 copy-done.8
  3.5 0.0 copy-start.10
  3.5 0.7 copy-done.10
  4.2 0.0 copy-start.12
  4.2 0.7 copy-done.12
  4.9 0.0 copy-start.14
  4.9 0.7 copy-done.14
  5.6 2.3 %pack.1 = (f32[384,128]{1,0:T(8,128)}, s32[2,2048]{1,0:T(2,128)S(1)}) custom-call(s32[1,2048]{1,0:T(1,128)S(1)} %bitcast.20, s32[1,2048]{1,0:T(1,128)S(1)} %bitcast.22, s32[1,2048]{1,0:T(1,128)S(1)} %bitcast.24, s32[1,2048]{1,0:T(1,128)S(1)} %bitcast.26, s32[1,2048]{1,0:T(1,128)S(1)} %bitcast.17, f32[1,2048]{1,0:T(1,128)S(1)} %bitcast.28, ...), custom_call_target="tpu_custom_call" | custom-call | tf_op jit(solution)/shard_map/pack/pallas_call | solution.py:495
  7.9 7.4 %all-to-all-start = ((f32[16,24,128]{2,1,0:T(8,128)}), f32[16,24,128]{2,1,0:T(8,128)S(1)}, u32[]{:S(2)}, u32[]{:S(2)}) async-start(f32[16,24,128]{2,1,0:T(8,128)} %bitcast.7), calls=%async_computation | async-start | bytes 393216 | tf_op jit(solution)/shard_map/all_to_all | solution.py:466
  15.3 9.0 %all-to-all-done = f32[16,24,128]{2,1,0:T(8,128)S(1)} async-done(((f32[16,24,128]{2,1,0:T(8,128)}), f32[16,24,128]{2,1,0:T(8,128)S(1)}, u32[]{:S(2)}, u32[]{:S(2)}) %all-to-all-start) | async-done | bytes 196640 | tf_op jit(solution)/shard_map/all_to_all | solution.py:466
  24.3 0.0 copy-done
  24.3 3.9 %density.1 = (f32[448,256]{1,0:T(8,128)S(1)}, f32[192,256]{1,0:T(8,128)S(1)}, f32[192,256]{1,0:T(8,128)S(1)}) custom-call(s32[1]{0:T(128)} %bitcast.place_ref, f32[384,128]{1,0:T(8,128)S(1)} %bitcast.12, f32[4,64,256]{2,1,0:T(8,128)S(1)} %copy-done), custom_call_target="tpu_custom_call" | custom-call | tf_op jit(solution)/shard_map/density/pallas_call | solution.py:507
  28.2 1.7 %collective-permute-start = (f32[192,256]{1,0:T(8,128)S(1)}, f32[192,256]{1,0:T(8,128)S(1)}, u32[]{:S(2)}, u32[]{:S(2)}) collective-permute-start(f32[192,256]{1,0:T(8,128)S(1)} %get-tuple-element.14), channel_id=1, source_target_pairs={{0,1},{1,2},{2,3},{3,4},{4,5},{5,6},{6,7},{7,8},{8,9},{9,10},{10,1... | collective-permute-start | bytes 589832 | tf_op jit(solution)/shard_map/ppermute | solution.py:462
  29.9 1.5 %collective-permute-start.1 = (f32[192,256]{1,0:T(8,128)S(1)}, f32[192,256]{1,0:T(8,128)S(1)}, u32[]{:S(2)}, u32[]{:S(2)}) collective-permute-start(f32[192,256]{1,0:T(8,128)S(1)} %get-tuple-element.15), channel_id=1, source_target_pairs={{1,0},{2,1},{3,2},{4,3},{5,4},{6,5},{7,6},{8,7},{9,8},{10,9},{11,1... | collective-permute-start | bytes 589832 | tf_op jit(solution)/shard_map/ppermute | solution.py:462
  31.3 0.0 collective-permute-done.below_ref
  31.4 1.8 %collective-permute-done.1.above_ref = f32[192,256]{1,0:T(8,128)S(1)} collective-permute-done((f32[192,256]{1,0:T(8,128)S(1)}, f32[192,256]{1,0:T(8,128)S(1)}, u32[]{:S(2)}, u32[]{:S(2)}) %collective-permute-start.1) | collective-permute-done | bytes 196640 | tf_op jit(solution)/shard_map/ppermute | solution.py:462
  33.2 10.9 %middle.1 = (f32[384,128]{1,0:T(8,128)S(1)}, f32[384,128]{1,0:T(8,128)S(1)}, f32[448,256]{1,0:T(8,128)S(1)}, f32[192,256]{1,0:T(8,128)S(1)}, f32[192,256]{1,0:T(8,128)S(1)}) custom-call(s32[1]{0:T(128)} %bitcast.place_ref, f32[384,128]{1,0:T(8,128)S(1)} %bitcast.13, f32[448,256]{1,0:T(8,128)S(1)} %get-tuple-element.13.was_ref, ...), custom_call_target="tpu_custom_call" | custom-call | tf_op jit(solution)/shard_map/middle/pallas_call | solution.py:517
  44.1 5.6 %collective-permute-start.2 = (f32[192,256]{1,0:T(8,128)S(1)}, f32[192,256]{1,0:T(8,128)S(1)}, u32[]{:S(2)}, u32[]{:S(2)}) collective-permute-start(f32[192,256]{1,0:T(8,128)S(1)} %get-tuple-element.19), channel_id=1, source_target_pairs={{0,1},{1,2},{2,3},{3,4},{4,5},{5,6},{6,7},{7,8},{8,9},{9,10},{10,1... | collective-permute-start | bytes 589832 | tf_op jit(solution)/shard_map/ppermute | solution.py:462
  49.6 1.5 %collective-permute-start.3 = (f32[192,256]{1,0:T(8,128)S(1)}, f32[192,256]{1,0:T(8,128)S(1)}, u32[]{:S(2)}, u32[]{:S(2)}) collective-permute-start(f32[192,256]{1,0:T(8,128)S(1)} %get-tuple-element.20), channel_id=1, source_target_pairs={{1,0},{2,1},{3,2},{4,3},{5,4},{6,5},{7,6},{8,7},{9,8},{10,9},{11,1... | collective-permute-start | bytes 589832 | tf_op jit(solution)/shard_map/ppermute | solution.py:462
  51.2 0.0 collective-permute-done.2.below_ref
  51.2 1.8 %collective-permute-done.3.above_ref = f32[192,256]{1,0:T(8,128)S(1)} collective-permute-done((f32[192,256]{1,0:T(8,128)S(1)}, f32[192,256]{1,0:T(8,128)S(1)}, u32[]{:S(2)}, u32[]{:S(2)}) %collective-permute-start.3) | collective-permute-done | bytes 196640 | tf_op jit(solution)/shard_map/ppermute | solution.py:462
  53.0 6.0 %last.1 = f32[384,128]{1,0:T(8,128)S(1)} custom-call(s32[1]{0:T(128)} %bitcast.place_ref, f32[384,128]{1,0:T(8,128)S(1)} %bitcast.14, f32[384,128]{1,0:T(8,128)S(1)} %get-tuple-element.16.moved_ref, f32[384,128]{1,0:T(8,128)S(1)} %get-tuple-element.17.first_ref, f32[448,256]{1,0:T(8,128)S(1)} %get-tuple-element.18.was_ref, ...), custom_call_target="tpu_custom_call" | custom-call | tf_op jit(solution)/shard_map/last/pallas_call | solution.py:533
  59.0 0.0 copy-start.2
  59.0 0.0 copy-start.4
  59.0 0.0 copy-start.5
  59.0 0.0 copy-start.7
  59.0 0.0 copy-start.9
  59.1 0.0 copy-start.11
  59.1 0.0 copy-start.13
  59.1 18.0 %all_to_all.22 = f32[16,24,128]{2,1,0:T(8,128)S(1)} all-to-all(f32[16,24,128]{2,1,0:T(8,128)S(1)} %bitcast.15), channel_id=1, replica_groups=mesh['grp'=2,'bx'=16] {'bx'}, dimensions={0} | all-to-all | bytes 393216 | tf_op jit(solution)/shard_map/all_to_all | solution.py:466
  77.1 0.0 copy-done.2
  77.1 0.0 copy-done.4
  77.1 0.0 copy-done.5
  77.1 0.0 copy-done.7
  77.1 0.0 copy-done.9
  77.2 0.0 copy-done.11
  77.2 0.0 copy-done.13
  77.2 1.7 %chains.1 = (f32[2,2048]{1,0:T(2,128)}, f32[6,2048]{1,0:T(8,128)}) custom-call(f32[384,128]{1,0:T(8,128)S(1)} %bitcast.16, s32[2,2048]{1,0:T(2,128)S(1)} %get-tuple-element.21.slot_ref, s32[1,2048]{1,0:T(1,128)S(1)} %bitcast.21, s32[1,2048]{1,0:T(1,128)S(1)} %bitcast.23, s32[1,2048]{1,0:T(1,128)S(1)} %bitcast.25, s32[1,2048]{1,0:T(1,128)S(1)} %bitcast.27, ...), custom_call_target="tpu_custom_call" | custom-call | tf_op jit(solution)/shard_map/chains/pallas_call | solution.py:543
Async XLA Ops:
  0.6 23.6 %copy-start = (f32[4,64,256]{2,1,0:T(8,128)S(1)}, f32[4,64,256]{2,1,0:T(8,128)}, u32[]{:S(2)}) copy-start(f32[4,64,256]{2,1,0:T(8,128)} %map_ref.3) | copy-start | bytes 786436
  0.6 0.8 %copy-start.1 = (f32[3,2048]{1,0:T(4,128)S(1)}, f32[3,2048]{1,0:T(4,128)}, u32[]{:S(2)}) copy-start(f32[3,2048]{1,0:T(4,128)} %frac_ref.3) | copy-start | bytes 73732
  1.4 0.7 copy-start.3
  2.1 0.7 copy-start.6
  2.8 0.7 copy-start.8
  3.5 0.7 copy-start.10
  4.2 0.7 copy-start.12
  4.9 0.7 copy-start.14
  7.9 16.4 %all-to-all-start = ((f32[16,24,128]{2,1,0:T(8,128)}), f32[16,24,128]{2,1,0:T(8,128)S(1)}, u32[]{:S(2)}, u32[]{:S(2)}) async-start(f32[16,24,128]{2,1,0:T(8,128)} %bitcast.7), calls=%async_computation | async-start | bytes 393216 | tf_op jit(solution)/shard_map/all_to_all | solution.py:466
  28.2 3.1 %collective-permute-start = (f32[192,256]{1,0:T(8,128)S(1)}, f32[192,256]{1,0:T(8,128)S(1)}, u32[]{:S(2)}, u32[]{:S(2)}) collective-permute-start(f32[192,256]{1,0:T(8,128)S(1)} %get-tuple-element.14), channel_id=1, source_target_pairs={{0,1},{1,2},{2,3},{3,4},{4,5},{5,6},{6,7},{7,8},{8,9},{9,10},{10,1... | collective-permute-start | bytes 589832 | tf_op jit(solution)/shard_map/ppermute | solution.py:462
  29.9 3.3 %collective-permute-start.1 = (f32[192,256]{1,0:T(8,128)S(1)}, f32[192,256]{1,0:T(8,128)S(1)}, u32[]{:S(2)}, u32[]{:S(2)}) collective-permute-start(f32[192,256]{1,0:T(8,128)S(1)} %get-tuple-element.15), channel_id=1, source_target_pairs={{1,0},{2,1},{3,2},{4,3},{5,4},{6,5},{7,6},{8,7},{9,8},{10,9},{11,1... | collective-permute-start | bytes 589832 | tf_op jit(solution)/shard_map/ppermute | solution.py:462
  44.1 7.1 %collective-permute-start.2 = (f32[192,256]{1,0:T(8,128)S(1)}, f32[192,256]{1,0:T(8,128)S(1)}, u32[]{:S(2)}, u32[]{:S(2)}) collective-permute-start(f32[192,256]{1,0:T(8,128)S(1)} %get-tuple-element.19), channel_id=1, source_target_pairs={{0,1},{1,2},{2,3},{3,4},{4,5},{5,6},{6,7},{7,8},{8,9},{9,10},{10,1... | collective-permute-start | bytes 589832 | tf_op jit(solution)/shard_map/ppermute | solution.py:462
  49.6 3.3 %collective-permute-start.3 = (f32[192,256]{1,0:T(8,128)S(1)}, f32[192,256]{1,0:T(8,128)S(1)}, u32[]{:S(2)}, u32[]{:S(2)}) collective-permute-start(f32[192,256]{1,0:T(8,128)S(1)} %get-tuple-element.20), channel_id=1, source_target_pairs={{1,0},{2,1},{3,2},{4,3},{5,4},{6,5},{7,6},{8,7},{9,8},{10,9},{11,1... | collective-permute-start | bytes 589832 | tf_op jit(solution)/shard_map/ppermute | solution.py:462
  59.0 18.1 %copy-start.2 = (f32[3,2048]{1,0:T(4,128)S(1)}, f32[3,2048]{1,0:T(4,128)}, u32[]{:S(2)}) copy-start(f32[3,2048]{1,0:T(4,128)} %frac_ref.3) | copy-start | bytes 73732
  59.0 18.1 %copy-start.4 = (s32[2048]{0:T(1024)S(1)}, s32[2048]{0:T(1024)}, u32[]{:S(2)}) copy-start(s32[2048]{0:T(1024)} %param.17) | copy-start | bytes 24580
  59.0 18.1 %copy-start.5 = (f32[3,2048]{1,0:T(4,128)S(1)}, f32[3,2048]{1,0:T(4,128)}, u32[]{:S(2)}) copy-start(f32[3,2048]{1,0:T(4,128)} %axis_ref.1) | copy-start | bytes 73732
  59.0 18.1 %copy-start.7 = (s32[2048,1]{0,1:T(1,128)S(1)}, s32[2048,1]{0,1:T(1,128)}, u32[]{:S(2)}) copy-start(s32[2048,1]{0,1:T(1,128)} %param.13) | copy-start | bytes 24580
  59.0 18.1 %copy-start.9 = (s32[2048]{0:T(1024)S(1)}, s32[2048]{0:T(1024)}, u32[]{:S(2)}) copy-start(s32[2048]{0:T(1024)} %param.14) | copy-start | bytes 24580
  59.1 18.1 %copy-start.11 = (s32[2048]{0:T(1024)S(1)}, s32[2048]{0:T(1024)}, u32[]{:S(2)}) copy-start(s32[2048]{0:T(1024)} %param.15) | copy-start | bytes 24580
  59.1 18.1 %copy-start.13 = (s32[2048]{0:T(1024)S(1)}, s32[2048]{0:T(1024)}, u32[]{:S(2)}) copy-start(s32[2048]{0:T(1024)} %param.16) | copy-start | bytes 24580

commit v3 on v2

v3 whole, which is shorter than its diff:
```python
import functools

import jax
import jax.numpy as jnp
from jax import lax
from jax.experimental import pallas as pl
from jax.experimental.pallas import tpu as pltpu
from jax.sharding import PartitionSpec as P

side_tap = 0.25
middle_tap = 0.5
probe_step = 0.2
lanes = 128
fields = 8
f32, bf16 = jnp.float32, jnp.bfloat16
room = 48 * 1024 * 1024


def dot_nt(left, right):
    return lax.dot_general(left, right, (((1,), (1,)), ((), ())), preferred_element_type=f32)


def dot_nn(left, right):
    return lax.dot_general(left, right, (((1,), (0,)), ((), ())), preferred_element_type=f32)


def halves(x):
    high = x.astype(bf16)
    return high, (x - high.astype(f32)).astype(bf16)


def thirds(x):
    high, rest = x.astype(bf16), None
    rest = x - high.astype(f32)
    middle = rest.astype(bf16)
    return high, middle, (rest - middle.astype(f32)).astype(bf16)


def down_rows(count, width):
    return lax.broadcasted_iota(jnp.int32, (count, width), 0)


def spread(row, count):
    tile = jnp.broadcast_to(row, (16, row.shape[1])).astype(bf16)
    return jnp.concatenate([tile] * (count // 16), 0)


def counting(count, width):
    part = down_rows(count, lanes).astype(f32).astype(bf16)
    return jnp.concatenate([part] * (width // lanes), 1)


def pack_kernel(devices, sub, planes, rows, across, *refs):
    hbm, (message_ref, slot_ref, home_ref), held = refs[:8], refs[8:11], refs[11:19]
    semaphores = refs[19]
    copies = [
        pltpu.make_async_copy(source, target, semaphores.at[i])
        for i, (source, target) in enumerate(zip(hbm, held))
    ]
    for copy in copies:
        copy.start()
    for copy in copies:
        copy.wait()
    owner_ref, plane_ref, row_ref, column_ref, chain_ref, amp_ref, frac_ref, axis_ref = held
    atoms = owner_ref.shape[1]
    blocks = atoms // lanes
    tiles = devices * sub
    owner, plane = owner_ref[...], plane_ref[...]
    chain = chain_ref[...].astype(f32)
    home_ref[0:1, :] = (owner * planes + plane).astype(f32)
    owner = seat(owner, across)
    home_ref[1:2, :] = row_ref[...].astype(f32)
    home_ref[2:3, :] = column_ref[...].astype(f32)
    home_ref[3:6, :] = frac_ref[...]
    home_ref[6:7, :] = chain
    home_ref[7:10, :] = axis_ref[...]
    groups = planes * devices
    mine = down_rows(groups, atoms) == plane * devices + owner
    onehot = jnp.where(mine, 1.0, 0.0)
    stacked = jnp.concatenate(
        [onehot[:, j * lanes : (j + 1) * lanes] for j in range(blocks)], 0
    ).astype(bf16)
    k = lax.broadcasted_iota(jnp.int32, (lanes, 2 * lanes), 0)
    a = lax.broadcasted_iota(jnp.int32, (lanes, 2 * lanes), 1)
    before = jnp.where((k < a) | (a >= lanes), 1.0, 0.0).astype(bf16)
    counts = dot_nn(stacked, before)
    parts = [counts[j * groups : (j + 1) * groups] for j in range(blocks)]
    total = parts[0][:, lanes:]
    for part in parts[1:]:
        total = total + part[:, lanes:]
    held_by = [total[p * devices : (p + 1) * devices] for p in range(planes)]
    half = planes // 2
    none = jnp.zeros((devices, lanes), f32)
    offsets = [sum(held_by[:p], none) for p in range(half)]
    offsets += [sum(held_by[p + 1 :], none) for p in range(half, planes)]
    running = jnp.concatenate(offsets, 0)
    ranks = []
    for j, part in enumerate(parts):
        here = onehot[:, j * lanes : (j + 1) * lanes]
        ranks.append(jnp.sum((part[:, :lanes] + running) * here, 0, keepdims=True))
        running = running + part[:, lanes:]
    rank = jnp.concatenate(ranks, 1).astype(jnp.int32)
    rank = jnp.where(plane < half, rank, sub * lanes - 1 - rank)
    tile = owner * sub + lax.shift_right_logical(rank, 7)
    lane = rank & (lanes - 1)
    slot_ref[...] = jnp.concatenate([tile, lane], 0)
    values = jnp.concatenate(
        [
            (plane * rows + row_ref[...]).astype(f32),
            column_ref[...].astype(f32),
            frac_ref[...],
            amp_ref[...],
            chain,
            jnp.zeros((1, atoms), f32),
        ],
        0,
    )
    pieces = [piece.astype(f32) for piece in thirds(values)]
    width = 512
    for c in range(atoms // width):
        at = slice(c * width, (c + 1) * width)
        spot = jnp.where(down_rows(lanes, width) == lane[:, at], 1.0, 0.0).astype(bf16)
        which = jnp.broadcast_to(tile[:, at], (fields, width))
        picks = [which == t for t in range(tiles)]
        total = None
        for piece in pieces:
            part = piece[:, at]
            left = jnp.concatenate([jnp.where(pick, part, 0.0) for pick in picks], 0).astype(bf16)
            one = dot_nt(left, spot)
            total = one if total is None else total + one
        if c == 0:
            message_ref[...] = total
        else:
            message_ref[...] += total
    last = jnp.broadcast_to(chain[:, atoms - 1 :], (1, lanes))
    for b in range(devices):
        message_ref[b * sub * fields + fields - 1 : b * sub * fields + fields, :] = last
    if sorted_buckets(planes, sub):
        fits = 1.0
        lower, upper = held_by[0] + held_by[1], held_by[2] + held_by[3]
        limits = (lower, 2.0 * lanes), (upper, 2.0 * lanes), (held_by[0], lanes), (held_by[3], lanes)
        for amount, limit in limits:
            fits = fits * jnp.where(amount <= limit, 1.0, 0.0)
        for b in range(devices):
            row = (b * sub + 1) * fields + fields - 1
            message_ref[row : row + 1, :] = fits[b : b + 1]


def sorted_buckets(planes, sub):
    return planes == 4 and sub == 3


def neighbours_of(state, rows, columns):
    cell, column = state[0:1], state[1:2]
    plane = jnp.floor(cell * (1.0 / rows))
    row = cell - plane * rows
    next_row = jnp.where(row == rows - 1.0, 0.0, row + 1.0)
    next_column = jnp.where(column == columns - 1.0, 0.0, column + 1.0)
    return plane, row, next_row, column, next_column


def density_part(state, base, span, rows, columns):
    width = state.shape[1]
    plane, row, next_row, column, next_column = neighbours_of(state, rows, columns)
    fx, fy, fz, amplitude = (state[2 + i : 3 + i] for i in range(4))
    zero = jnp.zeros((), bf16)
    steps = counting(columns, width)
    here, there = steps == spread(column, columns), steps == spread(next_column, columns)

    def columns_of(near, far):
        return jnp.where(here, spread(near, columns), jnp.where(there, spread(far, columns), zero))

    near, far = halves(1.0 - fz), halves(fz)
    right_high = columns_of(near[0].astype(f32), far[0].astype(f32))
    right_low = columns_of(near[1].astype(f32), far[1].astype(f32))
    level = down_rows(fields, width).astype(f32) + float(base)
    along = amplitude * jnp.where(level == plane, 1.0 - fx, jnp.where(level == plane + 1.0, fx, 0.0))
    near, far = halves(along * (1.0 - fy)), halves(along * fy)
    steps = counting(rows, width)
    here, there = steps == spread(row, rows), steps == spread(next_row, rows)
    lefts = []
    for grade in range(2):
        first, second = near[grade].astype(f32), far[grade].astype(f32)
        lefts.append(
            jnp.concatenate(
                [
                    jnp.where(
                        here,
                        spread(first[p : p + 1], rows),
                        jnp.where(there, spread(second[p : p + 1], rows), zero),
                    )
                    for p in range(span + 1)
                ],
                0,
            )
        )
    return (
        dot_nt(lefts[0], right_high) + dot_nt(lefts[0], right_low) + dot_nt(lefts[1], right_high)
    )


def gradient_part(state, table_ref, base, span, planes, rows, columns):
    width = state.shape[1]
    plane, row, next_row, column, _ = neighbours_of(state, rows, columns)
    fx, fy, fz, amplitude = (state[2 + i : 3 + i] for i in range(4))
    spot = jnp.where(
        counting(columns, width) == spread(column, columns),
        jnp.ones((), bf16),
        jnp.zeros((), bf16),
    )
    table = jnp.concatenate(
        [
            table_ref[(e2 * (planes + 1) + base) * rows : (e2 * (planes + 1) + base + span + 1) * rows, :]
            for e2 in range(2)
        ],
        0,
    )
    sampled = dot_nn(table, jnp.concatenate([spot, spot], 0))
    sheets = [sampled[i * rows : (i + 1) * rows] for i in range(2 * (span + 1))]
    steps = down_rows(rows, width).astype(f32)
    at_plane = [jnp.broadcast_to(plane, (rows, width)) == float(base + p) for p in range(span)]
    at_row = (steps == row, steps == next_row)
    corner = {}
    for e2 in range(2):
        for e0 in range(2):
            chosen = sheets[e2 * (span + 1) + e0]
            for p in range(1, span):
                chosen = jnp.where(at_plane[p], sheets[e2 * (span + 1) + e0 + p], chosen)
            for e1 in range(2):
                corner[e0, e1, e2] = jnp.sum(jnp.where(at_row[e1], chosen, 0.0), 0, keepdims=True)
    wx, wy, wz = (1.0 - fx, fx), (1.0 - fy, fy), (1.0 - fz, fz)
    gx = gy = gz = 0.0
    for u in range(2):
        for v in range(2):
            gx = gx + wy[u] * wz[v] * (corner[1, u, v] - corner[0, u, v])
            gy = gy + wx[u] * wz[v] * (corner[u, 1, v] - corner[u, 0, v])
            gz = gz + wx[u] * wy[v] * (corner[u, v, 1] - corner[u, v, 0])
    return jnp.concatenate([amplitude * gx, amplitude * gy, amplitude * gz], 0)


def blur_sheet(sheet):
    rows, columns = sheet.shape
    sheet = middle_tap * sheet + side_tap * (pltpu.roll(sheet, 1, 0) + pltpu.roll(sheet, rows - 1, 0))
    return middle_tap * sheet + side_tap * (
        pltpu.roll(sheet, 1, 1) + pltpu.roll(sheet, columns - 1, 1)
    )


def blur_along(sheets):
    return [
        middle_tap * sheets[i] + side_tap * (sheets[i - 1] + sheets[i + 1])
        for i in range(1, len(sheets) - 1)
    ]


def edges(place_ref, devices):
    not_first = jnp.where(place_ref[0] == 0, 0.0, 1.0)
    not_last = jnp.where(place_ref[0] == devices - 1, 0.0, 1.0)
    return not_first, not_last


def share_misfit(place_ref, devices, planes, rows, density, map_ref, own_ref, near_ref, far_ref):
    _, not_last = edges(place_ref, devices)
    density[planes] = density[planes] * not_last
    zero = jnp.zeros_like(density[0])
    parts = [blur_sheet(sheet) for sheet in blur_along([zero, zero] + density + [zero, zero])]
    for p in range(planes):
        parts[p + 1] = parts[p + 1] - map_ref[p]
    for p in range(planes + 3):
        own_ref[p * rows : (p + 1) * rows, :] = parts[p]
    even = place_ref[0] % 2 == 0
    for p in range(3):
        up, down = parts[planes + p], parts[p]
        near_ref[p * rows : (p + 1) * rows, :] = jnp.where(even, up, down)
        far_ref[p * rows : (p + 1) * rows, :] = jnp.where(even, down, up)


def make_table(place_ref, devices, planes, rows, columns, own_ref, near_ref, far_ref, table_ref):
    not_first, not_last = edges(place_ref, devices)
    misfit = [own_ref[p * rows : (p + 1) * rows, :] for p in range(planes + 3)]
    even = place_ref[0] % 2 == 0
    for p in range(3):
        near = near_ref[p * rows : (p + 1) * rows, :]
        far = far_ref[p * rows : (p + 1) * rows, :]
        misfit[p] = misfit[p] + jnp.where(even, far, near)
        misfit[planes + p] = misfit[planes + p] + jnp.where(even, near, far)
    misfit[0] = misfit[0] * not_first
    misfit[planes + 1] = misfit[planes + 1] * not_last
    misfit[planes + 2] = misfit[planes + 2] * not_last
    pulled = [blur_sheet(sheet) for sheet in blur_along(misfit)]
    pulled[planes] = pulled[planes] * not_last
    for p in range(planes + 1):
        shifted = pltpu.roll(pulled[p], columns - 1, 1)
        for turn, sheet in enumerate((pulled[p], shifted)):
            high, low = halves(sheet)
            at = slice((turn * (planes + 1) + p) * rows, (turn * (planes + 1) + p + 1) * rows)
            table_ref[at, :columns] = high
            table_ref[at, columns:] = low


def load_tiles(ref, tiles):
    return jnp.concatenate([ref[t * fields : (t + 1) * fields, :] for t in tiles], 1)


def store_tiles(ref, tiles, value):
    for i, t in enumerate(tiles):
        ref[t * fields : (t + 1) * fields, :] = value[:, i * lanes : (i + 1) * lanes]


def chunks(devices, sub, planes, ordered):
    if ordered:
        return [([b * sub + k for b in range(devices)], k, 2) for k in range(sub)]
    tiles = devices * sub
    batch = max(b for b in range(1, 25) if tiles % b == 0)
    return [(range(i, i + batch), 0, planes) for i in range(0, tiles, batch)]


def in_order(message_ref, devices, sub):
    rows = [(b * sub + 1) * fields + fields - 1 for b in range(devices)]
    flags = jnp.concatenate([message_ref[row : row + 1, :] for row in rows], 0)
    return jnp.min(flags) > 0.5


def either(ordered_ref, planes, sub, work):
    if not sorted_buckets(planes, sub):
        work(False)
        return
    ordered = ordered_ref[0] == 1

    @pl.when(ordered)
    def _():
        work(True)

    @pl.when(jnp.logical_not(ordered))
    def _():
        work(False)


def all_density(state_ref, devices, sub, planes, rows, columns, ordered):
    sheets = [None] * (planes + 1)
    for tiles, base, span in chunks(devices, sub, planes, ordered):
        part = density_part(load_tiles(state_ref, tiles), base, span, rows, columns)
        for p in range(span + 1):
            sheet = part[p * rows : (p + 1) * rows]
            sheets[base + p] = sheet if sheets[base + p] is None else sheets[base + p] + sheet
    return sheets


def density_kernel(
    devices, sub, planes, rows, columns, place_ref, message_ref, map_ref, own_ref, near_ref, far_ref,
    ordered_ref,
):
    if sorted_buckets(planes, sub):
        ordered_ref[0] = jnp.where(in_order(message_ref, devices, sub), 1, 0)
    else:
        ordered_ref[0] = 0

    def work(ordered):
        sheets = all_density(message_ref, devices, sub, planes, rows, columns, ordered)
        share_misfit(place_ref, devices, planes, rows, sheets, map_ref, own_ref, near_ref, far_ref)

    either(ordered_ref, planes, sub, work)


def middle_kernel(
    devices, sub, planes, rows, columns, place_ref, ordered_ref, message_ref, was_ref, from_near_ref,
    from_far_ref, map_ref, moved_ref, first_ref, own_ref, near_ref, far_ref, table_ref,
):
    make_table(
        place_ref, devices, planes, rows, columns, was_ref, from_near_ref, from_far_ref, table_ref
    )

    def work(ordered):
        for tiles, base, span in chunks(devices, sub, planes, ordered):
            state = load_tiles(message_ref, tiles)
            gradient = gradient_part(state, table_ref, base, span, planes, rows, columns)
            moved = jnp.concatenate(
                [state[0:2], state[2:5] - probe_step * jnp.tanh(gradient), state[5:8]], 0
            )
            store_tiles(moved_ref, tiles, moved)
            store_tiles(
                first_ref, tiles,
                jnp.concatenate([gradient, jnp.zeros((5, gradient.shape[1]), f32)], 0),
            )
        sheets = all_density(moved_ref, devices, sub, planes, rows, columns, ordered)
        share_misfit(place_ref, devices, planes, rows, sheets, map_ref, own_ref, near_ref, far_ref)

    either(ordered_ref, planes, sub, work)


def cross_list(left, right):
    return [
        left[1] * right[2] - left[2] * right[1],
        left[2] * right[0] - left[0] * right[2],
        left[0] * right[1] - left[1] * right[0],
    ]


def last_kernel(
    devices, sub, planes, rows, columns, place_ref, ordered_ref, message_ref, moved_ref, first_ref,
    was_ref, from_near_ref, from_far_ref, reply_ref, table_ref,
):
    make_table(
        place_ref, devices, planes, rows, columns, was_ref, from_near_ref, from_far_ref, table_ref
    )
    last_of = jnp.concatenate(
        [
            message_ref[d * sub * fields + fields - 1 : d * sub * fields + fields, :]
            for d in range(devices)
        ],
        0,
    )
    slab_plane = (place_ref[0] * planes).astype(f32)

    def work(ordered):
        sums = jnp.zeros((devices, 16), f32)
        for tiles, base, span in chunks(devices, sub, planes, ordered):
            state = load_tiles(message_ref, tiles)
            moved = load_tiles(moved_ref, tiles)
            first = load_tiles(first_ref, tiles)[0:3]
            second = gradient_part(moved, table_ref, base, span, planes, rows, columns)
            width = state.shape[1]
            plane, row, _, column, _ = neighbours_of(state, rows, columns)
            cells = (plane + slab_plane, row, column)
            pieces = []
            for gradient, offset in ((first, state), (second, moved)):
                g = [gradient[d : d + 1] for d in range(3)]
                pieces += g + cross_list([cells[d] + offset[2 + d : 3 + d] for d in range(3)], g)
            pieces.append(jnp.where(state[5:6] > 0.0, 1.0, 0.0))
            pieces.append(jnp.zeros((3, width), f32))
            block = jnp.concatenate(pieces, 0)
            receiver = down_rows(devices, lanes)
            chosen = jnp.concatenate(
                [
                    jnp.where(
                        (receiver < t // sub)
                        & (last_of == state[6:7, i * lanes : (i + 1) * lanes]),
                        1.0,
                        0.0,
                    )
                    for i, t in enumerate(tiles)
                ],
                1,
            ).astype(bf16)
            sums = sums + sum(dot_nt(chosen, piece) for piece in thirds(block))
            store_tiles(
                reply_ref, tiles,
                jnp.concatenate([first, second, jnp.zeros((2, width), f32)], 0),
            )
        sums = jnp.concatenate([sums, jnp.zeros((devices, lanes - 16), f32)], 1)
        for d in range(devices):
            reply_ref[d * sub * fields + fields - 1 : d * sub * fields + fields, :] = sums[d : d + 1]

    either(ordered_ref, planes, sub, work)


def chain_kernel(
    devices, sub, planes, columns, reply_ref, slot_ref, home_ref, torque_ref, gradient_ref
):
    atoms = slot_ref.shape[1]
    blocks = atoms // lanes
    tiles = devices * sub
    high, low = halves(reply_ref[...])
    left = jnp.concatenate([high, low], 1)
    width = 512
    found = []
    for c in range(atoms // width):
        at = slice(c * width, (c + 1) * width)
        spot = jnp.where(down_rows(lanes, width) == slot_ref[1:2, at], 1.0, 0.0).astype(bf16)
        picked = dot_nn(left, jnp.concatenate([spot, spot], 0))
        which = jnp.broadcast_to(slot_ref[0:1, at], (fields, width))
        total = jnp.zeros((fields, width), f32)
        for t in range(tiles):
            total = jnp.where(which == t, picked[t * fields : (t + 1) * fields], total)
        found.append(total)
    gradients = jnp.concatenate(found, 1)[0:6]
    gradient_ref[...] = gradients
    fraction = home_ref[3:6, :]
    moved = fraction - probe_step * jnp.tanh(gradients[0:3])
    base = [home_ref[d : d + 1, :] for d in range(3)]
    axis = [home_ref[7 + d : 8 + d, :] for d in range(3)]
    positions = [[base[d] + offset[d : d + 1] for d in range(3)] for offset in (fraction, moved)]
    pieces = []
    for e in range(2):
        g = [gradients[3 * e + d : 3 * e + d + 1] for d in range(3)]
        pieces += g + cross_list(positions[e], g)
    pieces.append(jnp.ones((1, atoms), f32))
    pieces.append(jnp.zeros((3, atoms), f32))
    stacked = jnp.concatenate(thirds(jnp.concatenate(pieces, 0)), 0)

    def joined(x):
        return x[0:16] + x[16:32] + x[32:48]

    chain = home_ref[6:7, :]
    chain_rows = jnp.concatenate([chain[:, j * lanes : (j + 1) * lanes] for j in range(blocks)], 0)
    ends = jnp.broadcast_to(chain_rows[:, lanes - 1 :], (blocks, atoms))
    later = lax.broadcasted_iota(jnp.int32, (blocks, atoms), 1) >= lanes * (
        down_rows(blocks, atoms) + 1
    )
    bridge = jnp.where(later & (ends == chain), 1.0, 0.0).astype(bf16)
    carries = joined(dot_nt(stacked, bridge))
    arrived = jnp.zeros((1, lanes), f32)
    for d in range(devices):
        arrived = arrived + reply_ref[d * sub * fields + fields - 1 : d * sub * fields + fields, :]
    diagonal = down_rows(16, lanes) == lax.broadcasted_iota(jnp.int32, (16, lanes), 1)
    arrived = jnp.sum(jnp.where(diagonal, arrived, 0.0), 1, keepdims=True)
    padded = jnp.concatenate([chain_rows, jnp.zeros((lanes - blocks, lanes), f32)], 0)
    down_chain = jnp.transpose(padded)
    not_before = down_rows(lanes, lanes) >= lax.broadcasted_iota(jnp.int32, (lanes, lanes), 1)
    closing = chain[:, atoms - 1 :]
    sums = []
    for j in range(blocks):
        at = slice(j * lanes, (j + 1) * lanes)
        mask = not_before & (down_chain[:, j : j + 1] == chain[:, at])
        local = joined(dot_nn(stacked[:, at], jnp.where(mask, 1.0, 0.0).astype(bf16)))
        end = chain[:, (j + 1) * lanes - 1 : (j + 1) * lanes]
        carry = carries[:, j : j + 1] + jnp.where(end == closing, arrived, 0.0)
        sums.append(local + jnp.where(chain[:, at] == end, carry, 0.0))
    totals = jnp.concatenate(sums, 1)
    scale = 1.0 / (columns * jnp.sqrt(totals[12:13]))
    torques = []
    for e in range(2):
        force = [totals[6 * e + d : 6 * e + d + 1] for d in range(3)]
        lever = cross_list(positions[e], force)
        turn = 0.0
        for d in range(3):
            turn = turn + axis[d] * (totals[6 * e + 3 + d : 6 * e + 4 + d] - lever[d])
        torques.append(turn * scale)
    torque_ref[...] = jnp.concatenate(torques, 0)


def whole(count):
    return [pl.BlockSpec(memory_space=pltpu.VMEM)] * count


def settings():
    return pltpu.CompilerParams(vmem_limit_bytes=room)


def shape_of(*dims, dtype=f32):
    return jax.ShapeDtypeStruct(dims, dtype)


def seat(slab, across):
    turned = (slab // (2 * across)) % 2
    return slab ^ (turned * (2 * across - 2))


def seats_across(mesh):
    devices = mesh.devices[0]
    count = len(devices)
    if not all(hasattr(device, "coords") for device in devices):
        return count
    across = len({device.coords[0] for device in devices})
    if across & (across - 1) or count % (4 * across):
        return count
    first = devices[0].coords
    for i, device in enumerate(devices):
        x, z = i // 2 % across, i // (2 * across)
        if device.coords[0] - first[0] != x or device.coords[2] - first[2] != z:
            return count
    return across


def swap_near(value, across):
    count = lax.axis_size("bx")
    pairs = [(seat(i, across), seat(i ^ 1, across)) for i in range(count)]
    return lax.ppermute(value, "bx", pairs)


def swap_far(value, across):
    count = lax.axis_size("bx")
    pairs = []
    for i in range(1, count - 1, 2):
        pairs += [(seat(i, across), seat(i + 1, across)), (seat(i + 1, across), seat(i, across))]
    return lax.ppermute(value, "bx", pairs)


def exchange(value):
    return lax.all_to_all(value, "bx", split_axis=0, concat_axis=0, tiled=True)


def shards(
    across,
    density_map,
    amplitude,
    fraction,
    torsion_axis,
    brick_owner,
    plane_offset,
    row_offset,
    column_offset,
    chain_index,
):
    planes, rows, columns = density_map.shape
    atoms = amplitude.shape[0]
    devices = lax.axis_size("bx")
    capacity = 3 * atoms // devices
    sub = -(-capacity // lanes)
    tiles = devices * sub
    grid = (planes, rows, columns)
    place = seat(lax.axis_index("bx").astype(jnp.int32), across).reshape(1)
    moves = [(i, seat(i, across)) for i in range(devices)]
    if any(i != j for i, j in moves):
        density_map = lax.ppermute(density_map, "bx", moves)
    scalar = [pl.BlockSpec(memory_space=pltpu.SMEM)]

    owner, plane, row, column, chain = (
        item.reshape(1, atoms)
        for item in (brick_owner, plane_offset, row_offset, column_offset, chain_index)
    )
    held = [pltpu.VMEM((1, atoms), jnp.int32)] * 5
    held += [pltpu.VMEM((1, atoms), f32)] + [pltpu.VMEM((3, atoms), f32)] * 2
    message, slot, home = pl.pallas_call(
        functools.partial(pack_kernel, devices, sub, planes, rows, across),
        out_shape=(
            shape_of(tiles * fields, lanes),
            shape_of(2, atoms, dtype=jnp.int32),
            shape_of(10, atoms),
        ),
        in_specs=[pl.BlockSpec(memory_space=pltpu.HBM)] * 8,
        out_specs=whole(3),
        scratch_shapes=held + [pltpu.SemaphoreType.DMA((8,))],
        name="pack",
    )(owner, plane, row, column, chain, amplitude.reshape(1, atoms), fraction, torsion_axis)
    message = exchange(message)

    own_shape = shape_of((planes + 3) * rows, columns)
    edge_shape = shape_of(3 * rows, columns)
    own, near, far, ordered = pl.pallas_call(
        functools.partial(density_kernel, devices, sub, *grid),
        out_shape=(own_shape, edge_shape, edge_shape, shape_of(1, dtype=jnp.int32)),
        in_specs=scalar + whole(2),
        out_specs=whole(3) + scalar,
        compiler_params=settings(),
        name="density",
    )(place, message, density_map)
    near, far = swap_near(near, across), swap_far(far, across)
    table = pltpu.VMEM((2 * (planes + 1) * rows, 2 * columns), bf16)
    moved, first, own, near, far = pl.pallas_call(
        functools.partial(middle_kernel, devices, sub, *grid),
        out_shape=(
            shape_of(tiles * fields, lanes),
            shape_of(tiles * fields, lanes),
            own_shape,
            edge_shape,
            edge_shape,
        ),
        in_specs=scalar * 2 + whole(5),
        out_specs=whole(5),
        scratch_shapes=[table],
        compiler_params=settings(),
        name="middle",
    )(place, ordered, message, own, near, far, density_map)
    near, far = swap_near(near, across), swap_far(far, across)
    reply = pl.pallas_call(
        functools.partial(last_kernel, devices, sub, *grid),
        out_shape=shape_of(tiles * fields, lanes),
        in_specs=scalar * 2 + whole(6),
        out_specs=whole(1)[0],
        scratch_shapes=[table],
        compiler_params=settings(),
        name="last",
    )(place, ordered, message, moved, first, own, near, far)
    reply = exchange(reply)
    torques, gradients = pl.pallas_call(
        functools.partial(chain_kernel, devices, sub, planes, columns),
        out_shape=(shape_of(2, atoms), shape_of(6, atoms)),
        in_specs=whole(3),
        out_specs=whole(2),
        compiler_params=settings(),
        name="chains",
    )(reply, slot, home)
    return torques, gradients


def solution(mesh):
    return jax.shard_map(
        functools.partial(shards, seats_across(mesh)),
        mesh=mesh,
        in_specs=(
            P(("grp", "bx"), None, None),
            P(("grp", "bx")),
            P(None, ("grp", "bx")),
            P(None, ("grp", "bx")),
            P(("grp", "bx"), None),
            P(("grp", "bx")),
            P(("grp", "bx")),
            P(("grp", "bx")),
            P(("grp", "bx")),
        ),
        out_specs=(P(None, ("grp", "bx")), P(None, ("grp", "bx"))),
        check_vma=False,
    )
```

time: 79.6 us -> 72.2 us (0.907)
  local copies, waits for them, and re-layouts: 5.02 us -> 0.01 us
  blocking collectives: 18 us -> 22.6 us
  waiting for transfers between devices: 12.6 us -> 9.41 us
  starting transfers between devices: 17.6 us -> 15.6 us
  Pallas kernels: 24.8 us -> 23.5 us
    unnamed x30 -> x6, local copies, waits for them, and re-layouts: 5.02 us -> 0.01 us
    all_to_all x1, blocking collectives: 18 us -> 22.6 us  [exchange(): return lax.all_to_all(value, 'bx', split_axis=0, concat_axis=0, tiled=True)]
    ppermute x4 -> x5, waiting for transfers between devices: 3.65 us -> 1.16 us  [the longest x2 1.15 us: swap_near(): return lax.ppermute(value, 'bx', pairs)]
    ppermute x4 -> x5, starting transfers between devices: 10.2 us -> 8.18 us  [the longest x2 6.17 us: swap_near(): return lax.ppermute(value, 'bx', pairs)]
    pallas_call x4, Pallas kernels: 23.1 us -> 21.8 us  [the longest x1 8.74 us: shards(): pl.pallas_call(functools.partial(middle_kernel, devices, sub, *grid), out...]
  transfers between devices with their start and end apart: 5 -> 6, of which waited for: 3 -> 3; matrix products, arithmetic and copies ran while one was open for 0% -> 0% of each run, Pallas kernels for 0% -> 0%
where the time goes in v3:
time: 72.2 us; the launch traced here: 71.8 us
  Pallas kernels  23.5 us (33%)
  blocking collectives  22.6 us (31%)
  starting transfers between devices  15.6 us (22%)
  waiting for transfers between devices  9.41 us (13%)
  between operations  0.76 us (1%)
    all_to_all x1, blocking collectives, exchange(): return lax.all_to_all(value, 'bx', split_axis=0, concat_axis=0, tiled=True)  22.6 us
    pallas_call x1, Pallas kernels, shards(): pl.pallas_call(functools.partial(middle_kernel, devices, sub, *grid), out...  8.74 us
    all_to_all x1, waiting for transfers between devices, exchange(): return lax.all_to_all(value, 'bx', split_axis=0, concat_axis=0, tiled=True)  8.26 us
    all_to_all x1, starting transfers between devices, exchange(): return lax.all_to_all(value, 'bx', split_axis=0, concat_axis=0, tiled=True)  7.37 us
    ppermute x2, starting transfers between devices, swap_near(): return lax.ppermute(value, 'bx', pairs)  6.17 us
    pallas_call x1, Pallas kernels, shards(): pl.pallas_call(functools.partial(last_kernel, devices, sub, *grid), out_s...  5.13 us
    pallas_call x1, Pallas kernels, shards(): pl.pallas_call(functools.partial(density_kernel, devices, sub, *grid), ou...  4.25 us
    pallas_call x1, Pallas kernels, shards(): pl.pallas_call(functools.partial(pack_kernel, devices, sub, planes, rows,...  3.66 us
  transfers between devices with their start and end apart: 6, of which 3 were waited for; matrix products, arithmetic and copies ran while one was open for 0% of the time, Pallas kernels for 0%

profile of v3, /device:TPU:0, one launch (start us, length us, event | category | flops | bytes accessed | tf_op | source)
XLA Modules:
  0.0 71.8 jit_solution(1357654773635953677)
XLA Ops:
  0.6 0.0 copy-start.2
  0.6 3.7 %pack.1 = (f32[384,128]{1,0:T(8,128)}, s32[2,2048]{1,0:T(2,128)}, f32[10,2048]{1,0:T(8,128)}) custom-call(s32[1,2048]{1,0:T(1,128)} %bitcast.17, s32[1,2048]{1,0:T(1,128)} %bitcast.18, s32[1,2048]{1,0:T(1,128)} %bitcast.19, s32[1,2048]{1,0:T(1,128)} %bitcast.20, s32[1,2048]{1,0:T(1,128)} %bitcast.21, f32[1,2048]{1,0:T(1,128)} %bitcast.22, ...), custom_call_target="tpu_custom_call" | custom-call | tf_op jit(solution)/shard_map/pack/pallas_call | solution.py:614
  4.3 7.4 %all-to-all-start = ((f32[16,24,128]{2,1,0:T(8,128)}), f32[16,24,128]{2,1,0:T(8,128)S(1)}, u32[]{:S(2)}, u32[]{:S(2)}) async-start(f32[16,24,128]{2,1,0:T(8,128)} %bitcast.16), calls=%async_computation | async-start | bytes 393216 | tf_op jit(solution)/shard_map/all_to_all | solution.py:580
  11.7 0.0 copy-done.2
  11.7 0.7 collective-permute-start
  12.4 0.0 collective-permute-done.map_ref
  12.4 8.3 %all-to-all-done = f32[16,24,128]{2,1,0:T(8,128)S(1)} async-done(((f32[16,24,128]{2,1,0:T(8,128)}), f32[16,24,128]{2,1,0:T(8,128)S(1)}, u32[]{:S(2)}, u32[]{:S(2)}) %all-to-all-start) | async-done | bytes 196640 | tf_op jit(solution)/shard_map/all_to_all | solution.py:580
  20.7 4.3 %density.1 = (f32[448,256]{1,0:T(8,128)S(1)}, f32[192,256]{1,0:T(8,128)S(1)}, f32[192,256]{1,0:T(8,128)S(1)}, s32[1]{0:T(128)}) custom-call(s32[1]{0:T(128)} %bitcast.place_ref, f32[384,128]{1,0:T(8,128)S(1)} %bitcast.11, f32[4,64,256]{2,1,0:T(8,128)S(1)} %collective-permute-done.map_ref), custom_call_target="tpu_custom_call" | custom-call | tf_op jit(solution)/shard_map/density/pallas_call | solution.py:630
  24.9 0.1 collective-permute-start.1
  25.0 0.7 collective-permute-start.2
  25.7 0.7 %collective-permute-done.1.from_near_ref = f32[192,256]{1,0:T(8,128)S(1)} collective-permute-done((f32[192,256]{1,0:T(8,128)S(1)}, f32[192,256]{1,0:T(8,128)S(1)}, u32[]{:S(2)}, u32[]{:S(2)}) %collective-permute-start.1) | collective-permute-done | bytes 196640 | tf_op jit(solution)/shard_map/ppermute | solution.py:568
  26.5 0.0 collective-permute-done.2.from_far_ref
  26.5 8.7 %middle.1 = (f32[384,128]{1,0:T(8,128)S(1)}, f32[384,128]{1,0:T(8,128)S(1)}, f32[448,256]{1,0:T(8,128)S(1)}, f32[192,256]{1,0:T(8,128)S(1)}, f32[192,256]{1,0:T(8,128)S(1)}) custom-call(s32[1]{0:T(128)} %bitcast.place_ref, s32[1]{0:T(128)} %get-tuple-element.15.ordered_ref, f32[384,128]{1,0:T(8,128)S(1)} %bitcast.12, ...), custom_call_target="tpu_custom_call" | custom-call | tf_op jit(solution)/shard_map/middle/pallas_call | solution.py:640
  35.2 6.1 %collective-permute-start.3 = (f32[192,256]{1,0:T(8,128)S(1)}, f32[192,256]{1,0:T(8,128)S(1)}, u32[]{:S(2)}, u32[]{:S(2)}) collective-permute-start(f32[192,256]{1,0:T(8,128)S(1)} %get-tuple-element.22), channel_id=1, source_target_pairs={{0,1},{1,0},{2,3},{3,2},{6,7},{7,6},{4,5},{5,4},{8,9},{9,8},{10,11... | collective-permute-start | bytes 589832 | tf_op jit(solution)/shard_map/ppermute | solution.py:568
  41.3 0.7 collective-permute-start.4
  42.0 0.4 collective-permute-done.3.from_near_ref
  42.4 0.0 collective-permute-done.4.from_far_ref
  42.4 5.1 %last.1 = f32[384,128]{1,0:T(8,128)S(1)} custom-call(s32[1]{0:T(128)} %bitcast.place_ref, s32[1]{0:T(128)} %get-tuple-element.15.ordered_ref, f32[384,128]{1,0:T(8,128)S(1)} %bitcast.13, f32[384,128]{1,0:T(8,128)S(1)} %get-tuple-element.19.moved_ref, f32[384,128]{1,0:T(8,128)S(1)} %get-tuple-element.20.first_ref, f32[448,256]{1,0:T(8,128)S(1)} %get-tuple-element.21.was_ref, ...), custom_call_target="tpu_custom_call" | custom-call | tf_op jit(solution)/shard_map/last/pallas_call | solution.py:656
  47.5 0.0 copy-start
  47.5 0.0 copy-start.1
  47.5 22.6 %all_to_all.22 = f32[16,24,128]{2,1,0:T(8,128)S(1)} all-to-all(f32[16,24,128]{2,1,0:T(8,128)S(1)} %bitcast.15), channel_id=1, replica_groups=mesh['grp'=2,'bx'=16] {'bx'}, dimensions={0} | all-to-all | bytes 393216 | tf_op jit(solution)/shard_map/all_to_all | solution.py:580
  70.1 0.0 copy-done
  70.1 0.0 copy-done.1
  70.1 1.7 %chains.1 = (f32[2,2048]{1,0:T(2,128)}, f32[6,2048]{1,0:T(8,128)}) custom-call(f32[384,128]{1,0:T(8,128)S(1)} %bitcast.14, s32[2,2048]{1,0:T(2,128)S(1)} %copy-done.1, f32[10,2048]{1,0:T(8,128)S(1)} %copy-done), custom_call_target="tpu_custom_call" | custom-call | tf_op jit(solution)/shard_map/chains/pallas_call | solution.py:666
Async XLA Ops:
  0.6 11.1 %copy-start.2 = (f32[4,64,256]{2,1,0:T(8,128)S(1)}, f32[4,64,256]{2,1,0:T(8,128)}, u32[]{:S(2)}) copy-start(f32[4,64,256]{2,1,0:T(8,128)} %param.9) | copy-start | bytes 786436
  4.3 16.4 %all-to-all-start = ((f32[16,24,128]{2,1,0:T(8,128)}), f32[16,24,128]{2,1,0:T(8,128)S(1)}, u32[]{:S(2)}, u32[]{:S(2)}) async-start(f32[16,24,128]{2,1,0:T(8,128)} %bitcast.16), calls=%async_computation | async-start | bytes 393216 | tf_op jit(solution)/shard_map/all_to_all | solution.py:580
  11.7 0.7 %collective-permute-start = (f32[4,64,256]{2,1,0:T(8,128)S(1)}, f32[4,64,256]{2,1,0:T(8,128)S(1)}, u32[]{:S(2)}, u32[]{:S(2)}) collective-permute-start(f32[4,64,256]{2,1,0:T(8,128)S(1)} %copy-done.2), channel_id=1, source_target_pairs={{0,0},{1,1},{2,2},{3,3},{4,6},{5,7},{6,4},{7,5},{8,8},{9,9},{10,10... | collective-permute-start | bytes 786440 | tf_op jit(solution)/shard_map/ppermute | solution.py:605
  24.9 1.5 %collective-permute-start.1 = (f32[192,256]{1,0:T(8,128)S(1)}, f32[192,256]{1,0:T(8,128)S(1)}, u32[]{:S(2)}, u32[]{:S(2)}) collective-permute-start(f32[192,256]{1,0:T(8,128)S(1)} %get-tuple-element.17), channel_id=1, source_target_pairs={{0,1},{1,0},{2,3},{3,2},{6,7},{7,6},{4,5},{5,4},{8,9},{9,8},{10,11... | collective-permute-start | bytes 589832 | tf_op jit(solution)/shard_map/ppermute | solution.py:568
  25.0 1.4 %collective-permute-start.2 = (f32[192,256]{1,0:T(8,128)S(1)}, f32[192,256]{1,0:T(8,128)S(1)}, u32[]{:S(2)}, u32[]{:S(2)}) collective-permute-start(f32[192,256]{1,0:T(8,128)S(1)} %get-tuple-element.18), channel_id=1, source_target_pairs={{1,2},{2,1},{3,6},{6,3},{7,4},{4,7},{5,8},{8,5},{9,10},{10,9},{11,... | collective-permute-start | bytes 589832 | tf_op jit(solution)/shard_map/ppermute | solution.py:576
  35.2 7.2 %collective-permute-start.3 = (f32[192,256]{1,0:T(8,128)S(1)}, f32[192,256]{1,0:T(8,128)S(1)}, u32[]{:S(2)}, u32[]{:S(2)}) collective-permute-start(f32[192,256]{1,0:T(8,128)S(1)} %get-tuple-element.22), channel_id=1, source_target_pairs={{0,1},{1,0},{2,3},{3,2},{6,7},{7,6},{4,5},{5,4},{8,9},{9,8},{10,11... | collective-permute-start | bytes 589832 | tf_op jit(solution)/shard_map/ppermute | solution.py:568
  41.3 1.1 %collective-permute-start.4 = (f32[192,256]{1,0:T(8,128)S(1)}, f32[192,256]{1,0:T(8,128)S(1)}, u32[]{:S(2)}, u32[]{:S(2)}) collective-permute-start(f32[192,256]{1,0:T(8,128)S(1)} %get-tuple-element.23), channel_id=1, source_target_pairs={{1,2},{2,1},{3,6},{6,3},{7,4},{4,7},{5,8},{8,5},{9,10},{10,9},{11,... | collective-permute-start | bytes 589832 | tf_op jit(solution)/shard_map/ppermute | solution.py:576
  47.5 22.6 %copy-start = (f32[10,2048]{1,0:T(8,128)S(1)}, f32[10,2048]{1,0:T(8,128)}, u32[]{:S(2)}) copy-start(f32[10,2048]{1,0:T(8,128)} %get-tuple-element.25.home_ref) | copy-start | bytes 245764
  47.5 22.6 %copy-start.1 = (s32[2,2048]{1,0:T(2,128)S(1)}, s32[2,2048]{1,0:T(2,128)}, u32[]{:S(2)}) copy-start(s32[2,2048]{1,0:T(2,128)} %get-tuple-element.24.slot_ref) | copy-start | bytes 49156

commit v4 on v3

--- a/solution.py
+++ b/solution.py
@@ -115,7 +115,7 @@
         ],
         0,
     )
-    pieces = [piece.astype(f32) for piece in thirds(values)]
+    pieces = [piece.astype(f32) for piece in halves(values)]
     width = 512
     for c in range(atoms // width):
         at = slice(c * width, (c + 1) * width)
@@ -194,9 +194,9 @@
                 0,
             )
         )
-    return (
-        dot_nt(lefts[0], right_high) + dot_nt(lefts[0], right_low) + dot_nt(lefts[1], right_high)
-    )
+    both = dot_nt(jnp.concatenate(lefts, 0), right_high)
+    count = lefts[0].shape[0]
+    return both[:count] + both[count:] + dot_nt(lefts[0], right_low)
 
 
 def gradient_part(state, table_ref, base, span, planes, rows, columns):
@@ -216,26 +216,44 @@
         0,
     )
     sampled = dot_nn(table, jnp.concatenate([spot, spot], 0))
-    sheets = [sampled[i * rows : (i + 1) * rows] for i in range(2 * (span + 1))]
-    steps = down_rows(rows, width).astype(f32)
-    at_plane = [jnp.broadcast_to(plane, (rows, width)) == float(base + p) for p in range(span)]
-    at_row = (steps == row, steps == next_row)
+
+    def eight(x):
+        return jnp.broadcast_to(x, (8, width))
+
+    level = down_rows(8, width).astype(f32)
+    at_plane = [eight(plane) == float(base + p) for p in range(span)]
+    eighths = [jnp.floor(at * 0.125) for at in (row, next_row)]
+    at_eighth = [[eight(part) == float(j) for j in range(rows // 8)] for part in eighths]
     corner = {}
     for e2 in range(2):
         for e0 in range(2):
-            chosen = sheets[e2 * (span + 1) + e0]
-            for p in range(1, span):
-                chosen = jnp.where(at_plane[p], sheets[e2 * (span + 1) + e0 + p], chosen)
+            chosen = []
+            for j in range(rows // 8):
+                at = (e2 * (span + 1) + e0) * rows + 8 * j
+                pick = sampled[at : at + 8]
+                for p in range(1, span):
+                    pick = jnp.where(at_plane[p], sampled[at + p * rows : at + p * rows + 8], pick)
+                chosen.append(pick)
             for e1 in range(2):
-                corner[e0, e1, e2] = jnp.sum(jnp.where(at_row[e1], chosen, 0.0), 0, keepdims=True)
-    wx, wy, wz = (1.0 - fx, fx), (1.0 - fy, fy), (1.0 - fz, fz)
+                pick = chosen[0]
+                for j in range(1, rows // 8):
+                    pick = jnp.where(at_eighth[e1][j], chosen[j], pick)
+                corner[e0, e1, e2] = pick
+    fx, fz = eight(fx), eight(fz)
+    weights = (amplitude * (1.0 - fy), amplitude * fy)
     gx = gy = gz = 0.0
-    for u in range(2):
-        for v in range(2):
-            gx = gx + wy[u] * wz[v] * (corner[1, u, v] - corner[0, u, v])
-            gy = gy + wx[u] * wz[v] * (corner[u, 1, v] - corner[u, 0, v])
-            gz = gz + wx[u] * wy[v] * (corner[u, v, 1] - corner[u, v, 0])
-    return jnp.concatenate([amplitude * gx, amplitude * gy, amplitude * gz], 0)
+    for e1 in range(2):
+        here = level == eight((row, next_row)[e1] - 8.0 * eighths[e1])
+        weight = jnp.where(here, eight(weights[e1]), 0.0)
+        signed = jnp.where(here, eight(amplitude), 0.0)
+        drop = [corner[e0, e1, 1] - corner[e0, e1, 0] for e0 in range(2)]
+        value = [corner[e0, e1, 0] + fz * drop[e0] for e0 in range(2)]
+        slope = value[1] - value[0]
+        gx = gx + weight * slope
+        gz = gz + weight * (drop[0] + fx * (drop[1] - drop[0]))
+        middle = signed * (value[0] + fx * slope)
+        gy = gy + middle if e1 else gy - middle
+    return jnp.concatenate([jnp.sum(g, 0, keepdims=True) for g in (gx, gy, gz)], 0)
 
 
 def blur_sheet(sheet):
@@ -336,14 +354,11 @@
         work(False)
 
 
-def all_density(state_ref, devices, sub, planes, rows, columns, ordered):
-    sheets = [None] * (planes + 1)
-    for tiles, base, span in chunks(devices, sub, planes, ordered):
-        part = density_part(load_tiles(state_ref, tiles), base, span, rows, columns)
-        for p in range(span + 1):
-            sheet = part[p * rows : (p + 1) * rows]
-            sheets[base + p] = sheet if sheets[base + p] is None else sheets[base + p] + sheet
-    return sheets
+def add_density(sheets, state, base, span, rows, columns):
+    part = density_part(state, base, span, rows, columns)
+    for p in range(span + 1):
+        sheet = part[p * rows : (p + 1) * rows]
+        sheets[base + p] = sheet if sheets[base + p] is None else sheets[base + p] + sheet
 
 
 def density_kernel(
@@ -356,7 +371,9 @@
         ordered_ref[0] = 0
 
     def work(ordered):
-        sheets = all_density(message_ref, devices, sub, planes, rows, columns, ordered)
+        sheets = [None] * (planes + 1)
+        for tiles, base, span in chunks(devices, sub, planes, ordered):
+            add_density(sheets, load_tiles(message_ref, tiles), base, span, rows, columns)
         share_misfit(place_ref, devices, planes, rows, sheets, map_ref, own_ref, near_ref, far_ref)
 
     either(ordered_ref, planes, sub, work)
@@ -371,6 +388,7 @@
     )
 
     def work(ordered):
+        sheets, waiting = [None] * (planes + 1), None
         for tiles, base, span in chunks(devices, sub, planes, ordered):
             state = load_tiles(message_ref, tiles)
             gradient = gradient_part(state, table_ref, base, span, planes, rows, columns)
@@ -382,7 +400,10 @@
                 first_ref, tiles,
                 jnp.concatenate([gradient, jnp.zeros((5, gradient.shape[1]), f32)], 0),
             )
-        sheets = all_density(moved_ref, devices, sub, planes, rows, columns, ordered)
+            if waiting is not None:
+                add_density(sheets, *waiting, rows, columns)
+            waiting = (moved, base, span)
+        add_density(sheets, *waiting, rows, columns)
         share_misfit(place_ref, devices, planes, rows, sheets, map_ref, own_ref, near_ref, far_ref)
 
     either(ordered_ref, planes, sub, work)

time: 72.2 us -> 69.5 us (0.963)
  Pallas kernels: 23.5 us -> 20.8 us
    pallas_call x1, Pallas kernels: 8.74 us -> 7.75 us  [shards(): pl.pallas_call(functools.partial(middle_kernel, devices, sub, *grid), out...]
    pallas_call x1, Pallas kernels: 4.25 us -> 3.43 us  [shards(): pl.pallas_call(functools.partial(density_kernel, devices, sub, *grid), ou...]
where the time goes in v4:
time: 69.5 us; the launch traced here: 69.2 us
  blocking collectives  22.6 us (33%)
  Pallas kernels  20.8 us (30%)
  starting transfers between devices  15.6 us (22%)
  waiting for transfers between devices  9.41 us (14%)
  between operations  0.78 us (1%)
    all_to_all x1, blocking collectives, exchange(): return lax.all_to_all(value, 'bx', split_axis=0, concat_axis=0, tiled=True)  22.6 us
    all_to_all x1, waiting for transfers between devices, exchange(): return lax.all_to_all(value, 'bx', split_axis=0, concat_axis=0, tiled=True)  8.26 us
    pallas_call x1, Pallas kernels, shards(): pl.pallas_call(functools.partial(middle_kernel, devices, sub, *grid), out...  7.75 us
    all_to_all x1, starting transfers between devices, exchange(): return lax.all_to_all(value, 'bx', split_axis=0, concat_axis=0, tiled=True)  7.37 us
    ppermute x2, starting transfers between devices, swap_near(): return lax.ppermute(value, 'bx', pairs)  6.18 us
    pallas_call x1, Pallas kernels, shards(): pl.pallas_call(functools.partial(last_kernel, devices, sub, *grid), out_s...  4.65 us
    pallas_call x1, Pallas kernels, shards(): pl.pallas_call(functools.partial(density_kernel, devices, sub, *grid), ou...  3.43 us
    pallas_call x1, Pallas kernels, shards(): pl.pallas_call(functools.partial(pack_kernel, devices, sub, planes, rows,...  3.26 us
  transfers between devices with their start and end apart: 6, of which 3 were waited for; matrix products, arithmetic and copies ran while one was open for 0% of the time, Pallas kernels for 0%

profile of v4, /device:TPU:0, one launch (start us, length us, event | category | flops | bytes accessed | tf_op | source)
XLA Modules:
  0.0 69.2 jit_solution(12477941109785241387)
XLA Ops:
  0.6 0.0 copy-start.2
  0.6 3.3 %pack.1 = (f32[384,128]{1,0:T(8,128)}, s32[2,2048]{1,0:T(2,128)}, f32[10,2048]{1,0:T(8,128)}) custom-call(s32[1,2048]{1,0:T(1,128)} %bitcast.17, s32[1,2048]{1,0:T(1,128)} %bitcast.18, s32[1,2048]{1,0:T(1,128)} %bitcast.19, s32[1,2048]{1,0:T(1,128)} %bitcast.20, s32[1,2048]{1,0:T(1,128)} %bitcast.21, f32[1,2048]{1,0:T(1,128)} %bitcast.22, ...), custom_call_target="tpu_custom_call" | custom-call | tf_op jit(solution)/shard_map/pack/pallas_call | solution.py:635
  3.9 7.4 %all-to-all-start = ((f32[16,24,128]{2,1,0:T(8,128)}), f32[16,24,128]{2,1,0:T(8,128)S(1)}, u32[]{:S(2)}, u32[]{:S(2)}) async-start(f32[16,24,128]{2,1,0:T(8,128)} %bitcast.16), calls=%async_computation | async-start | bytes 393216 | tf_op jit(solution)/shard_map/all_to_all | solution.py:601
  11.3 0.0 copy-done.2
  11.3 0.7 collective-permute-start
  12.0 0.0 collective-permute-done.map_ref
  12.0 8.3 %all-to-all-done = f32[16,24,128]{2,1,0:T(8,128)S(1)} async-done(((f32[16,24,128]{2,1,0:T(8,128)}), f32[16,24,128]{2,1,0:T(8,128)S(1)}, u32[]{:S(2)}, u32[]{:S(2)}) %all-to-all-start) | async-done | bytes 196640 | tf_op jit(solution)/shard_map/all_to_all | solution.py:601
  20.3 3.4 %density.1 = (f32[448,256]{1,0:T(8,128)S(1)}, f32[192,256]{1,0:T(8,128)S(1)}, f32[192,256]{1,0:T(8,128)S(1)}, s32[1]{0:T(128)}) custom-call(s32[1]{0:T(128)} %bitcast.place_ref, f32[384,128]{1,0:T(8,128)S(1)} %bitcast.11, f32[4,64,256]{2,1,0:T(8,128)S(1)} %collective-permute-done.map_ref), custom_call_target="tpu_custom_call" | custom-call | tf_op jit(solution)/shard_map/density/pallas_call | solution.py:651
  23.7 0.1 collective-permute-start.1
  23.8 0.7 collective-permute-start.2
  24.5 0.7 %collective-permute-done.1.from_near_ref = f32[192,256]{1,0:T(8,128)S(1)} collective-permute-done((f32[192,256]{1,0:T(8,128)S(1)}, f32[192,256]{1,0:T(8,128)S(1)}, u32[]{:S(2)}, u32[]{:S(2)}) %collective-permute-start.1) | collective-permute-done | bytes 196640 | tf_op jit(solution)/shard_map/ppermute | solution.py:589
  25.2 0.0 collective-permute-done.2.from_far_ref
  25.2 7.7 %middle.1 = (f32[384,128]{1,0:T(8,128)S(1)}, f32[384,128]{1,0:T(8,128)S(1)}, f32[448,256]{1,0:T(8,128)S(1)}, f32[192,256]{1,0:T(8,128)S(1)}, f32[192,256]{1,0:T(8,128)S(1)}) custom-call(s32[1]{0:T(128)} %bitcast.place_ref, s32[1]{0:T(128)} %get-tuple-element.15.ordered_ref, f32[384,128]{1,0:T(8,128)S(1)} %bitcast.12, ...), custom_call_target="tpu_custom_call" | custom-call | tf_op jit(solution)/shard_map/middle/pallas_call | solution.py:661
  33.0 6.1 %collective-permute-start.3 = (f32[192,256]{1,0:T(8,128)S(1)}, f32[192,256]{1,0:T(8,128)S(1)}, u32[]{:S(2)}, u32[]{:S(2)}) collective-permute-start(f32[192,256]{1,0:T(8,128)S(1)} %get-tuple-element.22), channel_id=1, source_target_pairs={{0,1},{1,0},{2,3},{3,2},{6,7},{7,6},{4,5},{5,4},{8,9},{9,8},{10,11... | collective-permute-start | bytes 589832 | tf_op jit(solution)/shard_map/ppermute | solution.py:589
  39.1 0.7 collective-permute-start.4
  39.8 0.4 collective-permute-done.3.from_near_ref
  40.2 0.0 collective-permute-done.4.from_far_ref
  40.2 4.6 %last.1 = f32[384,128]{1,0:T(8,128)S(1)} custom-call(s32[1]{0:T(128)} %bitcast.place_ref, s32[1]{0:T(128)} %get-tuple-element.15.ordered_ref, f32[384,128]{1,0:T(8,128)S(1)} %bitcast.13, f32[384,128]{1,0:T(8,128)S(1)} %get-tuple-element.19.moved_ref, f32[384,128]{1,0:T(8,128)S(1)} %get-tuple-element.20.first_ref, f32[448,256]{1,0:T(8,128)S(1)} %get-tuple-element.21.was_ref, ...), custom_call_target="tpu_custom_call" | custom-call | tf_op jit(solution)/shard_map/last/pallas_call | solution.py:677
  44.8 0.0 copy-start
  44.8 0.0 copy-start.1
  44.9 22.6 %all_to_all.22 = f32[16,24,128]{2,1,0:T(8,128)S(1)} all-to-all(f32[16,24,128]{2,1,0:T(8,128)S(1)} %bitcast.15), channel_id=1, replica_groups=mesh['grp'=2,'bx'=16] {'bx'}, dimensions={0} | all-to-all | bytes 393216 | tf_op jit(solution)/shard_map/all_to_all | solution.py:601
  67.4 0.0 copy-done
  67.4 0.0 copy-done.1
  67.4 1.7 %chains.1 = (f32[2,2048]{1,0:T(2,128)}, f32[6,2048]{1,0:T(8,128)}) custom-call(f32[384,128]{1,0:T(8,128)S(1)} %bitcast.14, s32[2,2048]{1,0:T(2,128)S(1)} %copy-done.1, f32[10,2048]{1,0:T(8,128)S(1)} %copy-done), custom_call_target="tpu_custom_call" | custom-call | tf_op jit(solution)/shard_map/chains/pallas_call | solution.py:687
Async XLA Ops:
  0.6 10.7 %copy-start.2 = (f32[4,64,256]{2,1,0:T(8,128)S(1)}, f32[4,64,256]{2,1,0:T(8,128)}, u32[]{:S(2)}) copy-start(f32[4,64,256]{2,1,0:T(8,128)} %param.9) | copy-start | bytes 786436
  3.9 16.4 %all-to-all-start = ((f32[16,24,128]{2,1,0:T(8,128)}), f32[16,24,128]{2,1,0:T(8,128)S(1)}, u32[]{:S(2)}, u32[]{:S(2)}) async-start(f32[16,24,128]{2,1,0:T(8,128)} %bitcast.16), calls=%async_computation | async-start | bytes 393216 | tf_op jit(solution)/shard_map/all_to_all | solution.py:601
  11.3 0.7 %collective-permute-start = (f32[4,64,256]{2,1,0:T(8,128)S(1)}, f32[4,64,256]{2,1,0:T(8,128)S(1)}, u32[]{:S(2)}, u32[]{:S(2)}) collective-permute-start(f32[4,64,256]{2,1,0:T(8,128)S(1)} %copy-done.2), channel_id=1, source_target_pairs={{0,0},{1,1},{2,2},{3,3},{4,6},{5,7},{6,4},{7,5},{8,8},{9,9},{10,10... | collective-permute-start | bytes 786440 | tf_op jit(solution)/shard_map/ppermute | solution.py:626
  23.7 1.5 %collective-permute-start.1 = (f32[192,256]{1,0:T(8,128)S(1)}, f32[192,256]{1,0:T(8,128)S(1)}, u32[]{:S(2)}, u32[]{:S(2)}) collective-permute-start(f32[192,256]{1,0:T(8,128)S(1)} %get-tuple-element.17), channel_id=1, source_target_pairs={{0,1},{1,0},{2,3},{3,2},{6,7},{7,6},{4,5},{5,4},{8,9},{9,8},{10,11... | collective-permute-start | bytes 589832 | tf_op jit(solution)/shard_map/ppermute | solution.py:589
  23.8 1.4 %collective-permute-start.2 = (f32[192,256]{1,0:T(8,128)S(1)}, f32[192,256]{1,0:T(8,128)S(1)}, u32[]{:S(2)}, u32[]{:S(2)}) collective-permute-start(f32[192,256]{1,0:T(8,128)S(1)} %get-tuple-element.18), channel_id=1, source_target_pairs={{1,2},{2,1},{3,6},{6,3},{7,4},{4,7},{5,8},{8,5},{9,10},{10,9},{11,... | collective-permute-start | bytes 589832 | tf_op jit(solution)/shard_map/ppermute | solution.py:597
  33.0 7.2 %collective-permute-start.3 = (f32[192,256]{1,0:T(8,128)S(1)}, f32[192,256]{1,0:T(8,128)S(1)}, u32[]{:S(2)}, u32[]{:S(2)}) collective-permute-start(f32[192,256]{1,0:T(8,128)S(1)} %get-tuple-element.22), channel_id=1, source_target_pairs={{0,1},{1,0},{2,3},{3,2},{6,7},{7,6},{4,5},{5,4},{8,9},{9,8},{10,11... | collective-permute-start | bytes 589832 | tf_op jit(solution)/shard_map/ppermute | solution.py:589
  39.1 1.1 %collective-permute-start.4 = (f32[192,256]{1,0:T(8,128)S(1)}, f32[192,256]{1,0:T(8,128)S(1)}, u32[]{:S(2)}, u32[]{:S(2)}) collective-permute-start(f32[192,256]{1,0:T(8,128)S(1)} %get-tuple-element.23), channel_id=1, source_target_pairs={{1,2},{2,1},{3,6},{6,3},{7,4},{4,7},{5,8},{8,5},{9,10},{10,9},{11,... | collective-permute-start | bytes 589832 | tf_op jit(solution)/shard_map/ppermute | solution.py:597
  44.8 22.6 %copy-start = (f32[10,2048]{1,0:T(8,128)S(1)}, f32[10,2048]{1,0:T(8,128)}, u32[]{:S(2)}) copy-start(f32[10,2048]{1,0:T(8,128)} %get-tuple-element.25.home_ref) | copy-start | bytes 245764
  44.8 22.6 %copy-start.1 = (s32[2,2048]{1,0:T(2,128)S(1)}, s32[2,2048]{1,0:T(2,128)}, u32[]{:S(2)}) copy-start(s32[2,2048]{1,0:T(2,128)} %get-tuple-element.24.slot_ref) | copy-start | bytes 49156

commit v5 on v4

--- a/solution.py
+++ b/solution.py
@@ -50,7 +50,7 @@
     return jnp.concatenate([part] * (width // lanes), 1)
 
 
-def pack_kernel(devices, sub, planes, rows, across, *refs):
+def pack_kernel(devices, sub, planes, rows, *refs):
     hbm, (message_ref, slot_ref, home_ref), held = refs[:8], refs[8:11], refs[11:19]
     semaphores = refs[19]
     copies = [
@@ -68,7 +68,6 @@
     owner, plane = owner_ref[...], plane_ref[...]
     chain = chain_ref[...].astype(f32)
     home_ref[0:1, :] = (owner * planes + plane).astype(f32)
-    owner = seat(owner, across)
     home_ref[1:2, :] = row_ref[...].astype(f32)
     home_ref[2:3, :] = column_ref[...].astype(f32)
     home_ref[3:6, :] = frac_ref[...]
@@ -117,21 +116,24 @@
     )
     pieces = [piece.astype(f32) for piece in halves(values)]
     width = 512
+    pair = lax.shift_right_logical(tile, 1)
+    inside = (tile & 1) * lanes + lane
+    total = None
     for c in range(atoms // width):
         at = slice(c * width, (c + 1) * width)
-        spot = jnp.where(down_rows(lanes, width) == lane[:, at], 1.0, 0.0).astype(bf16)
-        which = jnp.broadcast_to(tile[:, at], (fields, width))
-        picks = [which == t for t in range(tiles)]
-        total = None
-        for piece in pieces:
-            part = piece[:, at]
-            left = jnp.concatenate([jnp.where(pick, part, 0.0) for pick in picks], 0).astype(bf16)
-            one = dot_nt(left, spot)
-            total = one if total is None else total + one
-        if c == 0:
-            message_ref[...] = total
-        else:
-            message_ref[...] += total
+        spot = jnp.where(down_rows(2 * lanes, width) == inside[:, at], 1.0, 0.0).astype(bf16)
+        which = jnp.broadcast_to(pair[:, at], (fields, width))
+        picks = [which == t for t in range(tiles // 2)]
+        left = jnp.concatenate(
+            [jnp.where(pick, piece[:, at], 0.0) for piece in pieces for pick in picks], 0
+        ).astype(bf16)
+        one = dot_nt(left, spot)
+        one = one[: one.shape[0] // 2] + one[one.shape[0] // 2 :]
+        total = one if total is None else total + one
+    for t in range(tiles):
+        message_ref[t * fields : (t + 1) * fields, :] = total[
+            t // 2 * fields : (t // 2 + 1) * fields, t % 2 * lanes : (t % 2 + 1) * lanes
+        ]
     last = jnp.broadcast_to(chain[:, atoms - 1 :], (1, lanes))
     for b in range(devices):
         message_ref[b * sub * fields + fields - 1 : b * sub * fields + fields, :] = last
@@ -562,38 +564,16 @@
     return jax.ShapeDtypeStruct(dims, dtype)
 
 
-def seat(slab, across):
-    turned = (slab // (2 * across)) % 2
-    return slab ^ (turned * (2 * across - 2))
-
-
-def seats_across(mesh):
-    devices = mesh.devices[0]
-    count = len(devices)
-    if not all(hasattr(device, "coords") for device in devices):
-        return count
-    across = len({device.coords[0] for device in devices})
-    if across & (across - 1) or count % (4 * across):
-        return count
-    first = devices[0].coords
-    for i, device in enumerate(devices):
-        x, z = i // 2 % across, i // (2 * across)
-        if device.coords[0] - first[0] != x or device.coords[2] - first[2] != z:
-            return count
-    return across
-
-
-def swap_near(value, across):
+def swap_near(value):
     count = lax.axis_size("bx")
-    pairs = [(seat(i, across), seat(i ^ 1, across)) for i in range(count)]
-    return lax.ppermute(value, "bx", pairs)
-
-
-def swap_far(value, across):
+    return lax.ppermute(value, "bx", [(i, i ^ 1) for i in range(count)])
+
+
+def swap_far(value):
     count = lax.axis_size("bx")
     pairs = []
     for i in range(1, count - 1, 2):
-        pairs += [(seat(i, across), seat(i + 1, across)), (seat(i + 1, across), seat(i, across))]
+        pairs += [(i, i + 1), (i + 1, i)]
     return lax.ppermute(value, "bx", pairs)
 
 
@@ -602,7 +582,6 @@
 
 
 def shards(
-    across,
     density_map,
     amplitude,
     fraction,
@@ -620,10 +599,7 @@
     sub = -(-capacity // lanes)
     tiles = devices * sub
     grid = (planes, rows, columns)
-    place = seat(lax.axis_index("bx").astype(jnp.int32), across).reshape(1)
-    moves = [(i, seat(i, across)) for i in range(devices)]
-    if any(i != j for i, j in moves):
-        density_map = lax.ppermute(density_map, "bx", moves)
+    place = lax.axis_index("bx").astype(jnp.int32).reshape(1)
     scalar = [pl.BlockSpec(memory_space=pltpu.SMEM)]
 
     owner, plane, row, column, chain = (
@@ -633,7 +609,7 @@
     held = [pltpu.VMEM((1, atoms), jnp.int32)] * 5
     held += [pltpu.VMEM((1, atoms), f32)] + [pltpu.VMEM((3, atoms), f32)] * 2
     message, slot, home = pl.pallas_call(
-        functools.partial(pack_kernel, devices, sub, planes, rows, across),
+        functools.partial(pack_kernel, devices, sub, planes, rows),
         out_shape=(
             shape_of(tiles * fields, lanes),
             shape_of(2, atoms, dtype=jnp.int32),
@@ -656,7 +632,7 @@
         compiler_params=settings(),
         name="density",
     )(place, message, density_map)
-    near, far = swap_near(near, across), swap_far(far, across)
+    near, far = swap_near(near), swap_far(far)
     table = pltpu.VMEM((2 * (planes + 1) * rows, 2 * columns), bf16)
     moved, first, own, near, far = pl.pallas_call(
         functools.partial(middle_kernel, devices, sub, *grid),
@@ -673,7 +649,7 @@
         compiler_params=settings(),
         name="middle",
     )(place, ordered, message, own, near, far, density_map)
-    near, far = swap_near(near, across), swap_far(far, across)
+    near, far = swap_near(near), swap_far(far)
     reply = pl.pallas_call(
         functools.partial(last_kernel, devices, sub, *grid),
         out_shape=shape_of(tiles * fields, lanes),
@@ -697,7 +673,7 @@
 
 def solution(mesh):
     return jax.shard_map(
-        functools.partial(shards, seats_across(mesh)),
+        shards,
         mesh=mesh,
         in_specs=(
             P(("grp", "bx"), None, None),

time: 69.5 us -> 67.4 us (0.970)
  blocking collectives: 22.6 us -> 20.9 us
  starting transfers between devices: 15.6 us -> 14.9 us
    all_to_all x1, blocking collectives: 22.6 us -> 20.9 us  [exchange(): return lax.all_to_all(value, 'bx', split_axis=0, concat_axis=0, tiled=True)]
    all_to_all x1, waiting for transfers between devices: 8.26 us -> 8.99 us  [exchange(): return lax.all_to_all(value, 'bx', split_axis=0, concat_axis=0, tiled=True)]
    ppermute x3 -> x2, starting transfers between devices: 6.86 us -> 6.18 us  [swap_near(): return lax.ppermute(value, 'bx', [(i, i ^ 1) for i in range(count)])]
  transfers between devices with their start and end apart: 6 -> 5, of which waited for: 3 -> 3; matrix products, arithmetic and copies ran while one was open for 0% -> 0% of each run, Pallas kernels for 0% -> 0%
where the time goes in v5:
time: 67.4 us; the launch traced here: 67.1 us
  blocking collectives  20.9 us (31%)
  Pallas kernels  20.4 us (30%)
  starting transfers between devices  14.9 us (22%)
  waiting for transfers between devices  10.1 us (15%)
  between operations  0.73 us (1%)
    all_to_all x1, blocking collectives, exchange(): return lax.all_to_all(value, 'bx', split_axis=0, concat_axis=0, tiled=True)  20.9 us
    all_to_all x1, waiting for transfers between devices, exchange(): return lax.all_to_all(value, 'bx', split_axis=0, concat_axis=0, tiled=True)  8.99 us
    pallas_call x1, Pallas kernels, shards(): pl.pallas_call(functools.partial(middle_kernel, devices, sub, *grid), out...  7.74 us
    all_to_all x1, starting transfers between devices, exchange(): return lax.all_to_all(value, 'bx', split_axis=0, concat_axis=0, tiled=True)  7.37 us
    ppermute x2, starting transfers between devices, swap_near(): return lax.ppermute(value, 'bx', [(i, i ^ 1) for i in range(count)])  6.18 us
    pallas_call x1, Pallas kernels, shards(): pl.pallas_call(functools.partial(last_kernel, devices, sub, *grid), out_s...  4.63 us
    pallas_call x1, Pallas kernels, shards(): pl.pallas_call(functools.partial(density_kernel, devices, sub, *grid), ou...  3.43 us
    pallas_call x1, Pallas kernels, shards(): pl.pallas_call(functools.partial(pack_kernel, devices, sub, planes, rows)...  2.87 us
  transfers between devices with their start and end apart: 5, of which 3 were waited for; matrix products, arithmetic and copies ran while one was open for 0% of the time, Pallas kernels for 0%

profile of v5, /device:TPU:0, one launch (start us, length us, event | category | flops | bytes accessed | tf_op | source)
XLA Modules:
  0.0 67.1 jit_solution(10330486245105538525)
XLA Ops:
  0.6 0.0 copy-start
  0.6 2.9 %pack.1 = (f32[384,128]{1,0:T(8,128)}, s32[2,2048]{1,0:T(2,128)}, f32[10,2048]{1,0:T(8,128)}) custom-call(s32[1,2048]{1,0:T(1,128)} %bitcast.17, s32[1,2048]{1,0:T(1,128)} %bitcast.18, s32[1,2048]{1,0:T(1,128)} %bitcast.19, s32[1,2048]{1,0:T(1,128)} %bitcast.20, s32[1,2048]{1,0:T(1,128)} %bitcast.21, f32[1,2048]{1,0:T(1,128)} %bitcast.22, ...), custom_call_target="tpu_custom_call" | custom-call | tf_op jit(solution)/shard_map/pack/pallas_call | solution.py:611
  3.5 7.4 %all-to-all-start = ((f32[16,24,128]{2,1,0:T(8,128)}), f32[16,24,128]{2,1,0:T(8,128)S(1)}, u32[]{:S(2)}, u32[]{:S(2)}) async-start(f32[16,24,128]{2,1,0:T(8,128)} %bitcast.16), calls=%async_computation | async-start | bytes 393216 | tf_op jit(solution)/shard_map/all_to_all | solution.py:581
  10.9 9.0 %all-to-all-done = f32[16,24,128]{2,1,0:T(8,128)S(1)} async-done(((f32[16,24,128]{2,1,0:T(8,128)}), f32[16,24,128]{2,1,0:T(8,128)S(1)}, u32[]{:S(2)}, u32[]{:S(2)}) %all-to-all-start) | async-done | bytes 196640 | tf_op jit(solution)/shard_map/all_to_all | solution.py:581
  19.9 0.0 copy-done
  19.9 3.4 %density.1 = (f32[448,256]{1,0:T(8,128)S(1)}, f32[192,256]{1,0:T(8,128)S(1)}, f32[192,256]{1,0:T(8,128)S(1)}, s32[1]{0:T(128)}) custom-call(s32[1]{0:T(128)} %bitcast.place_ref, f32[384,128]{1,0:T(8,128)S(1)} %bitcast.11, f32[4,64,256]{2,1,0:T(8,128)S(1)} %copy-done), custom_call_target="tpu_custom_call" | custom-call | tf_op jit(solution)/shard_map/density/pallas_call | solution.py:627
  23.3 0.1 collective-permute-start
  23.4 0.7 %collective-permute-start.1 = (f32[192,256]{1,0:T(8,128)S(1)}, f32[192,256]{1,0:T(8,128)S(1)}, u32[]{:S(2)}, u32[]{:S(2)}) collective-permute-start(f32[192,256]{1,0:T(8,128)S(1)} %get-tuple-element.18), channel_id=1, source_target_pairs={{1,2},{2,1},{3,4},{4,3},{5,6},{6,5},{7,8},{8,7},{9,10},{10,9},{11,... | collective-permute-start | bytes 589832 | tf_op jit(solution)/shard_map/ppermute | solution.py:577
  24.1 0.7 %collective-permute-done.from_near_ref = f32[192,256]{1,0:T(8,128)S(1)} collective-permute-done((f32[192,256]{1,0:T(8,128)S(1)}, f32[192,256]{1,0:T(8,128)S(1)}, u32[]{:S(2)}, u32[]{:S(2)}) %collective-permute-start) | collective-permute-done | bytes 196640 | tf_op jit(solution)/shard_map/ppermute | solution.py:569
  24.8 0.0 collective-permute-done.1.from_far_ref
  24.8 7.7 %middle.1 = (f32[384,128]{1,0:T(8,128)S(1)}, f32[384,128]{1,0:T(8,128)S(1)}, f32[448,256]{1,0:T(8,128)S(1)}, f32[192,256]{1,0:T(8,128)S(1)}, f32[192,256]{1,0:T(8,128)S(1)}) custom-call(s32[1]{0:T(128)} %bitcast.place_ref, s32[1]{0:T(128)} %get-tuple-element.15.ordered_ref, f32[384,128]{1,0:T(8,128)S(1)} %bitcast.12, ...), custom_call_target="tpu_custom_call" | custom-call | tf_op jit(solution)/shard_map/middle/pallas_call | solution.py:637
  32.6 6.1 %collective-permute-start.2 = (f32[192,256]{1,0:T(8,128)S(1)}, f32[192,256]{1,0:T(8,128)S(1)}, u32[]{:S(2)}, u32[]{:S(2)}) collective-permute-start(f32[192,256]{1,0:T(8,128)S(1)} %get-tuple-element.22), channel_id=1, source_target_pairs={{0,1},{1,0},{2,3},{3,2},{4,5},{5,4},{6,7},{7,6},{8,9},{9,8},{10,11... | collective-permute-start | bytes 589832 | tf_op jit(solution)/shard_map/ppermute | solution.py:569
  38.7 0.7 collective-permute-start.3
  39.4 0.4 collective-permute-done.2.from_near_ref
  39.8 0.0 collective-permute-done.3.from_far_ref
  39.8 4.6 %last.1 = f32[384,128]{1,0:T(8,128)S(1)} custom-call(s32[1]{0:T(128)} %bitcast.place_ref, s32[1]{0:T(128)} %get-tuple-element.15.ordered_ref, f32[384,128]{1,0:T(8,128)S(1)} %bitcast.13, f32[384,128]{1,0:T(8,128)S(1)} %get-tuple-element.19.moved_ref, f32[384,128]{1,0:T(8,128)S(1)} %get-tuple-element.20.first_ref, f32[448,256]{1,0:T(8,128)S(1)} %get-tuple-element.21.was_ref, ...), custom_call_target="tpu_custom_call" | custom-call | tf_op jit(solution)/shard_map/last/pallas_call | solution.py:653
  44.4 0.0 copy-start.1
  44.4 0.0 copy-start.2
  44.4 20.9 %all_to_all.22 = f32[16,24,128]{2,1,0:T(8,128)S(1)} all-to-all(f32[16,24,128]{2,1,0:T(8,128)S(1)} %bitcast.15), channel_id=1, replica_groups=mesh['grp'=2,'bx'=16] {'bx'}, dimensions={0} | all-to-all | bytes 393216 | tf_op jit(solution)/shard_map/all_to_all | solution.py:581
  65.3 0.0 copy-done.1
  65.3 0.0 copy-done.2
  65.3 1.7 %chains.1 = (f32[2,2048]{1,0:T(2,128)}, f32[6,2048]{1,0:T(8,128)}) custom-call(f32[384,128]{1,0:T(8,128)S(1)} %bitcast.14, s32[2,2048]{1,0:T(2,128)S(1)} %copy-done.2, f32[10,2048]{1,0:T(8,128)S(1)} %copy-done.1), custom_call_target="tpu_custom_call" | custom-call | tf_op jit(solution)/shard_map/chains/pallas_call | solution.py:663
Async XLA Ops:
  0.6 19.3 %copy-start = (f32[4,64,256]{2,1,0:T(8,128)S(1)}, f32[4,64,256]{2,1,0:T(8,128)}, u32[]{:S(2)}) copy-start(f32[4,64,256]{2,1,0:T(8,128)} %map_ref.3) | copy-start | bytes 786436
  3.5 16.4 %all-to-all-start = ((f32[16,24,128]{2,1,0:T(8,128)}), f32[16,24,128]{2,1,0:T(8,128)S(1)}, u32[]{:S(2)}, u32[]{:S(2)}) async-start(f32[16,24,128]{2,1,0:T(8,128)} %bitcast.16), calls=%async_computation | async-start | bytes 393216 | tf_op jit(solution)/shard_map/all_to_all | solution.py:581
  23.3 1.5 %collective-permute-start = (f32[192,256]{1,0:T(8,128)S(1)}, f32[192,256]{1,0:T(8,128)S(1)}, u32[]{:S(2)}, u32[]{:S(2)}) collective-permute-start(f32[192,256]{1,0:T(8,128)S(1)} %get-tuple-element.17), channel_id=1, source_target_pairs={{0,1},{1,0},{2,3},{3,2},{4,5},{5,4},{6,7},{7,6},{8,9},{9,8},{10,11... | collective-permute-start | bytes 589832 | tf_op jit(solution)/shard_map/ppermute | solution.py:569
  23.4 1.4 %collective-permute-start.1 = (f32[192,256]{1,0:T(8,128)S(1)}, f32[192,256]{1,0:T(8,128)S(1)}, u32[]{:S(2)}, u32[]{:S(2)}) collective-permute-start(f32[192,256]{1,0:T(8,128)S(1)} %get-tuple-element.18), channel_id=1, source_target_pairs={{1,2},{2,1},{3,4},{4,3},{5,6},{6,5},{7,8},{8,7},{9,10},{10,9},{11,... | collective-permute-start | bytes 589832 | tf_op jit(solution)/shard_map/ppermute | solution.py:577
  32.6 7.2 %collective-permute-start.2 = (f32[192,256]{1,0:T(8,128)S(1)}, f32[192,256]{1,0:T(8,128)S(1)}, u32[]{:S(2)}, u32[]{:S(2)}) collective-permute-start(f32[192,256]{1,0:T(8,128)S(1)} %get-tuple-element.22), channel_id=1, source_target_pairs={{0,1},{1,0},{2,3},{3,2},{4,5},{5,4},{6,7},{7,6},{8,9},{9,8},{10,11... | collective-permute-start | bytes 589832 | tf_op jit(solution)/shard_map/ppermute | solution.py:569
  38.7 1.1 %collective-permute-start.3 = (f32[192,256]{1,0:T(8,128)S(1)}, f32[192,256]{1,0:T(8,128)S(1)}, u32[]{:S(2)}, u32[]{:S(2)}) collective-permute-start(f32[192,256]{1,0:T(8,128)S(1)} %get-tuple-element.23), channel_id=1, source_target_pairs={{1,2},{2,1},{3,4},{4,3},{5,6},{6,5},{7,8},{8,7},{9,10},{10,9},{11,... | collective-permute-start | bytes 589832 | tf_op jit(solution)/shard_map/ppermute | solution.py:577
  44.4 20.9 %copy-start.1 = (f32[10,2048]{1,0:T(8,128)S(1)}, f32[10,2048]{1,0:T(8,128)}, u32[]{:S(2)}) copy-start(f32[10,2048]{1,0:T(8,128)} %get-tuple-element.25.home_ref) | copy-start | bytes 245764
  44.4 20.9 %copy-start.2 = (s32[2,2048]{1,0:T(2,128)S(1)}, s32[2,2048]{1,0:T(2,128)}, u32[]{:S(2)}) copy-start(s32[2,2048]{1,0:T(2,128)} %get-tuple-element.24.slot_ref) | copy-start | bytes 49156

commit v6 on v5

--- a/solution.py
+++ b/solution.py
@@ -205,18 +205,15 @@
     width = state.shape[1]
     plane, row, next_row, column, _ = neighbours_of(state, rows, columns)
     fx, fy, fz, amplitude = (state[2 + i : 3 + i] for i in range(4))
+    pair = jnp.floor(column * 0.5)
     spot = jnp.where(
-        counting(columns, width) == spread(column, columns),
+        counting(columns // 2, width) == spread(pair, columns // 2),
         jnp.ones((), bf16),
         jnp.zeros((), bf16),
     )
-    table = jnp.concatenate(
-        [
-            table_ref[(e2 * (planes + 1) + base) * rows : (e2 * (planes + 1) + base + span + 1) * rows, :]
-            for e2 in range(2)
-        ],
-        0,
-    )
+    count = (span + 1) * rows
+    starts = [(v * (planes + 1) + base) * rows for v in range(3)]
+    table = jnp.concatenate([table_ref[start : start + count, :] for start in starts], 0)
     sampled = dot_nn(table, jnp.concatenate([spot, spot], 0))
 
     def eight(x):
@@ -227,15 +224,21 @@
     eighths = [jnp.floor(at * 0.125) for at in (row, next_row)]
     at_eighth = [[eight(part) == float(j) for j in range(rows // 8)] for part in eighths]
     corner = {}
-    for e2 in range(2):
+    odd = eight(column - 2.0 * pair) > 0.5
+    picked = {}
+    for v in range(3):
         for e0 in range(2):
-            chosen = []
             for j in range(rows // 8):
-                at = (e2 * (span + 1) + e0) * rows + 8 * j
+                at = (v * (span + 1) + e0) * rows + 8 * j
                 pick = sampled[at : at + 8]
                 for p in range(1, span):
                     pick = jnp.where(at_plane[p], sampled[at + p * rows : at + p * rows + 8], pick)
-                chosen.append(pick)
+                picked[v, e0, j] = pick
+    for e2 in range(2):
+        for e0 in range(2):
+            chosen = [
+                jnp.where(odd, picked[e2 + 1, e0, j], picked[e2, e0, j]) for j in range(rows // 8)
+            ]
             for e1 in range(2):
                 pick = chosen[0]
                 for j in range(1, rows // 8):
@@ -282,8 +285,11 @@
 def share_misfit(place_ref, devices, planes, rows, density, map_ref, own_ref, near_ref, far_ref):
     _, not_last = edges(place_ref, devices)
     density[planes] = density[planes] * not_last
-    zero = jnp.zeros_like(density[0])
-    parts = [blur_sheet(sheet) for sheet in blur_along([zero, zero] + density + [zero, zero])]
+    density = [blur_sheet(sheet) for sheet in density]
+    parts = [side_tap * density[0], middle_tap * density[0] + side_tap * density[1]]
+    parts += blur_along(density)
+    parts += [side_tap * density[planes - 1] + middle_tap * density[planes]]
+    parts += [side_tap * density[planes]]
     for p in range(planes):
         parts[p + 1] = parts[p + 1] - map_ref[p]
     for p in range(planes + 3):
@@ -309,13 +315,18 @@
     misfit[planes + 2] = misfit[planes + 2] * not_last
     pulled = [blur_sheet(sheet) for sheet in blur_along(misfit)]
     pulled[planes] = pulled[planes] * not_last
-    for p in range(planes + 1):
-        shifted = pltpu.roll(pulled[p], columns - 1, 1)
-        for turn, sheet in enumerate((pulled[p], shifted)):
-            high, low = halves(sheet)
-            at = slice((turn * (planes + 1) + p) * rows, (turn * (planes + 1) + p + 1) * rows)
-            table_ref[at, :columns] = high
-            table_ref[at, columns:] = low
+    half = columns // 2
+    source = down_rows(columns, 3 * half)
+    target = lax.broadcasted_iota(jnp.int32, (columns, 3 * half), 1)
+    turn = target // half
+    spread = jnp.where(source == (2 * (target - half * turn) + turn) % columns, 1.0, 0.0).astype(bf16)
+    for grade, piece in enumerate(halves(jnp.concatenate(pulled, 0))):
+        sorted_columns = dot_nn(piece, spread).astype(bf16)
+        count = (planes + 1) * rows
+        for v in range(3):
+            table_ref[v * count : (v + 1) * count, grade * half : (grade + 1) * half] = (
+                sorted_columns[:, v * half : (v + 1) * half]
+            )
 
 
 def load_tiles(ref, tiles):
@@ -421,11 +432,37 @@
 
 def last_kernel(
     devices, sub, planes, rows, columns, place_ref, ordered_ref, message_ref, moved_ref, first_ref,
-    was_ref, from_near_ref, from_far_ref, reply_ref, table_ref,
+    was_ref, from_near_ref, from_far_ref, reply_ref, table_ref, terms_ref,
 ):
     make_table(
         place_ref, devices, planes, rows, columns, was_ref, from_near_ref, from_far_ref, table_ref
     )
+    tiles = devices * sub
+
+    def work(ordered):
+        for group, base, span in chunks(devices, sub, planes, ordered):
+            first = load_tiles(first_ref, group)[0:3]
+            moved = load_tiles(moved_ref, group)
+            second = gradient_part(moved, table_ref, base, span, planes, rows, columns)
+            rest = jnp.zeros((2, second.shape[1]), f32)
+            store_tiles(reply_ref, group, jnp.concatenate([first, second, rest], 0))
+
+    either(ordered_ref, planes, sub, work)
+
+    def field(ref, f):
+        return ref[pl.ds(f, tiles, stride=fields), :]
+
+    cell = field(message_ref, 0)
+    plane = jnp.floor(cell * (1.0 / rows))
+    cells = (plane + (place_ref[0] * planes).astype(f32), cell - plane * rows, field(message_ref, 1))
+    terms = []
+    for e, ref in enumerate((message_ref, moved_ref)):
+        g = [field(reply_ref, 3 * e + d) for d in range(3)]
+        terms += g + cross_list([cells[d] + field(ref, 2 + d) for d in range(3)], g)
+    terms.append(jnp.where(field(message_ref, 5) > 0.0, 1.0, 0.0))
+    terms += [jnp.zeros_like(cell)] * 3
+    for i, term in enumerate(terms):
+        terms_ref[pl.ds(i, tiles, stride=16), :] = term
     last_of = jnp.concatenate(
         [
             message_ref[d * sub * fields + fields - 1 : d * sub * fields + fields, :]
@@ -433,48 +470,24 @@
         ],
         0,
     )
-    slab_plane = (place_ref[0] * planes).astype(f32)
-
-    def work(ordered):
-        sums = jnp.zeros((devices, 16), f32)
-        for tiles, base, span in chunks(devices, sub, planes, ordered):
-            state = load_tiles(message_ref, tiles)
-            moved = load_tiles(moved_ref, tiles)
-            first = load_tiles(first_ref, tiles)[0:3]
-            second = gradient_part(moved, table_ref, base, span, planes, rows, columns)
-            width = state.shape[1]
-            plane, row, _, column, _ = neighbours_of(state, rows, columns)
-            cells = (plane + slab_plane, row, column)
-            pieces = []
-            for gradient, offset in ((first, state), (second, moved)):
-                g = [gradient[d : d + 1] for d in range(3)]
-                pieces += g + cross_list([cells[d] + offset[2 + d : 3 + d] for d in range(3)], g)
-            pieces.append(jnp.where(state[5:6] > 0.0, 1.0, 0.0))
-            pieces.append(jnp.zeros((3, width), f32))
-            block = jnp.concatenate(pieces, 0)
-            receiver = down_rows(devices, lanes)
-            chosen = jnp.concatenate(
-                [
-                    jnp.where(
-                        (receiver < t // sub)
-                        & (last_of == state[6:7, i * lanes : (i + 1) * lanes]),
-                        1.0,
-                        0.0,
-                    )
-                    for i, t in enumerate(tiles)
-                ],
-                1,
-            ).astype(bf16)
-            sums = sums + sum(dot_nt(chosen, piece) for piece in thirds(block))
-            store_tiles(
-                reply_ref, tiles,
-                jnp.concatenate([first, second, jnp.zeros((2, width), f32)], 0),
+    receiver = down_rows(devices, lanes)
+    sums = jnp.zeros((devices, 16), f32)
+    batch = 16
+    for i in range(0, tiles, batch):
+        chosen = [
+            jnp.where(
+                (receiver < t // sub) & (last_of == message_ref[t * fields + 6 : t * fields + 7, :]),
+                1.0,
+                0.0,
             )
-        sums = jnp.concatenate([sums, jnp.zeros((devices, lanes - 16), f32)], 1)
-        for d in range(devices):
-            reply_ref[d * sub * fields + fields - 1 : d * sub * fields + fields, :] = sums[d : d + 1]
-
-    either(ordered_ref, planes, sub, work)
+            for t in range(i, i + batch)
+        ]
+        chosen = jnp.concatenate(chosen, 1).astype(bf16)
+        block = jnp.concatenate([terms_ref[t * 16 : (t + 1) * 16, :] for t in range(i, i + batch)], 1)
+        sums = sums + sum(dot_nt(chosen, piece) for piece in thirds(block))
+    sums = jnp.concatenate([sums, jnp.zeros((devices, lanes - 16), f32)], 1)
+    for d in range(devices):
+        reply_ref[d * sub * fields + fields - 1 : d * sub * fields + fields, :] = sums[d : d + 1]
 
 
 def chain_kernel(
@@ -633,7 +646,7 @@
         name="density",
     )(place, message, density_map)
     near, far = swap_near(near), swap_far(far)
-    table = pltpu.VMEM((2 * (planes + 1) * rows, 2 * columns), bf16)
+    table = pltpu.VMEM((3 * (planes + 1) * rows, columns), bf16)
     moved, first, own, near, far = pl.pallas_call(
         functools.partial(middle_kernel, devices, sub, *grid),
         out_shape=(
@@ -655,7 +668,7 @@
         out_shape=shape_of(tiles * fields, lanes),
         in_specs=scalar * 2 + whole(6),
         out_specs=whole(1)[0],
-        scratch_shapes=[table],
+        scratch_shapes=[table, pltpu.VMEM((tiles * 16, lanes), f32)],
         compiler_params=settings(),
         name="last",
     )(place, ordered, message, moved, first, own, near, far)

time: 67.4 us -> 67 us (level)
  no operation moved by 1% of the time
where the time goes in v6:
time: 67 us; the launch traced here: 66.6 us
  blocking collectives  20.9 us (31%)
  Pallas kernels  20 us (30%)
  starting transfers between devices  14.9 us (22%)
  waiting for transfers between devices  10.1 us (15%)
  between operations  0.72 us (1%)
    all_to_all x1, blocking collectives, exchange(): return lax.all_to_all(value, 'bx', split_axis=0, concat_axis=0, tiled=True)  20.9 us
    all_to_all x1, waiting for transfers between devices, exchange(): return lax.all_to_all(value, 'bx', split_axis=0, concat_axis=0, tiled=True)  8.99 us
    pallas_call x1, Pallas kernels, shards(): pl.pallas_call(functools.partial(middle_kernel, devices, sub, *grid), out...  7.37 us
    all_to_all x1, starting transfers between devices, exchange(): return lax.all_to_all(value, 'bx', split_axis=0, concat_axis=0, tiled=True)  7.37 us
    ppermute x2, starting transfers between devices, swap_near(): return lax.ppermute(value, 'bx', [(i, i ^ 1) for i in range(count)])  6.18 us
    pallas_call x1, Pallas kernels, shards(): pl.pallas_call(functools.partial(last_kernel, devices, sub, *grid), out_s...  4.62 us
    pallas_call x1, Pallas kernels, shards(): pl.pallas_call(functools.partial(density_kernel, devices, sub, *grid), ou...  3.35 us
    pallas_call x1, Pallas kernels, shards(): pl.pallas_call(functools.partial(pack_kernel, devices, sub, planes, rows)...  2.87 us
  transfers between devices with their start and end apart: 5, of which 3 were waited for; matrix products, arithmetic and copies ran while one was open for 0% of the time, Pallas kernels for 0%

profile of v6, /device:TPU:0, one launch (start us, length us, event | category | flops | bytes accessed | tf_op | source)
XLA Modules:
  0.0 66.6 jit_solution(18166113399606696262)
XLA Ops:
  0.6 0.0 copy-start
  0.6 2.9 %pack.1 = (f32[384,128]{1,0:T(8,128)}, s32[2,2048]{1,0:T(2,128)}, f32[10,2048]{1,0:T(8,128)}) custom-call(s32[1,2048]{1,0:T(1,128)} %bitcast.17, s32[1,2048]{1,0:T(1,128)} %bitcast.18, s32[1,2048]{1,0:T(1,128)} %bitcast.19, s32[1,2048]{1,0:T(1,128)} %bitcast.20, s32[1,2048]{1,0:T(1,128)} %bitcast.21, f32[1,2048]{1,0:T(1,128)} %bitcast.22, ...), custom_call_target="tpu_custom_call" | custom-call | tf_op jit(solution)/shard_map/pack/pallas_call | solution.py:624
  3.5 7.4 %all-to-all-start = ((f32[16,24,128]{2,1,0:T(8,128)}), f32[16,24,128]{2,1,0:T(8,128)S(1)}, u32[]{:S(2)}, u32[]{:S(2)}) async-start(f32[16,24,128]{2,1,0:T(8,128)} %bitcast.16), calls=%async_computation | async-start | bytes 393216 | tf_op jit(solution)/shard_map/all_to_all | solution.py:594
  10.9 9.0 %all-to-all-done = f32[16,24,128]{2,1,0:T(8,128)S(1)} async-done(((f32[16,24,128]{2,1,0:T(8,128)}), f32[16,24,128]{2,1,0:T(8,128)S(1)}, u32[]{:S(2)}, u32[]{:S(2)}) %all-to-all-start) | async-done | bytes 196640 | tf_op jit(solution)/shard_map/all_to_all | solution.py:594
  19.9 0.0 copy-done
  19.9 3.4 %density.1 = (f32[448,256]{1,0:T(8,128)S(1)}, f32[192,256]{1,0:T(8,128)S(1)}, f32[192,256]{1,0:T(8,128)S(1)}, s32[1]{0:T(128)}) custom-call(s32[1]{0:T(128)} %bitcast.place_ref, f32[384,128]{1,0:T(8,128)S(1)} %bitcast.11, f32[4,64,256]{2,1,0:T(8,128)S(1)} %copy-done), custom_call_target="tpu_custom_call" | custom-call | tf_op jit(solution)/shard_map/density/pallas_call | solution.py:640
  23.3 0.1 collective-permute-start
  23.3 0.7 %collective-permute-start.1 = (f32[192,256]{1,0:T(8,128)S(1)}, f32[192,256]{1,0:T(8,128)S(1)}, u32[]{:S(2)}, u32[]{:S(2)}) collective-permute-start(f32[192,256]{1,0:T(8,128)S(1)} %get-tuple-element.18), channel_id=1, source_target_pairs={{1,2},{2,1},{3,4},{4,3},{5,6},{6,5},{7,8},{8,7},{9,10},{10,9},{11,... | collective-permute-start | bytes 589832 | tf_op jit(solution)/shard_map/ppermute | solution.py:590
  24.0 0.7 %collective-permute-done.from_near_ref = f32[192,256]{1,0:T(8,128)S(1)} collective-permute-done((f32[192,256]{1,0:T(8,128)S(1)}, f32[192,256]{1,0:T(8,128)S(1)}, u32[]{:S(2)}, u32[]{:S(2)}) %collective-permute-start) | collective-permute-done | bytes 196640 | tf_op jit(solution)/shard_map/ppermute | solution.py:582
  24.8 0.0 collective-permute-done.1.from_far_ref
  24.8 7.4 %middle.1 = (f32[384,128]{1,0:T(8,128)S(1)}, f32[384,128]{1,0:T(8,128)S(1)}, f32[448,256]{1,0:T(8,128)S(1)}, f32[192,256]{1,0:T(8,128)S(1)}, f32[192,256]{1,0:T(8,128)S(1)}) custom-call(s32[1]{0:T(128)} %bitcast.place_ref, s32[1]{0:T(128)} %get-tuple-element.15.ordered_ref, f32[384,128]{1,0:T(8,128)S(1)} %bitcast.12, ...), custom_call_target="tpu_custom_call" | custom-call | tf_op jit(solution)/shard_map/middle/pallas_call | solution.py:650
  32.1 6.1 %collective-permute-start.2 = (f32[192,256]{1,0:T(8,128)S(1)}, f32[192,256]{1,0:T(8,128)S(1)}, u32[]{:S(2)}, u32[]{:S(2)}) collective-permute-start(f32[192,256]{1,0:T(8,128)S(1)} %get-tuple-element.22), channel_id=1, source_target_pairs={{0,1},{1,0},{2,3},{3,2},{4,5},{5,4},{6,7},{7,6},{8,9},{9,8},{10,11... | collective-permute-start | bytes 589832 | tf_op jit(solution)/shard_map/ppermute | solution.py:582
  38.3 0.7 collective-permute-start.3
  38.9 0.4 collective-permute-done.2.from_near_ref
  39.3 0.0 collective-permute-done.3.from_far_ref
  39.3 4.6 %last.1 = f32[384,128]{1,0:T(8,128)S(1)} custom-call(s32[1]{0:T(128)} %bitcast.place_ref, s32[1]{0:T(128)} %get-tuple-element.15.ordered_ref, f32[384,128]{1,0:T(8,128)S(1)} %bitcast.13, f32[384,128]{1,0:T(8,128)S(1)} %get-tuple-element.19.moved_ref, f32[384,128]{1,0:T(8,128)S(1)} %get-tuple-element.20.first_ref, f32[448,256]{1,0:T(8,128)S(1)} %get-tuple-element.21.was_ref, ...), custom_call_target="tpu_custom_call" | custom-call | tf_op jit(solution)/shard_map/last/pallas_call | solution.py:666
  44.0 0.0 copy-start.1
  44.0 0.0 copy-start.2
  44.0 20.9 %all_to_all.22 = f32[16,24,128]{2,1,0:T(8,128)S(1)} all-to-all(f32[16,24,128]{2,1,0:T(8,128)S(1)} %bitcast.15), channel_id=1, replica_groups=mesh['grp'=2,'bx'=16] {'bx'}, dimensions={0} | all-to-all | bytes 393216 | tf_op jit(solution)/shard_map/all_to_all | solution.py:594
  64.9 0.0 copy-done.1
  64.9 0.0 copy-done.2
  64.9 1.7 %chains.1 = (f32[2,2048]{1,0:T(2,128)}, f32[6,2048]{1,0:T(8,128)}) custom-call(f32[384,128]{1,0:T(8,128)S(1)} %bitcast.14, s32[2,2048]{1,0:T(2,128)S(1)} %copy-done.2, f32[10,2048]{1,0:T(8,128)S(1)} %copy-done.1), custom_call_target="tpu_custom_call" | custom-call | tf_op jit(solution)/shard_map/chains/pallas_call | solution.py:676
Async XLA Ops:
  0.6 19.3 %copy-start = (f32[4,64,256]{2,1,0:T(8,128)S(1)}, f32[4,64,256]{2,1,0:T(8,128)}, u32[]{:S(2)}) copy-start(f32[4,64,256]{2,1,0:T(8,128)} %map_ref.3) | copy-start | bytes 786436
  3.5 16.4 %all-to-all-start = ((f32[16,24,128]{2,1,0:T(8,128)}), f32[16,24,128]{2,1,0:T(8,128)S(1)}, u32[]{:S(2)}, u32[]{:S(2)}) async-start(f32[16,24,128]{2,1,0:T(8,128)} %bitcast.16), calls=%async_computation | async-start | bytes 393216 | tf_op jit(solution)/shard_map/all_to_all | solution.py:594
  23.3 1.5 %collective-permute-start = (f32[192,256]{1,0:T(8,128)S(1)}, f32[192,256]{1,0:T(8,128)S(1)}, u32[]{:S(2)}, u32[]{:S(2)}) collective-permute-start(f32[192,256]{1,0:T(8,128)S(1)} %get-tuple-element.17), channel_id=1, source_target_pairs={{0,1},{1,0},{2,3},{3,2},{4,5},{5,4},{6,7},{7,6},{8,9},{9,8},{10,11... | collective-permute-start | bytes 589832 | tf_op jit(solution)/shard_map/ppermute | solution.py:582
  23.3 1.4 %collective-permute-start.1 = (f32[192,256]{1,0:T(8,128)S(1)}, f32[192,256]{1,0:T(8,128)S(1)}, u32[]{:S(2)}, u32[]{:S(2)}) collective-permute-start(f32[192,256]{1,0:T(8,128)S(1)} %get-tuple-element.18), channel_id=1, source_target_pairs={{1,2},{2,1},{3,4},{4,3},{5,6},{6,5},{7,8},{8,7},{9,10},{10,9},{11,... | collective-permute-start | bytes 589832 | tf_op jit(solution)/shard_map/ppermute | solution.py:590
  32.1 7.2 %collective-permute-start.2 = (f32[192,256]{1,0:T(8,128)S(1)}, f32[192,256]{1,0:T(8,128)S(1)}, u32[]{:S(2)}, u32[]{:S(2)}) collective-permute-start(f32[192,256]{1,0:T(8,128)S(1)} %get-tuple-element.22), channel_id=1, source_target_pairs={{0,1},{1,0},{2,3},{3,2},{4,5},{5,4},{6,7},{7,6},{8,9},{9,8},{10,11... | collective-permute-start | bytes 589832 | tf_op jit(solution)/shard_map/ppermute | solution.py:582
  38.3 1.1 %collective-permute-start.3 = (f32[192,256]{1,0:T(8,128)S(1)}, f32[192,256]{1,0:T(8,128)S(1)}, u32[]{:S(2)}, u32[]{:S(2)}) collective-permute-start(f32[192,256]{1,0:T(8,128)S(1)} %get-tuple-element.23), channel_id=1, source_target_pairs={{1,2},{2,1},{3,4},{4,3},{5,6},{6,5},{7,8},{8,7},{9,10},{10,9},{11,... | collective-permute-start | bytes 589832 | tf_op jit(solution)/shard_map/ppermute | solution.py:590
  44.0 20.9 %copy-start.1 = (f32[10,2048]{1,0:T(8,128)S(1)}, f32[10,2048]{1,0:T(8,128)}, u32[]{:S(2)}) copy-start(f32[10,2048]{1,0:T(8,128)} %get-tuple-element.25.home_ref) | copy-start | bytes 245764
  44.0 20.9 %copy-start.2 = (s32[2,2048]{1,0:T(2,128)S(1)}, s32[2,2048]{1,0:T(2,128)}, u32[]{:S(2)}) copy-start(s32[2,2048]{1,0:T(2,128)} %get-tuple-element.24.slot_ref) | copy-start | bytes 49156

commit v7 on v6

--- a/solution.py
+++ b/solution.py
@@ -59,20 +59,14 @@
     ]
     for copy in copies:
         copy.start()
-    for copy in copies:
+    for copy in copies[:2]:
         copy.wait()
     owner_ref, plane_ref, row_ref, column_ref, chain_ref, amp_ref, frac_ref, axis_ref = held
     atoms = owner_ref.shape[1]
     blocks = atoms // lanes
     tiles = devices * sub
     owner, plane = owner_ref[...], plane_ref[...]
-    chain = chain_ref[...].astype(f32)
     home_ref[0:1, :] = (owner * planes + plane).astype(f32)
-    home_ref[1:2, :] = row_ref[...].astype(f32)
-    home_ref[2:3, :] = column_ref[...].astype(f32)
-    home_ref[3:6, :] = frac_ref[...]
-    home_ref[6:7, :] = chain
-    home_ref[7:10, :] = axis_ref[...]
     groups = planes * devices
     mine = down_rows(groups, atoms) == plane * devices + owner
     onehot = jnp.where(mine, 1.0, 0.0)
@@ -103,6 +97,14 @@
     tile = owner * sub + lax.shift_right_logical(rank, 7)
     lane = rank & (lanes - 1)
     slot_ref[...] = jnp.concatenate([tile, lane], 0)
+    for copy in copies[2:]:
+        copy.wait()
+    chain = chain_ref[...].astype(f32)
+    home_ref[1:2, :] = row_ref[...].astype(f32)
+    home_ref[2:3, :] = column_ref[...].astype(f32)
+    home_ref[3:6, :] = frac_ref[...]
+    home_ref[6:7, :] = chain
+    home_ref[7:10, :] = axis_ref[...]
     values = jnp.concatenate(
         [
             (plane * rows + row_ref[...]).astype(f32),

time: 67 us -> 66.8 us (level)
  no operation moved by 1% of the time
where the time goes in v7:
time: 66.8 us; the launch traced here: 66.5 us
  blocking collectives  20.9 us (31%)
  Pallas kernels  19.8 us (30%)
  starting transfers between devices  14.9 us (22%)
  waiting for transfers between devices  10.1 us (15%)
  between operations  0.72 us (1%)
    all_to_all x1, blocking collectives, exchange(): return lax.all_to_all(value, 'bx', split_axis=0, concat_axis=0, tiled=True)  20.9 us
    all_to_all x1, waiting for transfers between devices, exchange(): return lax.all_to_all(value, 'bx', split_axis=0, concat_axis=0, tiled=True)  8.99 us
    pallas_call x1, Pallas kernels, shards(): pl.pallas_call(functools.partial(middle_kernel, devices, sub, *grid), out...  7.38 us
    all_to_all x1, starting transfers between devices, exchange(): return lax.all_to_all(value, 'bx', split_axis=0, concat_axis=0, tiled=True)  7.37 us
    ppermute x2, starting transfers between devices, swap_near(): return lax.ppermute(value, 'bx', [(i, i ^ 1) for i in range(count)])  6.17 us
    pallas_call x1, Pallas kernels, shards(): pl.pallas_call(functools.partial(last_kernel, devices, sub, *grid), out_s...  4.62 us
    pallas_call x1, Pallas kernels, shards(): pl.pallas_call(functools.partial(density_kernel, devices, sub, *grid), ou...  3.35 us
    pallas_call x1, Pallas kernels, shards(): pl.pallas_call(functools.partial(pack_kernel, devices, sub, planes, rows)...  2.71 us
  transfers between devices with their start and end apart: 5, of which 3 were waited for; matrix products, arithmetic and copies ran while one was open for 0% of the time, Pallas kernels for 0%

profile of v7, /device:TPU:0, one launch (start us, length us, event | category | flops | bytes accessed | tf_op | source)
XLA Modules:
  0.0 66.5 jit_solution(17433555044681914243)
XLA Ops:
  0.6 0.0 copy-start
  0.6 2.7 %pack.1 = (f32[384,128]{1,0:T(8,128)}, s32[2,2048]{1,0:T(2,128)}, f32[10,2048]{1,0:T(8,128)}) custom-call(s32[1,2048]{1,0:T(1,128)} %bitcast.17, s32[1,2048]{1,0:T(1,128)} %bitcast.18, s32[1,2048]{1,0:T(1,128)} %bitcast.19, s32[1,2048]{1,0:T(1,128)} %bitcast.20, s32[1,2048]{1,0:T(1,128)} %bitcast.21, f32[1,2048]{1,0:T(1,128)} %bitcast.22, ...), custom_call_target="tpu_custom_call" | custom-call | tf_op jit(solution)/shard_map/pack/pallas_call | solution.py:626
  3.4 7.4 %all-to-all-start = ((f32[16,24,128]{2,1,0:T(8,128)}), f32[16,24,128]{2,1,0:T(8,128)S(1)}, u32[]{:S(2)}, u32[]{:S(2)}) async-start(f32[16,24,128]{2,1,0:T(8,128)} %bitcast.16), calls=%async_computation | async-start | bytes 393216 | tf_op jit(solution)/shard_map/all_to_all | solution.py:596
  10.7 9.0 %all-to-all-done = f32[16,24,128]{2,1,0:T(8,128)S(1)} async-done(((f32[16,24,128]{2,1,0:T(8,128)}), f32[16,24,128]{2,1,0:T(8,128)S(1)}, u32[]{:S(2)}, u32[]{:S(2)}) %all-to-all-start) | async-done | bytes 196640 | tf_op jit(solution)/shard_map/all_to_all | solution.py:596
  19.7 0.0 copy-done
  19.7 3.4 %density.1 = (f32[448,256]{1,0:T(8,128)S(1)}, f32[192,256]{1,0:T(8,128)S(1)}, f32[192,256]{1,0:T(8,128)S(1)}, s32[1]{0:T(128)}) custom-call(s32[1]{0:T(128)} %bitcast.place_ref, f32[384,128]{1,0:T(8,128)S(1)} %bitcast.11, f32[4,64,256]{2,1,0:T(8,128)S(1)} %copy-done), custom_call_target="tpu_custom_call" | custom-call | tf_op jit(solution)/shard_map/density/pallas_call | solution.py:642
  23.1 0.1 collective-permute-start
  23.2 0.7 %collective-permute-start.1 = (f32[192,256]{1,0:T(8,128)S(1)}, f32[192,256]{1,0:T(8,128)S(1)}, u32[]{:S(2)}, u32[]{:S(2)}) collective-permute-start(f32[192,256]{1,0:T(8,128)S(1)} %get-tuple-element.18), channel_id=1, source_target_pairs={{1,2},{2,1},{3,4},{4,3},{5,6},{6,5},{7,8},{8,7},{9,10},{10,9},{11,... | collective-permute-start | bytes 589832 | tf_op jit(solution)/shard_map/ppermute | solution.py:592
  23.9 0.7 %collective-permute-done.from_near_ref = f32[192,256]{1,0:T(8,128)S(1)} collective-permute-done((f32[192,256]{1,0:T(8,128)S(1)}, f32[192,256]{1,0:T(8,128)S(1)}, u32[]{:S(2)}, u32[]{:S(2)}) %collective-permute-start) | collective-permute-done | bytes 196640 | tf_op jit(solution)/shard_map/ppermute | solution.py:584
  24.6 0.0 collective-permute-done.1.from_far_ref
  24.6 7.4 %middle.1 = (f32[384,128]{1,0:T(8,128)S(1)}, f32[384,128]{1,0:T(8,128)S(1)}, f32[448,256]{1,0:T(8,128)S(1)}, f32[192,256]{1,0:T(8,128)S(1)}, f32[192,256]{1,0:T(8,128)S(1)}) custom-call(s32[1]{0:T(128)} %bitcast.place_ref, s32[1]{0:T(128)} %get-tuple-element.15.ordered_ref, f32[384,128]{1,0:T(8,128)S(1)} %bitcast.12, ...), custom_call_target="tpu_custom_call" | custom-call | tf_op jit(solution)/shard_map/middle/pallas_call | solution.py:652
  32.0 6.1 %collective-permute-start.2 = (f32[192,256]{1,0:T(8,128)S(1)}, f32[192,256]{1,0:T(8,128)S(1)}, u32[]{:S(2)}, u32[]{:S(2)}) collective-permute-start(f32[192,256]{1,0:T(8,128)S(1)} %get-tuple-element.22), channel_id=1, source_target_pairs={{0,1},{1,0},{2,3},{3,2},{4,5},{5,4},{6,7},{7,6},{8,9},{9,8},{10,11... | collective-permute-start | bytes 589832 | tf_op jit(solution)/shard_map/ppermute | solution.py:584
  38.1 0.7 collective-permute-start.3
  38.8 0.4 collective-permute-done.2.from_near_ref
  39.2 0.0 collective-permute-done.3.from_far_ref
  39.2 4.6 %last.1 = f32[384,128]{1,0:T(8,128)S(1)} custom-call(s32[1]{0:T(128)} %bitcast.place_ref, s32[1]{0:T(128)} %get-tuple-element.15.ordered_ref, f32[384,128]{1,0:T(8,128)S(1)} %bitcast.13, f32[384,128]{1,0:T(8,128)S(1)} %get-tuple-element.19.moved_ref, f32[384,128]{1,0:T(8,128)S(1)} %get-tuple-element.20.first_ref, f32[448,256]{1,0:T(8,128)S(1)} %get-tuple-element.21.was_ref, ...), custom_call_target="tpu_custom_call" | custom-call | tf_op jit(solution)/shard_map/last/pallas_call | solution.py:668
  43.8 0.0 copy-start.1
  43.8 0.0 copy-start.2
  43.8 20.9 %all_to_all.22 = f32[16,24,128]{2,1,0:T(8,128)S(1)} all-to-all(f32[16,24,128]{2,1,0:T(8,128)S(1)} %bitcast.15), channel_id=1, replica_groups=mesh['grp'=2,'bx'=16] {'bx'}, dimensions={0} | all-to-all | bytes 393216 | tf_op jit(solution)/shard_map/all_to_all | solution.py:596
  64.7 0.0 copy-done.1
  64.7 0.0 copy-done.2
  64.7 1.7 %chains.1 = (f32[2,2048]{1,0:T(2,128)}, f32[6,2048]{1,0:T(8,128)}) custom-call(f32[384,128]{1,0:T(8,128)S(1)} %bitcast.14, s32[2,2048]{1,0:T(2,128)S(1)} %copy-done.2, f32[10,2048]{1,0:T(8,128)S(1)} %copy-done.1), custom_call_target="tpu_custom_call" | custom-call | tf_op jit(solution)/shard_map/chains/pallas_call | solution.py:678
Async XLA Ops:
  0.6 19.1 %copy-start = (f32[4,64,256]{2,1,0:T(8,128)S(1)}, f32[4,64,256]{2,1,0:T(8,128)}, u32[]{:S(2)}) copy-start(f32[4,64,256]{2,1,0:T(8,128)} %map_ref.3) | copy-start | bytes 786436
  3.4 16.4 %all-to-all-start = ((f32[16,24,128]{2,1,0:T(8,128)}), f32[16,24,128]{2,1,0:T(8,128)S(1)}, u32[]{:S(2)}, u32[]{:S(2)}) async-start(f32[16,24,128]{2,1,0:T(8,128)} %bitcast.16), calls=%async_computation | async-start | bytes 393216 | tf_op jit(solution)/shard_map/all_to_all | solution.py:596
  23.1 1.5 %collective-permute-start = (f32[192,256]{1,0:T(8,128)S(1)}, f32[192,256]{1,0:T(8,128)S(1)}, u32[]{:S(2)}, u32[]{:S(2)}) collective-permute-start(f32[192,256]{1,0:T(8,128)S(1)} %get-tuple-element.17), channel_id=1, source_target_pairs={{0,1},{1,0},{2,3},{3,2},{4,5},{5,4},{6,7},{7,6},{8,9},{9,8},{10,11... | collective-permute-start | bytes 589832 | tf_op jit(solution)/shard_map/ppermute | solution.py:584
  23.2 1.4 %collective-permute-start.1 = (f32[192,256]{1,0:T(8,128)S(1)}, f32[192,256]{1,0:T(8,128)S(1)}, u32[]{:S(2)}, u32[]{:S(2)}) collective-permute-start(f32[192,256]{1,0:T(8,128)S(1)} %get-tuple-element.18), channel_id=1, source_target_pairs={{1,2},{2,1},{3,4},{4,3},{5,6},{6,5},{7,8},{8,7},{9,10},{10,9},{11,... | collective-permute-start | bytes 589832 | tf_op jit(solution)/shard_map/ppermute | solution.py:592
  32.0 7.2 %collective-permute-start.2 = (f32[192,256]{1,0:T(8,128)S(1)}, f32[192,256]{1,0:T(8,128)S(1)}, u32[]{:S(2)}, u32[]{:S(2)}) collective-permute-start(f32[192,256]{1,0:T(8,128)S(1)} %get-tuple-element.22), channel_id=1, source_target_pairs={{0,1},{1,0},{2,3},{3,2},{4,5},{5,4},{6,7},{7,6},{8,9},{9,8},{10,11... | collective-permute-start | bytes 589832 | tf_op jit(solution)/shard_map/ppermute | solution.py:584
  38.1 1.1 %collective-permute-start.3 = (f32[192,256]{1,0:T(8,128)S(1)}, f32[192,256]{1,0:T(8,128)S(1)}, u32[]{:S(2)}, u32[]{:S(2)}) collective-permute-start(f32[192,256]{1,0:T(8,128)S(1)} %get-tuple-element.23), channel_id=1, source_target_pairs={{1,2},{2,1},{3,4},{4,3},{5,6},{6,5},{7,8},{8,7},{9,10},{10,9},{11,... | collective-permute-start | bytes 589832 | tf_op jit(solution)/shard_map/ppermute | solution.py:592
  43.8 20.9 %copy-start.1 = (f32[10,2048]{1,0:T(8,128)S(1)}, f32[10,2048]{1,0:T(8,128)}, u32[]{:S(2)}) copy-start(f32[10,2048]{1,0:T(8,128)} %get-tuple-element.25.home_ref) | copy-start | bytes 245764
  43.8 20.9 %copy-start.2 = (s32[2,2048]{1,0:T(2,128)S(1)}, s32[2,2048]{1,0:T(2,128)}, u32[]{:S(2)}) copy-start(s32[2,2048]{1,0:T(2,128)} %get-tuple-element.24.slot_ref) | copy-start | bytes 49156
